TPU v7x, 32 devices: a whole 2x2x4 slice. The times are simulated.
32 devices in a mesh: dom: 4 (over y, x), rel: 8 (over z, core).
Axes of the slice: x: 2, y: 2, z: 4, core: 2. Of those that a mesh axis runs over, the one named last changes fastest.
Arguments:
- entity: float32 [4096, 512], P(('dom', 'rel')), may hold values from -1.8 to 1.8
- entity_acc: float32 [4096, 512], P(('dom', 'rel')), may hold values from 0.01 to 1
- relation: float32 [1024, 512], P('rel'), may hold values from -1 to 1, as said below
- relation_acc: float32 [1024, 512], P('rel'), may hold values from 0.01 to 1
- send_rows: int32 [32, 8, 16], P(('dom', 'rel')), may hold values from 0 to 127, as said below
- trip_head: int32 [8192], P(('dom', 'rel')), may hold values from 0 to 127
- trip_rel: int32 [8192], P(('dom', 'rel')), may hold values from 0 to 127
- trip_tail: int32 [8192], P(('dom', 'rel')), may hold values from 0 to 127
- neg_part: int32 [1], replicated, may hold values from 0 to 3
- neg_rows: int32 [8, 32], replicated, may hold values from 0 to 127
Outputs:
- new_entity: float32 [4096, 512], P(('dom', 'rel'))
- new_entity_acc: float32 [4096, 512], P(('dom', 'rel'))
- new_relation: float32 [1024, 512], P('rel')
- new_relation_acc: float32 [1024, 512], P('rel')
Inputs may be any that keep to these rules, and one draw needn't show every extreme that they name: `send_rows`: within one owner's list for one receiver the 16 rows are distinct. `relation`: every component has magnitude 0.1 or more.
All inputs are finite; a program needn't handle non-finite values.
Results may differ from a plain program's by a relative error of at most 0.0003.
Values sent between devices are 32-bit elements; how exact they have to be, the bound alone decides.
No kernel may reach another device: no remote copies, remote signals or barrier semaphores. Data moves between devices by JAX's collectives and lax.ppermute only.
A program may use at most 64 MiB of HBM per device.

v0:
```python
import jax
import jax.numpy as jnp
from jax import lax
from jax.sharding import PartitionSpec as P

step_size = 0.05


def broadcast(block, axis, owner):
    block = jnp.where(lax.axis_index(axis) == owner, block, jnp.zeros_like(block))
    return lax.psum(block, axis)


def hamilton(left, right):
    left_a, left_b, left_c, left_d = jnp.split(left, 4, axis=-1)
    right_a, right_b, right_c, right_d = jnp.split(right, 4, axis=-1)
    out_a = left_a * right_a - left_b * right_b - left_c * right_c - left_d * right_d
    out_b = left_a * right_b + left_b * right_a + left_c * right_d - left_d * right_c
    out_c = left_a * right_c - left_b * right_d + left_c * right_a + left_d * right_b
    out_d = left_a * right_d + left_b * right_c - left_c * right_b + left_d * right_a
    return jnp.concatenate([out_a, out_b, out_c, out_d], axis=-1)


def unit_rel(relation):
    comp_a, comp_b, comp_c, comp_d = jnp.split(relation, 4, axis=-1)
    magnitude = jnp.sqrt(comp_a * comp_a + comp_b * comp_b + comp_c * comp_c + comp_d * comp_d)
    return relation / jnp.concatenate([magnitude, magnitude, magnitude, magnitude], axis=-1)


def local_loss(touched, relation, negatives, heads, rels, tails):
    unit_rows = unit_rel(relation)
    one_hot = (rels[:, None] == jnp.arange(relation.shape[0])[None, :]).astype(unit_rows.dtype)
    rotation = jnp.dot(one_hot, unit_rows, precision=lax.Precision.HIGHEST)
    query = hamilton(touched[heads], rotation)
    positive = jnp.sum(query * touched[tails], axis=-1)
    scores = jnp.einsum("ik,jk->ij", query, negatives, precision=lax.Precision.HIGHEST)
    return (
        jnp.sum(jax.nn.softplus(-positive)) + jnp.sum(jax.nn.softplus(scores)) / negatives.shape[0]
    )


def adagrad(values, history, gradient):
    history_new = history + gradient * gradient
    return (values - step_size * gradient / jnp.sqrt(history_new), history_new)


def shards(
    entity,
    entity_acc,
    relation,
    relation_acc,
    send_rows,
    trip_head,
    trip_rel,
    trip_tail,
    neg_part,
    neg_rows,
):
    row_width = entity.shape[1]
    send_lists = send_rows[0]
    outgoing = entity[send_lists]
    touched = lax.all_to_all(outgoing, "rel", split_axis=0, concat_axis=0, tiled=True).reshape(
        -1, row_width
    )
    neg_root = neg_part[0]
    rel_here = lax.axis_index("rel")
    own_negs = entity[neg_rows[rel_here]]
    spread = broadcast(own_negs, "dom", neg_root)
    negatives = lax.all_gather(spread, "rel", axis=0, tiled=True)

    def scored(touched_in, relation_in, negatives_in):
        return local_loss(touched_in, relation_in, negatives_in, trip_head, trip_rel, trip_tail)

    loss_value, pullback = jax.vjp(scored, touched, relation, negatives)
    grad_rows, grad_rel, grad_neg = pullback(jnp.ones_like(loss_value))
    returned = lax.all_to_all(
        grad_rows.reshape(-1, send_lists.shape[1], row_width),
        "rel",
        split_axis=0,
        concat_axis=0,
        tiled=True,
    )
    ent_grad = jnp.zeros_like(entity).at[send_lists].add(returned)
    neg_share = lax.psum_scatter(grad_neg, "rel", scatter_dimension=0, tiled=True)
    neg_total = lax.psum(neg_share, "dom")
    is_owner = (lax.axis_index("dom") == neg_root).astype(jnp.float32)
    ent_grad = ent_grad.at[neg_rows[rel_here]].add(is_owner * neg_total)
    new_entity, new_entity_acc = adagrad(entity, entity_acc, ent_grad)
    rel_sum = lax.psum(grad_rel, "dom")
    new_relation, new_relation_acc = adagrad(relation, relation_acc, rel_sum)
    return (new_entity, new_entity_acc, new_relation, new_relation_acc)


def solution(mesh):
    in_specs = (
        P(("dom", "rel"), None),
        P(("dom", "rel"), None),
        P("rel", None),
        P("rel", None),
        P(("dom", "rel"), None, None),
        P(("dom", "rel")),
        P(("dom", "rel")),
        P(("dom", "rel")),
        P(),
        P(),
    )
    out_specs = (P(("dom", "rel"), None), P(("dom", "rel"), None), P("rel", None), P("rel", None))
    return jax.shard_map(shards, mesh=mesh, in_specs=in_specs, out_specs=out_specs, check_vma=False)
```

profile of v0, /device:TPU:0, one launch (start us, length us, event | category | flops | bytes accessed | tf_op | source)
XLA Modules:
  0.0 163.5 jit_solution(9277720325643311913)
XLA Ops:
  7.2 0.0 all-reduce.4.cloned.1.call-start
  7.9 0.7 fusion.40
  8.6 0.5 copy-done.15
  9.1 1.6 %gather_fusion.3 = f32[32,512]{1,0:T(8,128)S(1)} fusion(f32[128,512]{1,0:T(8,128)} %param.10, s32[1024]{0:T(1024)S(1)} %pad_clamp_fusion), kind=kCustom, calls=%fused_computation.3 | custom fusion | bytes 131200 | tf_op jit(solution)/shard_map/gather | solution.py:67
  10.8 0.6 broadcast_select_fusion
  11.4 0.0 all-reduce.4.cloned.1.call-update
  11.4 0.7 copy-done.12
  12.1 0.1 reshape.123
  12.2 1.5 gather_fusion
  13.6 6.5 %all-to-all-start = ((f32[8,16,512]{2,1,0:T(8,128)}), f32[8,16,512]{2,1,0:T(8,128)S(1)}, u32[]{:S(2)}, u32[]{:S(2)}) async-start(f32[8,16,512]{2,1,0:T(8,128)} %bitcast.1), calls=%async_computation | async-start | bytes 524288 | tf_op jit(solution)/shard_map/all_to_all | solution.py:62
  20.1 0.0 reduce-scatter.2.cloned.1.call-start
  20.2 0.6 copy-done.16
  20.9 0.4 fusion.22
  21.3 0.2 copy-done.10
  21.5 0.1 copy-done.14
  21.6 34.2 %all-reduce.4.cloned.1.call-done = f32[32,512]{1,0:T(8,128)} async-done(((f32[32,512]{1,0:T(8,128)}), f32[32,512]{1,0:T(8,128)}) %all-reduce.4.cloned.1.call-update) | async-done | bytes 65552 | tf_op jit(solution)/shard_map/psum | solution.py:11
  55.7 14.9 %all_gather.3 = f32[256,512]{1,0:T(8,128)S(1)} all-gather(f32[32,512]{1,0:T(8,128)} %all-reduce.4.cloned.1.call-done), channel_id=1, replica_groups=mesh['dom'=4,'rel'=8] {'rel'}, dimensions={0}, use_global_device_ids=true | all-gather | bytes 589824 | tf_op jit(solution)/shard_map/all_gather | solution.py:69
  70.7 1.0 gather_fusion.1
  71.6 0.1 multiply_subtract_fusion.3
  71.7 0.1 multiply_add_fusion.11
  71.8 1.0 gather_fusion.2
  72.8 0.1 multiply_reduce_fusion
  72.9 0.6 fusion.49
  73.6 1.6 fusion.34
  75.2 0.8 convolution_add_fusion
  76.1 0.1 multiply_add_fusion.9
  76.2 0.1 multiply_add_fusion.7
  76.2 0.1 multiply_add_fusion.4
  76.3 0.0 reduce-scatter.2.cloned.1.call-update
  76.4 0.1 multiply_add_fusion.5
  76.5 0.8 copy-done.3
  77.3 0.1 copy-done.5
  77.3 0.1 copy-done.7
  77.4 2.2 %scatter_custom_fusion = f32[128,512]{1,0:T(8,128)S(1)} fusion(s32[256]{0:T(256)S(1)} %compare_select_fusion.8, f32[256]{0:T(256)S(1)} %fusion.39, f32[]{:T(128)} %constant.11.clone.1, f32[256,128]{1,0:T(8,128)S(1)} %copy-done.7, f32[256,128]{1,0:T(8,128)S(1)} %copy-done.5, f32[256,128]{1,0:T(8,128)S(1)} %copy-done.3, f32[256,128]{1,0:T(8,128)S(1)} %get-tuple-element.20), kind=kCustom, calls=%fused_computation.29 | custom fusion | flops 655360 | bytes 787460 | tf_op jit(solution)/shard_map/transpose(jvp())/scatter-add | solution.py:35
  79.6 2.2 %scatter_custom_fusion.1 = f32[128,512]{1,0:T(8,128)S(1)} fusion(s32[256]{0:T(256)S(1)} %compare_select_fusion.7, f32[256,128]{1,0:T(8,128)S(1)} %get-tuple-element.19, f32[]{:T(128)} %constant.9, f32[256,128]{1,0:T(8,128)S(1)} %get-tuple-element.18, f32[256,128]{1,0:T(8,128)S(1)} %get-tuple-element.17, f32[256,128]{1,0:T(8,128)S(1)} %get-tuple-element.16, ...), kind=kCustom, calls=%fused_computation.13 | custom fusion | flops 524288 | bytes 786440 | tf_op jit(solution)/shard_map/transpose(jvp())/scatter-add | solution.py:34
  81.9 0.7 add_any.115
  82.6 4.9 %all-to-all-start.1 = ((f32[8,16,512]{2,1,0:T(8,128)}), f32[8,16,512]{2,1,0:T(8,128)S(1)}, u32[]{:S(2)}, u32[]{:S(2)}) async-start(f32[8,16,512]{2,1,0:T(8,128)} %bitcast.6), calls=%async_computation.1 | async-start | bytes 524288 | tf_op jit(solution)/shard_map/all_to_all | solution.py:76
  87.5 0.0 all-reduce.6.cloned.1.call-start
  87.5 0.7 copy-done.17
  88.2 0.4 multiply_negate_fusion
  88.6 0.1 add_multiply_fusion.3
  88.7 0.7 maximum_add_fusion
  89.4 18.4 %reduce-scatter.2.cloned.1.call-done = f32[32,512]{1,0:T(8,128)} async-done(((f32[256,512]{1,0:T(8,128)}), f32[32,512]{1,0:T(8,128)}) %reduce-scatter.2.cloned.1.call-update) | async-done | bytes 65552 | tf_op jit(solution)/shard_map/reduce_scatter | solution.py:84
  107.9 0.0 all-reduce.6.cloned.1.call-update
  107.9 1.4 scatter_custom_fusion.2
  109.3 44.4 %all-reduce.6.cloned.1.call-done = (f32[32,512]{1,0:T(8,128)}, f32[128,512]{1,0:T(8,128)}) async-done(((f32[32,512]{1,0:T(8,128)}, f32[128,512]{1,0:T(8,128)}), (f32[32,512]{1,0:T(8,128)}, f32[128,512]{1,0:T(8,128)})) %all-reduce.6.cloned.1.call-update) | async-done | bytes 327696 | tf_op jit(solution)/shard_map/psum | solution.py:85
  153.7 1.2 scatter_custom_fusion.3
  155.0 2.0 %multiply_subtract_fusion = (f32[128,512]{1,0:T(8,128)}, f32[128,512]{1,0:T(8,128)}, f32[128,512]{1,0:T(8,128)}, f32[128,512]{1,0:T(8,128)}) fusion(f32[128,512]{1,0:T(8,128)S(1)} %copy-done.1, f32[128,512]{1,0:T(8,128)} %get-tuple-element.5, f32[128,512]{1,0:T(8,128)S(1)} %copy-done.8, f32[128,512]{1,0:T(8,128)S(1)} %copy-done, ...), kind=kLoop, calls=%fused_computation.37 | loop fusion | flops 655360 | bytes 2621440 | tf_op jit(solution)/shard_map/sub | solution.py:44
  (39 shorter events, 0.2 us)
Async XLA Ops:
  7.2 48.6 %all-reduce.4.cloned.1.call-start = ((), (), s32[]{:S(2)}) async-start(), calls=%async_computation.3 | async-start | bytes 131072 | tf_op jit(solution)/shard_map/psum | solution.py:11
  8.6 0.5 copy-start.15
  9.1 3.1 %copy-start = (f32[128,512]{1,0:T(8,128)S(1)}, f32[128,512]{1,0:T(8,128)}, u32[]{:S(2)}) copy-start(f32[128,512]{1,0:T(8,128)} %param.10) | copy-start | bytes 786436
  11.4 0.7 copy-start.12
  13.6 6.5 %copy-start.13 = (s32[256]{0:T(256)S(1)}, s32[256]{0:T(256)}, u32[]{:S(2)}) copy-start(s32[256]{0:T(256)} %param.15) | copy-start | bytes 3076
  13.6 6.5 %copy-start.1 = (f32[128,512]{1,0:T(8,128)S(1)}, f32[128,512]{1,0:T(8,128)}, u32[]{:S(2)}) copy-start(f32[128,512]{1,0:T(8,128)} %param.12) | copy-start | bytes 786436
  13.6 57.0 %all-to-all-start = ((f32[8,16,512]{2,1,0:T(8,128)}), f32[8,16,512]{2,1,0:T(8,128)S(1)}, u32[]{:S(2)}, u32[]{:S(2)}) async-start(f32[8,16,512]{2,1,0:T(8,128)} %bitcast.1), calls=%async_computation | async-start | bytes 524288 | tf_op jit(solution)/shard_map/all_to_all | solution.py:62
  20.1 87.8 %reduce-scatter.2.cloned.1.call-start = ((), (), s32[]{:S(2)}) async-start(), calls=%async_computation.4 | async-start | bytes 589824 | tf_op jit(solution)/shard_map/reduce_scatter | solution.py:84
  20.2 0.7 copy-start.16
  20.9 0.6 copy-start.10
  20.9 0.7 copy-start.14
  71.7 1.9 %copy-start.2 = (f32[256,128]{1,0:T(8,128)}, f32[256,128]{1,0:T(8,128)S(1)}, u32[]{:S(2)}) copy-start(f32[256,128]{1,0:T(8,128)S(1)} %get-tuple-element.21) | copy-start | bytes 393220
  71.8 1.8 %copy-start.4 = (f32[256,128]{1,0:T(8,128)}, f32[256,128]{1,0:T(8,128)S(1)}, u32[]{:S(2)}) copy-start(f32[256,128]{1,0:T(8,128)S(1)} %get-tuple-element.22) | copy-start | bytes 393220
  71.8 1.8 %copy-start.6 = (f32[256,128]{1,0:T(8,128)}, f32[256,128]{1,0:T(8,128)S(1)}, u32[]{:S(2)}) copy-start(f32[256,128]{1,0:T(8,128)S(1)} %get-tuple-element.23) | copy-start | bytes 393220
  76.4 0.9 copy-start.3
  76.4 1.0 copy-start.5
  76.4 1.0 copy-start.7
  82.6 4.9 %copy-start.11 = (f32[128,128]{1,0:T(8,128)S(1)}, f32[128,128]{1,0:T(8,128)}, u32[]{:S(2)}) copy-start(f32[128,128]{1,0:T(8,128)} %copy-done.10) | copy-start | bytes 196612
  82.6 25.3 %all-to-all-start.1 = ((f32[8,16,512]{2,1,0:T(8,128)}), f32[8,16,512]{2,1,0:T(8,128)S(1)}, u32[]{:S(2)}, u32[]{:S(2)}) async-start(f32[8,16,512]{2,1,0:T(8,128)} %bitcast.6), calls=%async_computation.1 | async-start | bytes 524288 | tf_op jit(solution)/shard_map/all_to_all | solution.py:76
  87.5 66.3 %all-reduce.6.cloned.1.call-start = ((), (), s32[]{:S(2)}) async-start(), calls=%async_computation.5 | async-start | bytes 655360 | tf_op jit(solution)/shard_map/psum | solution.py:85
  87.5 0.7 copy-start.17
  107.9 47.1 %copy-start.8 = (f32[128,512]{1,0:T(8,128)S(1)}, f32[128,512]{1,0:T(8,128)}, u32[]{:S(2)}) copy-start(f32[128,512]{1,0:T(8,128)} %param.13) | copy-start | bytes 786436
  107.9 47.1 %copy-start.9 = (f32[128,512]{1,0:T(8,128)S(1)}, f32[128,512]{1,0:T(8,128)}, u32[]{:S(2)}) copy-start(f32[128,512]{1,0:T(8,128)} %param.11) | copy-start | bytes 786436
Sparse Core Ops, SparseCore 0:
  11.5 44.1 all-reduce.3
  76.5 31.3 reduce-scatter.1
  111.4 42.2 all-reduce.5
where the time goes:
time: 164 us; the launch traced here: 163 us
  waiting for transfers between devices  97.1 us (59%)
  blocking collectives  14.9 us (9%)
  between operations  14.7 us (9%)
  other arithmetic  12.6 us (8%)
  starting transfers between devices  11.4 us (7%)
  local copies, waits for them, and re-layouts  8.85 us (5%)
  matrix products  3.9 us (2%)
    psum x1, waiting for transfers between devices, shards(): neg_total = lax.psum(neg_share, 'dom')  44.4 us
    psum x1, waiting for transfers between devices, broadcast(): return lax.psum(block, axis)  34.2 us
    reduce_scatter x1, waiting for transfers between devices, shards(): lax.psum_scatter(grad_neg, 'rel', scatter_dimension=0, tiled=True)  18.4 us
    all_gather x1, blocking collectives, shards(): negatives = lax.all_gather(spread, 'rel', axis=0, tiled=True)  14.9 us
    all_to_all x1, starting transfers between devices, shards(): lax.all_to_all(outgoing, 'rel', split_axis=0, concat_axis=0, tiled=True)  6.46 us
    all_to_all x1, starting transfers between devices, shards(): lax.all_to_all(grad_rows.reshape(-1, send_lists.shape[1], row_width), 're...  4.87 us
    unnamed x36, local copies, waits for them, and re-layouts  3.72 us
  transfers between devices with their start and end apart: 5, of which 3 were waited for; matrix products, arithmetic and copies ran while one was open for 6% of the time, Pallas kernels for 0%

commit v1 on v0

v1 whole, which is shorter than its diff:
```python
import jax
import jax.numpy as jnp
from jax import lax
from jax.sharding import PartitionSpec as P

step_size = 0.05
HIGHEST = lax.Precision.HIGHEST


def exchange(block, axis, size, step):
    return lax.ppermute(block, axis, [(i, i ^ step) for i in range(size)])


def dot(left, right, dims):
    return lax.dot_general(
        left, right, (dims, ((), ())), precision=HIGHEST, preferred_element_type=jnp.float32
    )


def one_hot(index, size):
    return (index[:, None] == jnp.arange(size)[None, :]).astype(jnp.float32)


def hamilton(left, right):
    la, lb, lc, ld = jnp.split(left, 4, axis=-1)
    ra, rb, rc, rd = jnp.split(right, 4, axis=-1)
    out_a = la * ra - lb * rb - lc * rc - ld * rd
    out_b = la * rb + lb * ra + lc * rd - ld * rc
    out_c = la * rc - lb * rd + lc * ra + ld * rb
    out_d = la * rd + lb * rc - lc * rb + ld * ra
    return jnp.concatenate([out_a, out_b, out_c, out_d], axis=-1)


def conjugate(rows):
    quarter = rows.shape[-1] // 4
    return jnp.concatenate([rows[:, :quarter], -rows[:, quarter:]], axis=-1)


def four(block):
    return jnp.concatenate([block] * 4, axis=-1)


def fold(rows):
    a, b, c, d = jnp.split(rows, 4, axis=-1)
    return a + b + c + d


def adagrad(values, history, gradient):
    history_new = history + gradient * gradient
    return (values - step_size * gradient / jnp.sqrt(history_new), history_new)


def shards(
    entity,
    entity_acc,
    relation,
    relation_acc,
    send_rows,
    trip_head,
    trip_rel,
    trip_tail,
    neg_part,
    neg_rows,
    *,
    n_dom,
    n_rel,
):
    ents, width = entity.shape
    rels = relation.shape[0]
    slots = send_rows.shape[2]
    n_chip = n_rel // 2
    dom_here = lax.axis_index("dom")
    rel_here = lax.axis_index("rel")
    neg_root = neg_part[0]

    lists = send_rows[0][jnp.arange(n_rel) ^ rel_here].reshape(n_chip, 2, slots)
    own_rows = neg_rows[rel_here]
    outgoing = entity[lists]
    own_negs = entity[own_rows]

    spread = [own_negs] + [exchange(own_negs, "dom", n_dom, s) for s in range(1, n_dom)]
    picked = lax.dynamic_index_in_dim(jnp.stack(spread), dom_here ^ neg_root, 0, keepdims=False)

    from_core = exchange(outgoing[:, 1], "rel", n_rel, 1)
    parcels = jnp.stack([outgoing[:, 0], from_core], axis=1)
    touched = [parcels[0]] + [exchange(parcels[s], "rel", n_rel, 2 * s) for s in range(1, n_chip)]
    touched = jnp.stack(touched).reshape(-1, width)

    half = [picked] + [exchange(picked, "rel", n_rel, 2 * s) for s in range(1, n_chip)]
    half = jnp.concatenate(half, axis=0)

    ra, rb, rc, rd = jnp.split(relation, 4, axis=-1)
    inverse = four(lax.rsqrt(ra * ra + rb * rb + rc * rc + rd * rd))
    unit = relation * inverse
    pick_rel = one_hot(trip_rel, rels)
    pick_head = one_hot(((trip_head // slots) ^ rel_here) * slots + trip_head % slots, n_rel * slots)
    pick_tail = one_hot(((trip_tail // slots) ^ rel_here) * slots + trip_tail % slots, n_rel * slots)
    rotation = dot(pick_rel, unit, ((1,), (0,)))
    head = dot(pick_head, touched, ((1,), (0,)))
    tail = dot(pick_tail, touched, ((1,), (0,)))
    query = hamilton(head, rotation)
    pull = -jax.nn.sigmoid(-jnp.sum(query * tail, axis=-1, keepdims=True))
    queries = jnp.concatenate([query, exchange(query, "rel", n_rel, 1)], axis=0)

    push = jax.nn.sigmoid(dot(queries, half, ((1,), (1,)))) / (2 * half.shape[0])
    grad_half = dot(push, queries, ((0,), (0,)))
    grad_queries = dot(push, half, ((1,), (0,)))

    parts = grad_half.reshape(n_chip, -1, width)
    neg_share = parts[0]
    for s in range(1, n_chip):
        neg_share = neg_share + exchange(parts[s], "rel", n_rel, 2 * s)
    neg_total = neg_share
    for s in range(1, n_dom):
        neg_total = neg_total + exchange(neg_share, "dom", n_dom, s)

    trips = query.shape[0]
    grad_query = grad_queries[:trips] + exchange(grad_queries[trips:], "rel", n_rel, 1) + pull * tail
    grad_head = hamilton(grad_query, conjugate(rotation))
    grad_rot = hamilton(conjugate(head), grad_query)
    grad_touched = dot(pick_head, grad_head, ((0,), (0,))) + dot(
        pick_tail, pull * query, ((0,), (0,))
    )
    grad_unit = dot(pick_rel, grad_rot, ((0,), (0,)))
    rel_grad = inverse * (grad_unit - unit * four(fold(unit * grad_unit)))

    back = grad_touched.reshape(n_chip, 2, slots, width)
    back = jnp.stack([back[0]] + [exchange(back[s], "rel", n_rel, 2 * s) for s in range(1, n_chip)])
    returned = jnp.stack([back[:, 0], exchange(back[:, 1], "rel", n_rel, 1)], axis=1)

    bits = [1 << b for b in range((n_dom - 1).bit_length())]
    middle = rels // 2
    low, high = rel_grad[:middle], rel_grad[middle:]
    for up, down in zip(bits, bits[::-1]):
        low = low + exchange(low, "dom", n_dom, up)
        high = high + exchange(high, "dom", n_dom, down)
    rel_sum = jnp.concatenate([low, high], axis=0)

    is_owner = (dom_here == neg_root).astype(jnp.float32)
    ent_grad = dot(one_hot(lists.reshape(-1), ents), returned.reshape(-1, width), ((0,), (0,)))
    ent_grad = ent_grad + dot(one_hot(own_rows, ents), is_owner * neg_total, ((0,), (0,)))
    new_entity, new_entity_acc = adagrad(entity, entity_acc, ent_grad)
    new_relation, new_relation_acc = adagrad(relation, relation_acc, rel_sum)
    return (new_entity, new_entity_acc, new_relation, new_relation_acc)


def solution(mesh):
    def step(*arrays):
        return shards(*arrays, n_dom=mesh.shape["dom"], n_rel=mesh.shape["rel"])

    both = ("dom", "rel")
    in_specs = (
        P(both, None),
        P(both, None),
        P("rel", None),
        P("rel", None),
        P(both, None, None),
        P(both),
        P(both),
        P(both),
        P(),
        P(),
    )
    out_specs = (P(both, None), P(both, None), P("rel", None), P("rel", None))
    return jax.shard_map(step, mesh=mesh, in_specs=in_specs, out_specs=out_specs, check_vma=False)
```

time: 164 us -> 72.3 us (0.44)
  waiting for transfers between devices: 97.1 us -> 21.6 us
  starting transfers between devices: 11.4 us -> 30 us
  blocking collectives: 14.9 us -> 0 us
  between operations: 14.7 us -> 1.69 us
  other arithmetic: 12.6 us -> 2.59 us
  matrix products: 3.9 us -> 9.65 us
  local copies, waits for them, and re-layouts: 8.85 us -> 6.34 us
    psum x2 -> x0, waiting for transfers between devices: 78.6 us -> none  [the longest x1 44.4 us: shards(): neg_total = lax.psum(neg_share, 'dom')]
    ppermute x0 -> x26, starting transfers between devices: none -> 30 us  [exchange(): return lax.ppermute(block, axis, [(i, i ^ step) for i in range(size)])]
    ppermute x0 -> x26, waiting for transfers between devices: none -> 21.6 us  [exchange(): return lax.ppermute(block, axis, [(i, i ^ step) for i in range(size)])]
    reduce_scatter x1 -> x0, waiting for transfers between devices: 18.4 us -> none  [shards(): lax.psum_scatter(grad_neg, 'rel', scatter_dimension=0, tiled=True)]
    all_gather x1 -> x0, blocking collectives: 14.9 us -> none  [shards(): negatives = lax.all_gather(spread, 'rel', axis=0, tiled=True)]
    all_to_all x2 -> x0, starting transfers between devices: 11.3 us -> none  [the longest x1 6.46 us: shards(): lax.all_to_all(outgoing, 'rel', split_axis=0, concat_axis=0, tiled=True)]
    scatter-add x4 -> x0, other arithmetic: 7.05 us -> none  [the longest x1 2.24 us: local_loss(): positive = jnp.sum(query * touched[tails], axis=-1)]
    dot_general x5 -> x11, matrix products: 3.9 us -> 9.65 us  [dot(): lax.dot_general(left, right, (dims, ((), ())), precision=HIGHEST, preferr...]
  transfers between devices with their start and end apart: 5 -> 26, of which waited for: 3 -> 13; matrix products, arithmetic and copies ran while one was open for 6% -> 11% of each run, Pallas kernels for 0% -> 0%
where the time goes in v1:
time: 72.3 us; the launch traced here: 71.9 us
  starting transfers between devices  30 us (41%)
  waiting for transfers between devices  21.6 us (30%)
  matrix products  9.65 us (13%)
  local copies, waits for them, and re-layouts  6.34 us (9%)
  other arithmetic  2.59 us (4%)
  between operations  1.69 us (2%)
    ppermute x26, starting transfers between devices, exchange(): return lax.ppermute(block, axis, [(i, i ^ step) for i in range(size)])  30 us
    ppermute x26, waiting for transfers between devices, exchange(): return lax.ppermute(block, axis, [(i, i ^ step) for i in range(size)])  21.6 us
    dot_general x11, matrix products, dot(): lax.dot_general(left, right, (dims, ((), ())), precision=HIGHEST, preferr...  9.65 us
    unnamed x16, local copies, waits for them, and re-layouts  2.4 us
    gather x1, local copies, waits for them, and re-layouts, shards(): own_negs = entity[own_rows]  1.64 us
  transfers between devices with their start and end apart: 26, of which 13 were waited for; matrix products, arithmetic and copies ran while one was open for 11% of the time, Pallas kernels for 0%

profile of v1, /device:TPU:0, one launch (start us, length us, event | category | flops | bytes accessed | tf_op | source)
XLA Modules:
  0.0 71.9 jit_solution(3448399289143042596)
XLA Ops:
  0.7 0.7 fusion.60
  1.4 1.6 %gather_fusion.2 = f32[32,512]{1,0:T(8,128)S(1)} fusion(f32[128,512]{1,0:T(8,128)} %param.10, s32[1024]{0:T(1024)S(1)} %pad_clamp_fusion), kind=kCustom, calls=%fused_computation.2 | custom fusion | bytes 131200 | tf_op jit(solution)/shard_map/gather | solution.py:79
  3.0 3.0 %collective-permute-start.5 = (f32[32,512]{1,0:T(8,128)S(1)}, f32[32,512]{1,0:T(8,128)S(1)}, u32[]{:S(2)}, u32[]{:S(2)}) collective-permute-start(f32[32,512]{1,0:T(8,128)S(1)} %gather_fusion.2), channel_id=1, source_target_pairs={{0,8},{8,0},{16,24},{24,16},{1,9},{9,1},{17,25},{25,17},{2,10},{10... | collective-permute-start | bytes 196616 | tf_op jit(solution)/shard_map/ppermute | solution.py:11
  6.0 1.5 %collective-permute-start.6 = (f32[32,512]{1,0:T(8,128)S(1)}, f32[32,512]{1,0:T(8,128)S(1)}, u32[]{:S(2)}, u32[]{:S(2)}) collective-permute-start(f32[32,512]{1,0:T(8,128)S(1)} %gather_fusion.2), channel_id=1, source_target_pairs={{0,16},{8,24},{16,0},{24,8},{1,17},{9,25},{17,1},{25,9},{2,18},{10... | collective-permute-start | bytes 196616 | tf_op jit(solution)/shard_map/ppermute | solution.py:11
  7.6 0.6 gather_fusion
  8.2 0.8 %gather_fusion.1 = f32[128,512]{1,0:T(8,128)S(1)} fusion(f32[128,512]{1,0:T(8,128)S(1)} %copy-done.1, s32[1024]{0:T(1024)S(1)} %pad_clamp_fusion.1), kind=kCustom, calls=%fused_computation.1 | custom fusion | bytes 524800 | tf_op jit(solution)/shard_map/gather | solution.py:78
  9.1 0.8 %copy-done.2 = f32[128,512]{1,0:T(8,128)S(1)} copy-done((f32[128,512]{1,0:T(8,128)S(1)}, f32[128,512]{1,0:T(8,128)}, u32[]{:S(2)}) %copy-start.2) | copy-done | bytes 262168
  10.0 0.4 fusion.29
  10.7 3.7 %collective-permute-start.3 = (f32[2,16,512]{2,1,0:T(8,128)S(1)}, f32[2,16,512]{2,1,0:T(8,128)S(1)}, u32[]{:S(2)}, u32[]{:S(2)}) collective-permute-start(f32[2,16,512]{2,1,0:T(8,128)S(1)} %get-tuple-element.37), channel_id=1, source_target_pairs={{0,6},{1,7},{2,4},{3,5},{4,2},{5,3},{6,0},{7,1},{8,14},{9,15},{10,... | collective-permute-start | bytes 196616 | tf_op jit(solution)/shard_map/ppermute | solution.py:11
  14.4 0.8 %collective-permute-start.1 = (f32[2,16,512]{2,1,0:T(8,128)S(1)}, f32[2,16,512]{2,1,0:T(8,128)S(1)}, u32[]{:S(2)}, u32[]{:S(2)}) collective-permute-start(f32[2,16,512]{2,1,0:T(8,128)S(1)} %get-tuple-element.36), channel_id=1, source_target_pairs={{0,2},{1,3},{2,0},{3,1},{4,6},{5,7},{6,4},{7,5},{8,10},{9,11},{10,... | collective-permute-start | bytes 196616 | tf_op jit(solution)/shard_map/ppermute | solution.py:11
  15.2 2.2 %collective-permute-done.3 = f32[2,16,512]{2,1,0:T(8,128)S(1)} collective-permute-done((f32[2,16,512]{2,1,0:T(8,128)S(1)}, f32[2,16,512]{2,1,0:T(8,128)S(1)}, u32[]{:S(2)}, u32[]{:S(2)}) %collective-permute-start.3) | collective-permute-done | bytes 65568 | tf_op jit(solution)/shard_map/ppermute | solution.py:11
  17.4 2.7 %collective-permute-done.2 = f32[2,16,512]{2,1,0:T(8,128)S(1)} collective-permute-done((f32[2,16,512]{2,1,0:T(8,128)S(1)}, f32[2,16,512]{2,1,0:T(8,128)S(1)}, u32[]{:S(2)}, u32[]{:S(2)}) %collective-permute-start.2) | collective-permute-done | bytes 65568 | tf_op jit(solution)/shard_map/ppermute | solution.py:11
  20.1 0.4 fusion.30
  20.7 1.2 %multiply_reduce_fusion = (f32[256]{0:T(256)S(1)}, f32[256,512]{1,0:T(8,128)}, f32[256,512]{1,0:T(8,128)S(1)}) fusion(f32[256,128]{1,0:T(8,128)S(1)} %get-tuple-element.17, f32[256,128]{1,0:T(8,128)S(1)} %get-tuple-element.19, f32[256,128]{1,0:T(8,128)S(1)} %get-tuple-element.18, f32[256,128]{1,0:T(8,128)S(1)} %get-tuple-element.16, ...), kind=kOutput, calls=%fused_computation.31 | convolution fusion | flops 202014464 | bytes 1837056 | tf_op jit(solution)/shard_map/dot_general | solution.py:15
  22.6 0.7 fusion.61
  23.4 3.0 %collective-permute-start.10 = (f32[32,512]{1,0:T(8,128)S(1)}, f32[32,512]{1,0:T(8,128)S(1)}, u32[]{:S(2)}, u32[]{:S(2)}) collective-permute-start(f32[32,512]{1,0:T(8,128)S(1)} %fusion.34), channel_id=1, source_target_pairs={{0,6},{1,7},{2,4},{3,5},{4,2},{5,3},{6,0},{7,1},{8,14},{9,15},{10,... | collective-permute-start | bytes 196616 | tf_op jit(solution)/shard_map/ppermute | solution.py:11
  26.4 1.4 %collective-permute-start.8 = (f32[32,512]{1,0:T(8,128)S(1)}, f32[32,512]{1,0:T(8,128)S(1)}, u32[]{:S(2)}, u32[]{:S(2)}) collective-permute-start(f32[32,512]{1,0:T(8,128)S(1)} %fusion.34), channel_id=1, source_target_pairs={{0,2},{1,3},{2,0},{3,1},{4,6},{5,7},{6,4},{7,5},{8,10},{9,11},{10,... | collective-permute-start | bytes 196616 | tf_op jit(solution)/shard_map/ppermute | solution.py:11
  27.9 2.4 %collective-permute-done.10 = f32[32,512]{1,0:T(8,128)S(1)} collective-permute-done((f32[32,512]{1,0:T(8,128)S(1)}, f32[32,512]{1,0:T(8,128)S(1)}, u32[]{:S(2)}, u32[]{:S(2)}) %collective-permute-start.10) | collective-permute-done | bytes 65568 | tf_op jit(solution)/shard_map/ppermute | solution.py:11
  30.3 2.5 %collective-permute-done.9 = f32[32,512]{1,0:T(8,128)S(1)} collective-permute-done((f32[32,512]{1,0:T(8,128)S(1)}, f32[32,512]{1,0:T(8,128)S(1)}, u32[]{:S(2)}, u32[]{:S(2)}) %collective-permute-start.9) | collective-permute-done | bytes 65568 | tf_op jit(solution)/shard_map/ppermute | solution.py:11
  32.8 2.0 %fusion.3 = f32[512,128]{1,0:T(8,128)S(1)} fusion(f32[256,512]{1,0:T(8,128)} %collective-permute-done.4, f32[256,128]{1,0:T(8,128)S(1)} %get-tuple-element.17, f32[256,128]{1,0:T(8,128)S(1)} %get-tuple-element.19, f32[256,128]{1,0:T(8,128)S(1)} %get-tuple-element.18, f32[256,128]{1,0:T(8,128)S(1)} %get-tuple-element.16, ...), kind=kOutput, calls=%fused_computation.9 | convolution fusion | flops 404160512 | bytes 1572864 | tf_op jit(solution)/shard_map/dot_general | solution.py:15
  34.8 1.8 %fusion.22 = f32[128,512]{1,0:T(8,128)S(1)} fusion(f32[512,128]{1,0:T(8,128)S(1)} %fusion.3, f32[256,512]{1,0:T(8,128)} %collective-permute-done.4, f32[256,128]{1,0:T(8,128)S(1)} %get-tuple-element.17, f32[256,128]{1,0:T(8,128)S(1)} %get-tuple-element.19, f32[256,128]{1,0:T(8,128)S(1)} %get-tuple-element.18, f32[256,128]{1,0:T(8,128)S(1)} %get-tuple-element.16), kind=kOutput, calls=%fused_computation.32 | convolution fusion | flops 403701760 | bytes 1572864 | tf_op jit(solution)/shard_map/dot_general | solution.py:15
  36.7 2.5 %collective-permute-start.18 = (f32[32,512]{1,0:T(8,128)S(1)}, f32[32,512]{1,0:T(8,128)S(1)}, u32[]{:S(2)}, u32[]{:S(2)}) collective-permute-start(f32[32,512]{1,0:T(8,128)S(1)} %get-tuple-element.33), channel_id=1, source_target_pairs={{0,6},{1,7},{2,4},{3,5},{4,2},{5,3},{6,0},{7,1},{8,14},{9,15},{10,... | collective-permute-start | bytes 196616 | tf_op jit(solution)/shard_map/ppermute | solution.py:11
  39.2 1.9 %collective-permute-start.16 = (f32[32,512]{1,0:T(8,128)S(1)}, f32[32,512]{1,0:T(8,128)S(1)}, u32[]{:S(2)}, u32[]{:S(2)}) collective-permute-start(f32[32,512]{1,0:T(8,128)S(1)} %get-tuple-element.32), channel_id=1, source_target_pairs={{0,2},{1,3},{2,0},{3,1},{4,6},{5,7},{6,4},{7,5},{8,10},{9,11},{10,... | collective-permute-start | bytes 196616 | tf_op jit(solution)/shard_map/ppermute | solution.py:11
  41.1 1.0 %fusion.27 = f32[512,512]{1,0:T(8,128)S(1)} fusion(f32[512,128]{1,0:T(8,128)S(1)} %fusion.3, f32[32,512]{1,0:T(8,128)S(1)} %collective-permute-done.10, f32[32,512]{1,0:T(8,128)S(1)} %collective-permute-done.9, f32[32,512]{1,0:T(8,128)S(1)} %collective-permute-done.8, f32[32,512]{1,0:T(8,128)S(1)} %fusion.34), kind=kOutput, calls=%fused_computation.60 | convolution fusion | flops 402849792 | bytes 1572864 | tf_op jit(solution)/shard_map/dot_general | solution.py:15
  42.2 1.2 %collective-permute-done.18 = f32[32,512]{1,0:T(8,128)S(1)} collective-permute-done((f32[32,512]{1,0:T(8,128)S(1)}, f32[32,512]{1,0:T(8,128)S(1)}, u32[]{:S(2)}, u32[]{:S(2)}) %collective-permute-start.18) | collective-permute-done | bytes 65568 | tf_op jit(solution)/shard_map/ppermute | solution.py:11
  43.4 2.0 %collective-permute-done.17 = f32[32,512]{1,0:T(8,128)S(1)} collective-permute-done((f32[32,512]{1,0:T(8,128)S(1)}, f32[32,512]{1,0:T(8,128)S(1)}, u32[]{:S(2)}, u32[]{:S(2)}) %collective-permute-start.17) | collective-permute-done | bytes 65568 | tf_op jit(solution)/shard_map/ppermute | solution.py:11
  45.5 1.4 %collective-permute-start.21 = (f32[32,512]{1,0:T(8,128)S(1)}, f32[32,512]{1,0:T(8,128)S(1)}, u32[]{:S(2)}, u32[]{:S(2)}) collective-permute-start(f32[32,512]{1,0:T(8,128)S(1)} %fusion.41), channel_id=1, source_target_pairs={{0,24},{8,16},{16,8},{24,0},{1,25},{9,17},{17,9},{25,1},{2,26},{10... | collective-permute-start | bytes 196616 | tf_op jit(solution)/shard_map/ppermute | solution.py:11
  46.8 0.7 collective-permute-start.20
  47.5 1.5 %collective-permute-start.19 = (f32[32,512]{1,0:T(8,128)S(1)}, f32[32,512]{1,0:T(8,128)S(1)}, u32[]{:S(2)}, u32[]{:S(2)}) collective-permute-start(f32[32,512]{1,0:T(8,128)S(1)} %fusion.41), channel_id=1, source_target_pairs={{0,8},{8,0},{16,24},{24,16},{1,9},{9,1},{17,25},{25,17},{2,10},{10... | collective-permute-start | bytes 196616 | tf_op jit(solution)/shard_map/ppermute | solution.py:11
  49.0 2.1 %collective-permute-done.21 = f32[32,512]{1,0:T(8,128)S(1)} collective-permute-done((f32[32,512]{1,0:T(8,128)S(1)}, f32[32,512]{1,0:T(8,128)S(1)}, u32[]{:S(2)}, u32[]{:S(2)}) %collective-permute-start.21) | collective-permute-done | bytes 65568 | tf_op jit(solution)/shard_map/ppermute | solution.py:11
  51.1 0.7 collective-permute-done.20
  51.8 0.4 fusion.43
  53.1 0.4 convolution_add_fusion.1
  53.6 2.3 %collective-permute-start.14 = (f32[2,16,512]{2,1,0:T(8,128)S(1)}, f32[2,16,512]{2,1,0:T(8,128)S(1)}, u32[]{:S(2)}, u32[]{:S(2)}) collective-permute-start(f32[2,16,512]{2,1,0:T(8,128)S(1)} %bitcast.73), channel_id=1, source_target_pairs={{0,6},{1,7},{2,4},{3,5},{4,2},{5,3},{6,0},{7,1},{8,14},{9,15},{10,... | collective-permute-start | bytes 196616 | tf_op jit(solution)/shard_map/ppermute | solution.py:11
  55.9 2.1 %collective-permute-start.12 = (f32[2,16,512]{2,1,0:T(8,128)S(1)}, f32[2,16,512]{2,1,0:T(8,128)S(1)}, u32[]{:S(2)}, u32[]{:S(2)}) collective-permute-start(f32[2,16,512]{2,1,0:T(8,128)S(1)} %bitcast.69), channel_id=1, source_target_pairs={{0,2},{1,3},{2,0},{3,1},{4,6},{5,7},{6,4},{7,5},{8,10},{9,11},{10,... | collective-permute-start | bytes 196616 | tf_op jit(solution)/shard_map/ppermute | solution.py:11
  58.1 0.4 fusion.67
  58.6 1.5 %collective-permute-start.22 = (f32[64,512]{1,0:T(8,128)S(1)}, f32[64,512]{1,0:T(8,128)S(1)}, u32[]{:S(2)}, u32[]{:S(2)}) collective-permute-start(f32[64,512]{1,0:T(8,128)S(1)} %get-tuple-element.24), channel_id=1, source_target_pairs={{0,8},{8,0},{16,24},{24,16},{1,9},{9,1},{17,25},{25,17},{2,10},{10... | collective-permute-start | bytes 393224 | tf_op jit(solution)/shard_map/ppermute | solution.py:11
  60.1 0.5 collective-permute-start.24
  60.6 1.5 %collective-permute-done.13 = f32[2,16,512]{2,1,0:T(8,128)S(1)} collective-permute-done((f32[2,16,512]{2,1,0:T(8,128)S(1)}, f32[2,16,512]{2,1,0:T(8,128)S(1)}, u32[]{:S(2)}, u32[]{:S(2)}) %collective-permute-start.13) | collective-permute-done | bytes 65568 | tf_op jit(solution)/shard_map/ppermute | solution.py:11
  62.2 1.4 %collective-permute-done.22 = f32[64,512]{1,0:T(8,128)S(1)} collective-permute-done((f32[64,512]{1,0:T(8,128)S(1)}, f32[64,512]{1,0:T(8,128)S(1)}, u32[]{:S(2)}, u32[]{:S(2)}) %collective-permute-start.22) | collective-permute-done | bytes 131104 | tf_op jit(solution)/shard_map/ppermute | solution.py:11
  63.6 1.4 %collective-permute-done.24 = f32[64,512]{1,0:T(8,128)S(1)} collective-permute-done((f32[64,512]{1,0:T(8,128)S(1)}, f32[64,512]{1,0:T(8,128)S(1)}, u32[]{:S(2)}, u32[]{:S(2)}) %collective-permute-start.24) | collective-permute-done | bytes 131104 | tf_op jit(solution)/shard_map/ppermute | solution.py:11
  65.1 0.7 collective-permute-start.25
  65.7 1.3 %collective-permute-start.23 = (f32[64,512]{1,0:T(8,128)S(1)}, f32[64,512]{1,0:T(8,128)S(1)}, u32[]{:S(2)}, u32[]{:S(2)}) collective-permute-start(f32[64,512]{1,0:T(8,128)S(1)} %get-tuple-element.22), channel_id=1, source_target_pairs={{0,16},{8,24},{16,0},{24,8},{1,17},{9,25},{17,1},{25,9},{2,18},{10... | collective-permute-start | bytes 393224 | tf_op jit(solution)/shard_map/ppermute | solution.py:11
  67.0 0.9 %copy-done.4 = f32[128,512]{1,0:T(8,128)S(1)} copy-done((f32[128,512]{1,0:T(8,128)S(1)}, f32[128,512]{1,0:T(8,128)}, u32[]{:S(2)}) %copy-start.4) | copy-done | bytes 262168
  67.9 1.2 %multiply_subtract_fusion.1 = (f32[128,512]{1,0:T(8,128)}, f32[128,512]{1,0:T(8,128)}) fusion(f32[128,512]{1,0:T(8,128)S(1)} %copy-done.1, f32[128,512]{1,0:T(8,128)S(1)} %copy-done.4, f32[128,512]{1,0:T(8,128)S(1)} %fusion.43, f32[128,512]{1,0:T(8,128)S(1)} %bitcast.61, s32[128]{0:T(128)S(1)} %eq.75), kind=kOutput, calls=%fused_computation.56 | convolution fusion | flops 101072896 | bytes 1573376 | tf_op jit(solution)/shard_map/dot_general | solution.py:15
  69.2 0.9 %collective-permute-done.25 = f32[64,512]{1,0:T(8,128)S(1)} collective-permute-done((f32[64,512]{1,0:T(8,128)S(1)}, f32[64,512]{1,0:T(8,128)S(1)}, u32[]{:S(2)}, u32[]{:S(2)}) %collective-permute-start.25) | collective-permute-done | bytes 131104 | tf_op jit(solution)/shard_map/ppermute | solution.py:11
  70.1 0.6 collective-permute-done.23
  71.1 0.8 %multiply_subtract_fusion = (f32[128,512]{1,0:T(8,128)}, f32[128,512]{1,0:T(8,128)}) fusion(f32[128,512]{1,0:T(8,128)S(1)} %copy-done.2, f32[64,512]{1,0:T(8,128)S(1)} %add.243, f32[64,512]{1,0:T(8,128)S(1)} %add.241, f32[128,512]{1,0:T(8,128)S(1)} %copy-done.3), kind=kLoop, calls=%fused_computation.54 | loop fusion | flops 393216 | bytes 1310720 | tf_op jit(solution)/shard_map/sub | solution.py:50
  (74 shorter events, 2.6 us)
Async XLA Ops:
  0.6 6.9 %copy-start = (s32[1,8,16]{2,1,0:T(8,128)S(1)}, s32[1,8,16]{2,1,0:T(8,128)}, u32[]{:S(2)}) copy-start(s32[1,8,16]{2,1,0:T(8,128)} %param.14) | copy-start | bytes 1540
  1.4 6.9 %copy-start.1 = (f32[128,512]{1,0:T(8,128)S(1)}, f32[128,512]{1,0:T(8,128)}, u32[]{:S(2)}) copy-start(f32[128,512]{1,0:T(8,128)} %param.10) | copy-start | bytes 786436
  3.0 20.3 %collective-permute-start.5 = (f32[32,512]{1,0:T(8,128)S(1)}, f32[32,512]{1,0:T(8,128)S(1)}, u32[]{:S(2)}, u32[]{:S(2)}) collective-permute-start(f32[32,512]{1,0:T(8,128)S(1)} %gather_fusion.2), channel_id=1, source_target_pairs={{0,8},{8,0},{16,24},{24,16},{1,9},{9,1},{17,25},{25,17},{2,10},{10... | collective-permute-start | bytes 196616 | tf_op jit(solution)/shard_map/ppermute | solution.py:11
  6.0 17.3 %collective-permute-start.6 = (f32[32,512]{1,0:T(8,128)S(1)}, f32[32,512]{1,0:T(8,128)S(1)}, u32[]{:S(2)}, u32[]{:S(2)}) collective-permute-start(f32[32,512]{1,0:T(8,128)S(1)} %gather_fusion.2), channel_id=1, source_target_pairs={{0,16},{8,24},{16,0},{24,8},{1,17},{9,25},{17,1},{25,9},{2,18},{10... | collective-permute-start | bytes 196616 | tf_op jit(solution)/shard_map/ppermute | solution.py:11
  9.0 1.0 %copy-start.2 = (f32[128,512]{1,0:T(8,128)S(1)}, f32[128,512]{1,0:T(8,128)}, u32[]{:S(2)}) copy-start(f32[128,512]{1,0:T(8,128)} %param.12) | copy-start | bytes 786436
  9.0 0.9 %copy-start.5 = (s32[256]{0:T(256)S(1)}, s32[256]{0:T(256)}, u32[]{:S(2)}) copy-start(s32[256]{0:T(256)} %param.16) | copy-start | bytes 3076
  9.0 1.6 %collective-permute-start = (f32[4,16,512]{2,1,0:T(8,128)S(1)}, f32[4,16,512]{2,1,0:T(8,128)S(1)}, u32[]{:S(2)}, u32[]{:S(2)}) collective-permute-start(f32[4,16,512]{2,1,0:T(8,128)S(1)} %get-tuple-element.40), channel_id=1, source_target_pairs={{0,1},{1,0},{2,3},{3,2},{4,5},{5,4},{6,7},{7,6},{8,9},{9,8},{10,11... | collective-permute-start | bytes 393224 | tf_op jit(solution)/shard_map/ppermute | solution.py:11
  10.0 0.7 copy-start.6
  10.7 6.6 %collective-permute-start.3 = (f32[2,16,512]{2,1,0:T(8,128)S(1)}, f32[2,16,512]{2,1,0:T(8,128)S(1)}, u32[]{:S(2)}, u32[]{:S(2)}) collective-permute-start(f32[2,16,512]{2,1,0:T(8,128)S(1)} %get-tuple-element.37), channel_id=1, source_target_pairs={{0,6},{1,7},{2,4},{3,5},{4,2},{5,3},{6,0},{7,1},{8,14},{9,15},{10,... | collective-permute-start | bytes 196616 | tf_op jit(solution)/shard_map/ppermute | solution.py:11
  14.4 0.8 %copy-start.7 = (s32[256]{0:T(256)S(1)}, s32[256]{0:T(256)}, u32[]{:S(2)}) copy-start(s32[256]{0:T(256)} %param.17) | copy-start | bytes 3076
  14.4 5.7 %collective-permute-start.2 = (f32[2,16,512]{2,1,0:T(8,128)S(1)}, f32[2,16,512]{2,1,0:T(8,128)S(1)}, u32[]{:S(2)}, u32[]{:S(2)}) collective-permute-start(f32[2,16,512]{2,1,0:T(8,128)S(1)} %get-tuple-element.38), channel_id=1, source_target_pairs={{0,4},{1,5},{2,6},{3,7},{4,0},{5,1},{6,2},{7,3},{8,12},{9,13},{10,... | collective-permute-start | bytes 196616 | tf_op jit(solution)/shard_map/ppermute | solution.py:11
  14.4 5.7 %collective-permute-start.1 = (f32[2,16,512]{2,1,0:T(8,128)S(1)}, f32[2,16,512]{2,1,0:T(8,128)S(1)}, u32[]{:S(2)}, u32[]{:S(2)}) collective-permute-start(f32[2,16,512]{2,1,0:T(8,128)S(1)} %get-tuple-element.36), channel_id=1, source_target_pairs={{0,2},{1,3},{2,0},{3,1},{4,6},{5,7},{6,4},{7,5},{8,10},{9,11},{10,... | collective-permute-start | bytes 196616 | tf_op jit(solution)/shard_map/ppermute | solution.py:11
  17.3 6.0 %collective-permute-start.7 = (f32[32,512]{1,0:T(8,128)S(1)}, f32[32,512]{1,0:T(8,128)S(1)}, u32[]{:S(2)}, u32[]{:S(2)}) collective-permute-start(f32[32,512]{1,0:T(8,128)S(1)} %gather_fusion.2), channel_id=1, source_target_pairs={{0,24},{8,16},{16,8},{24,0},{1,25},{9,17},{17,9},{25,1},{2,26},{10... | collective-permute-start | bytes 196616 | tf_op jit(solution)/shard_map/ppermute | solution.py:11
  21.9 10.9 %collective-permute-start.4 = (f32[256,512]{1,0:T(8,128)}, f32[256,512]{1,0:T(8,128)}, u32[]{:S(2)}, u32[]{:S(2)}) collective-permute-start(f32[256,512]{1,0:T(8,128)} %get-tuple-element.21), channel_id=1, source_target_pairs={{0,1},{1,0},{2,3},{3,2},{4,5},{5,4},{6,7},{7,6},{8,9},{9,8},{10,11... | collective-permute-start | bytes 1572872 | tf_op jit(solution)/shard_map/ppermute | solution.py:11
  23.4 6.9 %collective-permute-start.10 = (f32[32,512]{1,0:T(8,128)S(1)}, f32[32,512]{1,0:T(8,128)S(1)}, u32[]{:S(2)}, u32[]{:S(2)}) collective-permute-start(f32[32,512]{1,0:T(8,128)S(1)} %fusion.34), channel_id=1, source_target_pairs={{0,6},{1,7},{2,4},{3,5},{4,2},{5,3},{6,0},{7,1},{8,14},{9,15},{10,... | collective-permute-start | bytes 196616 | tf_op jit(solution)/shard_map/ppermute | solution.py:11
  26.4 6.3 %collective-permute-start.9 = (f32[32,512]{1,0:T(8,128)S(1)}, f32[32,512]{1,0:T(8,128)S(1)}, u32[]{:S(2)}, u32[]{:S(2)}) collective-permute-start(f32[32,512]{1,0:T(8,128)S(1)} %fusion.34), channel_id=1, source_target_pairs={{0,4},{1,5},{2,6},{3,7},{4,0},{5,1},{6,2},{7,3},{8,12},{9,13},{10,... | collective-permute-start | bytes 196616 | tf_op jit(solution)/shard_map/ppermute | solution.py:11
  26.4 6.3 %collective-permute-start.8 = (f32[32,512]{1,0:T(8,128)S(1)}, f32[32,512]{1,0:T(8,128)S(1)}, u32[]{:S(2)}, u32[]{:S(2)}) collective-permute-start(f32[32,512]{1,0:T(8,128)S(1)} %fusion.34), channel_id=1, source_target_pairs={{0,2},{1,3},{2,0},{3,1},{4,6},{5,7},{6,4},{7,5},{8,10},{9,11},{10,... | collective-permute-start | bytes 196616 | tf_op jit(solution)/shard_map/ppermute | solution.py:11
  36.7 6.8 %collective-permute-start.18 = (f32[32,512]{1,0:T(8,128)S(1)}, f32[32,512]{1,0:T(8,128)S(1)}, u32[]{:S(2)}, u32[]{:S(2)}) collective-permute-start(f32[32,512]{1,0:T(8,128)S(1)} %get-tuple-element.33), channel_id=1, source_target_pairs={{0,6},{1,7},{2,4},{3,5},{4,2},{5,3},{6,0},{7,1},{8,14},{9,15},{10,... | collective-permute-start | bytes 196616 | tf_op jit(solution)/shard_map/ppermute | solution.py:11
  39.2 6.2 %collective-permute-start.17 = (f32[32,512]{1,0:T(8,128)S(1)}, f32[32,512]{1,0:T(8,128)S(1)}, u32[]{:S(2)}, u32[]{:S(2)}) collective-permute-start(f32[32,512]{1,0:T(8,128)S(1)} %get-tuple-element.34), channel_id=1, source_target_pairs={{0,4},{1,5},{2,6},{3,7},{4,0},{5,1},{6,2},{7,3},{8,12},{9,13},{10,... | collective-permute-start | bytes 196616 | tf_op jit(solution)/shard_map/ppermute | solution.py:11
  39.2 6.2 %collective-permute-start.16 = (f32[32,512]{1,0:T(8,128)S(1)}, f32[32,512]{1,0:T(8,128)S(1)}, u32[]{:S(2)}, u32[]{:S(2)}) collective-permute-start(f32[32,512]{1,0:T(8,128)S(1)} %get-tuple-element.32), channel_id=1, source_target_pairs={{0,2},{1,3},{2,0},{3,1},{4,6},{5,7},{6,4},{7,5},{8,10},{9,11},{10,... | collective-permute-start | bytes 196616 | tf_op jit(solution)/shard_map/ppermute | solution.py:11
  42.1 10.1 %collective-permute-start.11 = (f32[256,512]{1,0:T(8,128)S(1)}, f32[256,512]{1,0:T(8,128)S(1)}, u32[]{:S(2)}, u32[]{:S(2)}) collective-permute-start(f32[256,512]{1,0:T(8,128)S(1)} %slice.116), channel_id=1, source_target_pairs={{0,1},{1,0},{2,3},{3,2},{4,5},{5,4},{6,7},{7,6},{8,9},{9,8},{10,11... | collective-permute-start | bytes 1572872 | tf_op jit(solution)/shard_map/ppermute | solution.py:11
  45.5 5.7 %collective-permute-start.21 = (f32[32,512]{1,0:T(8,128)S(1)}, f32[32,512]{1,0:T(8,128)S(1)}, u32[]{:S(2)}, u32[]{:S(2)}) collective-permute-start(f32[32,512]{1,0:T(8,128)S(1)} %fusion.41), channel_id=1, source_target_pairs={{0,24},{8,16},{16,8},{24,0},{1,25},{9,17},{17,9},{25,1},{2,26},{10... | collective-permute-start | bytes 196616 | tf_op jit(solution)/shard_map/ppermute | solution.py:11
  46.8 5.0 %collective-permute-start.20 = (f32[32,512]{1,0:T(8,128)S(1)}, f32[32,512]{1,0:T(8,128)S(1)}, u32[]{:S(2)}, u32[]{:S(2)}) collective-permute-start(f32[32,512]{1,0:T(8,128)S(1)} %fusion.41), channel_id=1, source_target_pairs={{0,16},{8,24},{16,0},{24,8},{1,17},{9,25},{17,1},{25,9},{2,18},{10... | collective-permute-start | bytes 196616 | tf_op jit(solution)/shard_map/ppermute | solution.py:11
  47.5 4.3 %collective-permute-start.19 = (f32[32,512]{1,0:T(8,128)S(1)}, f32[32,512]{1,0:T(8,128)S(1)}, u32[]{:S(2)}, u32[]{:S(2)}) collective-permute-start(f32[32,512]{1,0:T(8,128)S(1)} %fusion.41), channel_id=1, source_target_pairs={{0,8},{8,0},{16,24},{24,16},{1,9},{9,1},{17,25},{25,17},{2,10},{10... | collective-permute-start | bytes 196616 | tf_op jit(solution)/shard_map/ppermute | solution.py:11
  53.6 7.0 %collective-permute-start.14 = (f32[2,16,512]{2,1,0:T(8,128)S(1)}, f32[2,16,512]{2,1,0:T(8,128)S(1)}, u32[]{:S(2)}, u32[]{:S(2)}) collective-permute-start(f32[2,16,512]{2,1,0:T(8,128)S(1)} %bitcast.73), channel_id=1, source_target_pairs={{0,6},{1,7},{2,4},{3,5},{4,2},{5,3},{6,0},{7,1},{8,14},{9,15},{10,... | collective-permute-start | bytes 196616 | tf_op jit(solution)/shard_map/ppermute | solution.py:11
  55.9 6.1 %collective-permute-start.13 = (f32[2,16,512]{2,1,0:T(8,128)S(1)}, f32[2,16,512]{2,1,0:T(8,128)S(1)}, u32[]{:S(2)}, u32[]{:S(2)}) collective-permute-start(f32[2,16,512]{2,1,0:T(8,128)S(1)} %bitcast.71), channel_id=1, source_target_pairs={{0,4},{1,5},{2,6},{3,7},{4,0},{5,1},{6,2},{7,3},{8,12},{9,13},{10,... | collective-permute-start | bytes 196616 | tf_op jit(solution)/shard_map/ppermute | solution.py:11
  55.9 6.1 %collective-permute-start.12 = (f32[2,16,512]{2,1,0:T(8,128)S(1)}, f32[2,16,512]{2,1,0:T(8,128)S(1)}, u32[]{:S(2)}, u32[]{:S(2)}) collective-permute-start(f32[2,16,512]{2,1,0:T(8,128)S(1)} %bitcast.69), channel_id=1, source_target_pairs={{0,2},{1,3},{2,0},{3,1},{4,6},{5,7},{6,4},{7,5},{8,10},{9,11},{10,... | collective-permute-start | bytes 196616 | tf_op jit(solution)/shard_map/ppermute | solution.py:11
  58.6 5.0 %collective-permute-start.22 = (f32[64,512]{1,0:T(8,128)S(1)}, f32[64,512]{1,0:T(8,128)S(1)}, u32[]{:S(2)}, u32[]{:S(2)}) collective-permute-start(f32[64,512]{1,0:T(8,128)S(1)} %get-tuple-element.24), channel_id=1, source_target_pairs={{0,8},{8,0},{16,24},{24,16},{1,9},{9,1},{17,25},{25,17},{2,10},{10... | collective-permute-start | bytes 393224 | tf_op jit(solution)/shard_map/ppermute | solution.py:11
  60.1 5.0 %collective-permute-start.24 = (f32[64,512]{1,0:T(8,128)S(1)}, f32[64,512]{1,0:T(8,128)S(1)}, u32[]{:S(2)}, u32[]{:S(2)}) collective-permute-start(f32[64,512]{1,0:T(8,128)S(1)} %get-tuple-element.25), channel_id=1, source_target_pairs={{0,16},{8,24},{16,0},{24,8},{1,17},{9,25},{17,1},{25,9},{2,18},{10... | collective-permute-start | bytes 393224 | tf_op jit(solution)/shard_map/ppermute | solution.py:11
  62.1 4.9 %collective-permute-start.15 = (f32[4,16,512]{2,1,0:T(8,128)S(1)}, f32[4,16,512]{2,1,0:T(8,128)S(1)}, u32[]{:S(2)}, u32[]{:S(2)}) collective-permute-start(f32[4,16,512]{2,1,0:T(8,128)S(1)} %get-tuple-element.27), channel_id=1, source_target_pairs={{0,1},{1,0},{2,3},{3,2},{4,5},{5,4},{6,7},{7,6},{8,9},{9,8},{10,11... | collective-permute-start | bytes 393224 | tf_op jit(solution)/shard_map/ppermute | solution.py:11
  65.1 5.0 %collective-permute-start.25 = (f32[64,512]{1,0:T(8,128)S(1)}, f32[64,512]{1,0:T(8,128)S(1)}, u32[]{:S(2)}, u32[]{:S(2)}) collective-permute-start(f32[64,512]{1,0:T(8,128)S(1)} %get-tuple-element.23), channel_id=1, source_target_pairs={{0,8},{8,0},{16,24},{24,16},{1,9},{9,1},{17,25},{25,17},{2,10},{10... | collective-permute-start | bytes 393224 | tf_op jit(solution)/shard_map/ppermute | solution.py:11
  65.7 5.0 %collective-permute-start.23 = (f32[64,512]{1,0:T(8,128)S(1)}, f32[64,512]{1,0:T(8,128)S(1)}, u32[]{:S(2)}, u32[]{:S(2)}) collective-permute-start(f32[64,512]{1,0:T(8,128)S(1)} %get-tuple-element.22), channel_id=1, source_target_pairs={{0,16},{8,24},{16,0},{24,8},{1,17},{9,25},{17,1},{25,9},{2,18},{10... | collective-permute-start | bytes 393224 | tf_op jit(solution)/shard_map/ppermute | solution.py:11
  67.0 1.0 %copy-start.4 = (f32[128,512]{1,0:T(8,128)S(1)}, f32[128,512]{1,0:T(8,128)}, u32[]{:S(2)}) copy-start(f32[128,512]{1,0:T(8,128)} %param.11) | copy-start | bytes 786436
  70.1 1.0 %copy-start.3 = (f32[128,512]{1,0:T(8,128)S(1)}, f32[128,512]{1,0:T(8,128)}, u32[]{:S(2)}) copy-start(f32[128,512]{1,0:T(8,128)} %param.13) | copy-start | bytes 786436

commit v2 on v1

v2 whole, which is shorter than its diff:
```python
import functools

import jax
import jax.numpy as jnp
from jax import lax
from jax.experimental import pallas as pl
from jax.experimental.pallas import tpu as pltpu
from jax.sharding import PartitionSpec as P

step_size = 0.05
SMEM = pl.BlockSpec(memory_space=pltpu.SMEM)
VMEM = pl.BlockSpec(memory_space=pltpu.VMEM)
HBM = pl.BlockSpec(memory_space=pltpu.HBM)
ROWS = ((1,), (0,))
COLS = ((1,), (1,))
LEFT = ((0,), (0,))


def exchange(block, axis, size, step):
    return lax.ppermute(block, axis, [(i, i ^ step) for i in range(size)])


def call(body, outs, specs, args, flops=0, scratch=()):
    shapes = [jax.ShapeDtypeStruct(shape, jnp.float32) for shape in outs]
    moved = 4 * sum(int(a.size) for a in args) + 4 * sum(int(s.size) for s in shapes)
    return pl.pallas_call(
        body,
        out_shape=shapes,
        in_specs=specs,
        out_specs=[VMEM] * len(shapes),
        scratch_shapes=scratch,
        compiler_params=pltpu.CompilerParams(vmem_limit_bytes=40 * 1024 * 1024),
        cost_estimate=pl.CostEstimate(flops=flops, bytes_accessed=moved, transcendentals=0),
    )(*args)


def dot(left, right, dims):
    return lax.dot_general(left, right, (dims, ((), ())), preferred_element_type=jnp.float32)


def halves(rows):
    high = rows.astype(jnp.bfloat16)
    low = (rows - high.astype(jnp.float32)).astype(jnp.bfloat16)
    return high, low


def pick(index, size):
    spots = lax.broadcasted_iota(jnp.int32, (size, index.shape[1]), 0)
    return (spots == index).astype(jnp.float32)


def take(chosen, table):
    high, low = halves(table)
    chosen = chosen.astype(jnp.bfloat16)
    return dot(
        jnp.concatenate([chosen, chosen], axis=0), jnp.concatenate([high, low], axis=0), LEFT
    )


def put(chosen, rows):
    high, low = halves(rows)
    chosen = chosen.astype(jnp.bfloat16)
    return dot(chosen, high, ROWS) + dot(chosen, low, ROWS)


def quarters(rows):
    size = rows.shape[-1] // 4
    return [rows[:, i * size : (i + 1) * size] for i in range(4)]


def hamilton(left, right):
    la, lb, lc, ld = left
    ra, rb, rc, rd = right
    return [
        la * ra - lb * rb - lc * rc - ld * rd,
        la * rb + lb * ra + lc * rd - ld * rc,
        la * rc - lb * rd + lc * ra + ld * rb,
        la * rd + lb * rc - lc * rb + ld * ra,
    ]


def conjugate(parts):
    return [parts[0], -parts[1], -parts[2], -parts[3]]


def join(parts):
    return jnp.concatenate(parts, axis=-1)


def gather_kernel(send_ref, neg_ref, entity_ref, negs_ref, keep_ref, give_ref, rows, sends, picks, sems):
    copies = [
        pltpu.make_async_copy(source, target, sems.at[i])
        for i, (source, target) in enumerate(
            ((entity_ref, rows), (send_ref, sends), (neg_ref, picks))
        )
    ]
    for copy in copies:
        copy.start()
    for copy in copies:
        copy.wait()
    rel_here = lax.axis_index("rel")
    slots = send_ref.shape[2]

    def neg_row(i, carry):
        negs_ref[pl.ds(i, 1), :] = rows[pl.ds(picks[rel_here, i], 1), :]
        return carry

    lax.fori_loop(0, neg_ref.shape[1], neg_row, 0, unroll=8)

    def chip(s, carry):
        for core, out in ((0, keep_ref), (1, give_ref)):
            peer = (2 * s + core) ^ rel_here
            for t in range(slots):
                out[pl.ds(s * slots + t, 1), :] = rows[pl.ds(sends[0, peer, t], 1), :]
        return carry

    lax.fori_loop(0, send_ref.shape[1] // 2, chip, 0)


def unit_parts(rows):
    parts = quarters(rows)
    inverse = lax.rsqrt(sum(part * part for part in parts))
    return [part * inverse for part in parts], inverse


def rotation_kernel(rel_index_ref, relation_ref, rot_ref):
    unit, _ = unit_parts(relation_ref[...])
    chosen = pick(rel_index_ref[...].reshape(1, -1), relation_ref.shape[0])
    rot_ref[...] = take(chosen, join(unit))


def relative(index_ref, rel_here, slots):
    index = index_ref[...].reshape(1, -1)
    return ((index // slots) ^ rel_here) * slots + index % slots


def both_picks(head_ref, tail_ref, slots, size):
    rel_here = lax.axis_index("rel")
    heads = pick(relative(head_ref, rel_here, slots), size)
    tails = pick(relative(tail_ref, rel_here, slots), size)
    return jnp.concatenate([heads, tails], axis=1)


def scores_kernel(
    slots, n_chip, head_ref, tail_ref, rot_ref, *refs
):
    parcels, blocks = refs[:n_chip], refs[n_chip : 3 * n_chip]
    mine_ref, theirs_ref, query_ref, head_out, tail_out, pull_ref, push_ref = refs[3 * n_chip :]
    touched = jnp.concatenate([ref[...] for ref in parcels], axis=0)
    negs = jnp.concatenate([ref[...] for ref in blocks], axis=0)
    trips = head_ref.shape[0]
    rows = take(both_picks(head_ref, tail_ref, slots, touched.shape[0]), touched)
    head, tail = rows[:trips], rows[trips:]
    query = join(hamilton(quarters(head), quarters(rot_ref[...])))
    positive = jnp.sum(query * tail, axis=-1, keepdims=True)
    pull_ref[...] = jnp.broadcast_to(-jax.nn.sigmoid(-positive), pull_ref.shape)
    query_ref[...], head_out[...], tail_out[...] = query, head, tail
    q_high, q_low = halves(query)
    n_high, n_low = halves(negs)
    scores = dot(q_high, n_high, COLS) + dot(q_high, n_low, COLS) + dot(q_low, n_high, COLS)
    push = jax.nn.sigmoid(scores) * (1.0 / negs.shape[0])
    push_ref[...] = push
    p_high, p_low = halves(push)
    grad = dot(p_high, q_high, LEFT) + dot(p_low, q_high, LEFT) + dot(p_high, q_low, LEFT)
    middle = mine_ref.shape[0]
    mine_ref[...] = grad[:middle]
    theirs_ref[...] = grad[middle:]


def grad_kernel(slots, n_chip, head_ref, rel_index_ref, tail_ref, relation_ref, rot_ref, *refs):
    blocks = refs[: 2 * n_chip]
    query_ref, head_rows, tail_rows, pull_ref, push_ref = refs[2 * n_chip : 2 * n_chip + 5]
    low_ref, high_ref, touched_ref = refs[2 * n_chip + 5 :]
    negs = jnp.concatenate([ref[...] for ref in blocks], axis=0)
    p_high, p_low = halves(push_ref[...])
    n_high, n_low = halves(negs)
    pulled = dot(p_high, n_high, ROWS) + dot(p_low, n_high, ROWS) + dot(p_high, n_low, ROWS)
    pull = pull_ref[:, :1]
    grad_query = quarters(pulled + pull * tail_rows[...])
    grad_head = join(hamilton(grad_query, conjugate(quarters(rot_ref[...]))))
    grad_rot = join(hamilton(conjugate(quarters(head_rows[...])), grad_query))
    grad_tail = pull * query_ref[...]
    chosen = both_picks(head_ref, tail_ref, slots, touched_ref.shape[0])
    touched_ref[...] = put(chosen, jnp.concatenate([grad_head, grad_tail], axis=0))
    unit, inverse = unit_parts(relation_ref[...])
    chosen = pick(rel_index_ref[...].reshape(1, -1), relation_ref.shape[0])
    grad_unit = quarters(put(chosen, grad_rot))
    along = sum(u * g for u, g in zip(unit, grad_unit))
    rel_grad = join([inverse * (g - u * along) for u, g in zip(unit, grad_unit)])
    middle = low_ref.shape[0]
    low_ref[...] = rel_grad[:middle]
    high_ref[...] = rel_grad[middle:]


def select_kernel(part_ref, after_ref, *refs):
    *blocks, out_ref = refs
    source = lax.axis_index("dom") ^ part_ref[0]
    picked = blocks[0][...]
    for s, ref in enumerate(blocks):
        picked = jnp.where(source == s, ref[...], picked)
    out_ref[...] = picked


def parcel_kernel(slots, own_ref, keep_ref, came_ref, copy_ref, *parcels):
    copy_ref[...] = own_ref[...]
    for s, ref in enumerate(parcels):
        rows = pl.ds(s * slots, slots)
        ref[:slots] = keep_ref[rows]
        ref[slots:] = came_ref[rows]


def pack_kernel(slots, n_neg, mine, theirs, touched, low, high, low_ref, high_ref, *back):
    low_ref[...] = low[...]
    high_ref[...] = high[...]
    for s, ref in enumerate(back):
        block = pl.ds(s * n_neg, n_neg)
        ref[: 2 * slots] = touched[2 * s * slots : 2 * (s + 1) * slots]
        ref[2 * slots :] = mine[block] + theirs[block]


def unpack_kernel(slots, n_chip, *refs):
    back, (neg_ref, stay_ref, cross_ref) = refs[:n_chip], refs[-3:]
    neg_ref[...] = sum(ref[2 * slots :] for ref in back)
    for s, ref in enumerate(back):
        rows = pl.ds(s * slots, slots)
        stay_ref[rows] = ref[:slots]
        cross_ref[rows] = ref[slots : 2 * slots]


def adagrad(values, history, gradient):
    history_new = history + gradient * gradient
    return values - step_size * gradient * lax.rsqrt(history_new), history_new


def entity_kernel(part_ref, send_ref, neg_ref, entity_ref, acc_ref, stay_ref, cross_ref, *refs):
    negs, (out_ref, acc_out) = refs[:-2], refs[-2:]
    rel_here = lax.axis_index("rel")
    owner = (lax.axis_index("dom") == part_ref[0]).astype(jnp.float32)
    size = entity_ref.shape[0]
    slots = send_ref.shape[2]
    neg = sum(ref[...] for ref in negs) * owner
    chosen = [pick(neg_ref[pl.ds(rel_here, 1), :], size)]
    rows = [neg]
    for k, ref in ((0, stay_ref), (1, cross_ref)):
        for s in range(send_ref.shape[1] // 2):
            peer = (2 * s + k) ^ rel_here
            chosen.append(pick(send_ref[0, pl.ds(peer, 1), :], size))
            rows.append(ref[s * slots : (s + 1) * slots])
    grad = put(jnp.concatenate(chosen, axis=1), jnp.concatenate(rows, axis=0))
    out_ref[...], acc_out[...] = adagrad(entity_ref[...], acc_ref[...], grad)


def relation_kernel(low_a, low_b, high_a, high_b, relation_ref, acc_ref, out_ref, acc_out):
    grad = jnp.concatenate([low_a[...] + low_b[...], high_a[...] + high_b[...]], axis=0)
    out_ref[...], acc_out[...] = adagrad(relation_ref[...], acc_ref[...], grad)


def shards(
    entity,
    entity_acc,
    relation,
    relation_acc,
    send_rows,
    trip_head,
    trip_rel,
    trip_tail,
    neg_part,
    neg_rows,
    *,
    n_dom,
    n_rel,
):
    ents, width = entity.shape
    rels = relation.shape[0]
    trips = trip_head.shape[0]
    slots = send_rows.shape[2]
    n_neg = neg_rows.shape[1]
    n_chip = n_rel // 2

    own_negs, keep, give = call(
        gather_kernel,
        [(n_neg, width), (n_chip * slots, width), (n_chip * slots, width)],
        [HBM, HBM, HBM],
        (send_rows, neg_rows, entity),
        scratch=[
            pltpu.VMEM(entity.shape, jnp.float32),
            pltpu.SMEM(send_rows.shape, jnp.int32),
            pltpu.SMEM(neg_rows.shape, jnp.int32),
            pltpu.SemaphoreType.DMA((3,)),
        ],
    )
    came = exchange(give, "rel", n_rel, 1)
    near = exchange(own_negs, "dom", n_dom, 1)
    copied, *parcels = call(
        functools.partial(parcel_kernel, slots),
        [own_negs.shape] + [(2 * slots, width)] * n_chip,
        [VMEM] * 3,
        (own_negs, keep, came),
    )
    arrived = [parcels[0]] + [exchange(parcels[s], "rel", n_rel, 2 * s) for s in range(1, n_chip)]
    spread = [copied, near] + [exchange(copied, "dom", n_dom, s) for s in range(2, n_dom)]
    (rot,) = call(rotation_kernel, [(trips, width)], [VMEM] * 2, (trip_rel, relation))
    (picked,) = call(
        select_kernel,
        [own_negs.shape],
        [SMEM, VMEM] + [VMEM] * n_dom,
        (neg_part, rot, *spread),
    )
    negs = [picked] + [exchange(picked, "rel", n_rel, 2 * s) for s in range(1, n_chip)]
    others = [exchange(block, "rel", n_rel, 1) for block in negs]

    mine, theirs, *saved = call(
        functools.partial(scores_kernel, slots, n_chip),
        [(n_chip * n_neg, width)] * 2 + [(trips, width)] * 3 + [(trips, 128), (trips, n_rel * n_neg)],
        [VMEM] * (3 + 3 * n_chip),
        (trip_head, trip_tail, rot, *arrived, *negs, *others),
    )
    theirs = exchange(theirs, "rel", n_rel, 1)
    low, high, touched = call(
        functools.partial(grad_kernel, slots, n_chip),
        [(rels // 2, width)] * 2 + [(n_rel * slots, width)],
        [VMEM] * (10 + 2 * n_chip),
        (trip_head, trip_rel, trip_tail, relation, rot, *negs, *others, *saved),
    )

    low, high, *back = call(
        functools.partial(pack_kernel, slots, n_neg),
        [low.shape, high.shape] + [(2 * slots + n_neg, width)] * n_chip,
        [VMEM] * 5,
        (mine, theirs, touched, low, high),
    )
    back = [back[0]] + [exchange(back[s], "rel", n_rel, 2 * s) for s in range(1, n_chip)]
    bits = [1 << b for b in range((n_dom - 1).bit_length())]
    sums = [[low], [high]]
    first = []
    for up, down in zip(bits, bits[::-1]):
        sums = [[sum(pair)] for pair in sums]
        first = first or ([sums[0][0], sums[1][0]] if len(bits) > 1 and up != bits[0] else [])
        sums[0].append(exchange(sums[0][0], "dom", n_dom, up))
        sums[1].append(exchange(sums[1][0], "dom", n_dom, down))
    neg_share, stay, cross = call(
        functools.partial(unpack_kernel, slots, n_chip),
        [(n_neg, width)] + [(n_chip * slots, width)] * 2,
        [VMEM] * (n_chip + len(first)),
        (*back, *first),
    )
    neg_shares = [neg_share] + [exchange(neg_share, "dom", n_dom, s) for s in range(1, n_dom)]
    cross = exchange(cross, "rel", n_rel, 1)

    new_relation, new_relation_acc = call(
        relation_kernel,
        [relation.shape] * 2,
        [VMEM] * 6,
        (*sums[0], *sums[1], relation, relation_acc),
    )

    new_entity, new_entity_acc = call(
        entity_kernel,
        [entity.shape] * 2,
        [SMEM] + [VMEM] * (6 + n_dom),
        (neg_part, send_rows, neg_rows, entity, entity_acc, stay, cross, *neg_shares),
    )
    return (new_entity, new_entity_acc, new_relation, new_relation_acc)


def solution(mesh):
    def step(*arrays):
        return shards(*arrays, n_dom=mesh.shape["dom"], n_rel=mesh.shape["rel"])

    both = ("dom", "rel")
    in_specs = (
        P(both, None),
        P(both, None),
        P("rel", None),
        P("rel", None),
        P(both, None, None),
        P(both),
        P(both),
        P(both),
        P(),
        P(),
    )
    out_specs = (P(both, None), P(both, None), P("rel", None), P("rel", None))
    return jax.shard_map(step, mesh=mesh, in_specs=in_specs, out_specs=out_specs, check_vma=False)
```

time: 72.3 us -> 55.1 us (0.76)
  matrix products: 9.65 us -> 0 us
  waiting for transfers between devices: 21.6 us -> 13.9 us
  Pallas kernels: 0 us -> 6.19 us
  local copies, waits for them, and re-layouts: 6.34 us -> 2.4 us
  other arithmetic: 2.59 us -> 0.04 us
  starting transfers between devices: 30 us -> 30.9 us
    dot_general x11 -> x0, matrix products: 9.65 us -> none  [dot(): lax.dot_general(left, right, (dims, ((), ())), precision=HIGHEST, preferr...]
    ppermute x26, waiting for transfers between devices: 21.6 us -> 13.9 us  [exchange(): return lax.ppermute(block, axis, [(i, i ^ step) for i in range(size)])]
    pallas_call x0 -> x10, Pallas kernels: none -> 6.19 us  [call(): pl.pallas_call(body, out_shape=shapes, in_specs=specs, out_specs=[VMEM] *...]
    gather x3 -> x0, local copies, waits for them, and re-layouts: 2.96 us -> none  [the longest x1 1.64 us: shards(): own_negs = entity[own_rows]]
    sub x7 -> x0, other arithmetic: 1.3 us -> none  [the longest x1 0.85 us: adagrad(): return (values - step_size * gradient / jnp.sqrt(history_new), history_new)]
    ppermute x26, starting transfers between devices: 30 us -> 30.9 us  [exchange(): return lax.ppermute(block, axis, [(i, i ^ step) for i in range(size)])]
    eq x2 -> x0, local copies, waits for them, and re-layouts: 0.78 us -> none  [one_hot(): return (index[:, None] == jnp.arange(size)[None, :]).astype(jnp.float32)]
    unnamed x16 -> x24, local copies, waits for them, and re-layouts: 2.4 us -> 2.4 us
  transfers between devices with their start and end apart: 26 -> 26, of which waited for: 13 -> 7; matrix products, arithmetic and copies ran while one was open for 11% -> 0% of each run, Pallas kernels for 0% -> 4%
where the time goes in v2:
time: 55.1 us; the launch traced here: 54.8 us
  starting transfers between devices  30.9 us (56%)
  waiting for transfers between devices  13.9 us (25%)
  Pallas kernels  6.19 us (11%)
  local copies, waits for them, and re-layouts  2.4 us (4%)
  between operations  1.48 us (3%)
    ppermute x26, starting transfers between devices, exchange(): return lax.ppermute(block, axis, [(i, i ^ step) for i in range(size)])  30.9 us
    ppermute x26, waiting for transfers between devices, exchange(): return lax.ppermute(block, axis, [(i, i ^ step) for i in range(size)])  13.9 us
    pallas_call x10, Pallas kernels, call(): pl.pallas_call(body, out_shape=shapes, in_specs=specs, out_specs=[VMEM] *...  6.19 us
    unnamed x24, local copies, waits for them, and re-layouts  2.4 us
  transfers between devices with their start and end apart: 26, of which 7 were waited for; matrix products, arithmetic and copies ran while one was open for 0% of the time, Pallas kernels for 4%

profile of v2, /device:TPU:0, one launch (start us, length us, event | category | flops | bytes accessed | tf_op | source)
XLA Modules:
  0.0 54.8 jit_solution(6490429563556522321)
XLA Ops:
  0.6 0.0 copy-start.1
  0.7 1.0 %copy-done.1 = f32[128,512]{1,0:T(8,128)S(1)} copy-done((f32[128,512]{1,0:T(8,128)S(1)}, f32[128,512]{1,0:T(8,128)}, u32[]{:S(2)}) %copy-start.1) | copy-done | bytes 262168
  1.6 0.7 %copy-done.5 = s32[1,8,16]{2,1,0:T(8,128)S(1)} copy-done((s32[1,8,16]{2,1,0:T(8,128)S(1)}, s32[1,8,16]{2,1,0:T(8,128)}, u32[]{:S(2)}) %copy-start.5) | copy-done | bytes 536
  2.3 0.7 %copy-done.7 = s32[8,32]{1,0:T(8,128)S(1)} copy-done((s32[8,32]{1,0:T(8,128)S(1)}, s32[8,32]{1,0:T(8,128)}, u32[]{:S(2)}) %copy-start.7) | copy-done | bytes 1048
  3.0 1.2 %shard_map.130 = (f32[32,512]{1,0:T(8,128)S(1)}, f32[64,512]{1,0:T(8,128)S(1)}, f32[64,512]{1,0:T(8,128)S(1)}) custom-call(s32[1,8,16]{2,1,0:T(8,128)S(1)} %copy-done.5, s32[8,32]{1,0:T(8,128)S(1)} %copy-done.7, f32[128,512]{1,0:T(8,128)S(1)} %copy-done.1), custom_call_target="tpu_custom_call" | custom-call | bytes 591360 | tf_op jit(solution)/shard_map/pallas_call | solution.py:26
  4.3 0.5 collective-permute-start
  4.8 2.6 %collective-permute-start.4 = (f32[32,512]{1,0:T(8,128)S(1)}, f32[32,512]{1,0:T(8,128)S(1)}, u32[]{:S(2)}, u32[]{:S(2)}) collective-permute-start(f32[32,512]{1,0:T(8,128)S(1)} %get-tuple-element.35.own_ref), channel_id=1, source_target_pairs={{0,8},{8,0},{16,24},{24,16},{1,9},{9,1},{17,25},{25,17},{2,10},{10... | collective-permute-start | bytes 196616 | tf_op jit(solution)/shard_map/ppermute | solution.py:20
  7.4 0.0 copy-start.11
  7.4 1.6 %collective-permute-start.5 = (f32[32,512]{1,0:T(8,128)S(1)}, f32[32,512]{1,0:T(8,128)S(1)}, u32[]{:S(2)}, u32[]{:S(2)}) collective-permute-start(f32[32,512]{1,0:T(8,128)S(1)} %get-tuple-element.42.refs_0_), channel_id=1, source_target_pairs={{0,16},{8,24},{16,0},{24,8},{1,17},{9,25},{17,1},{25,9},{2,18},{10... | collective-permute-start | bytes 196616 | tf_op jit(solution)/shard_map/ppermute | solution.py:20
  9.0 1.2 %collective-permute-start.6 = (f32[32,512]{1,0:T(8,128)S(1)}, f32[32,512]{1,0:T(8,128)S(1)}, u32[]{:S(2)}, u32[]{:S(2)}) collective-permute-start(f32[32,512]{1,0:T(8,128)S(1)} %get-tuple-element.42.refs_0_), channel_id=1, source_target_pairs={{0,24},{8,16},{16,8},{24,0},{1,25},{9,17},{17,9},{25,1},{2,26},{10... | collective-permute-start | bytes 196616 | tf_op jit(solution)/shard_map/ppermute | solution.py:20
  10.8 0.3 shard_map.129.after_ref.rot_ref
  11.1 1.6 %collective-permute-start.1 = (f32[32,512]{1,0:T(8,128)S(1)}, f32[32,512]{1,0:T(8,128)S(1)}, u32[]{:S(2)}, u32[]{:S(2)}) collective-permute-start(f32[32,512]{1,0:T(8,128)S(1)} %get-tuple-element.39), channel_id=1, source_target_pairs={{0,2},{1,3},{2,0},{3,1},{4,6},{5,7},{6,4},{7,5},{8,10},{9,11},{10,... | collective-permute-start | bytes 196616 | tf_op jit(solution)/shard_map/ppermute | solution.py:20
  12.8 2.6 %collective-permute-start.2 = (f32[32,512]{1,0:T(8,128)S(1)}, f32[32,512]{1,0:T(8,128)S(1)}, u32[]{:S(2)}, u32[]{:S(2)}) collective-permute-start(f32[32,512]{1,0:T(8,128)S(1)} %get-tuple-element.40), channel_id=1, source_target_pairs={{0,4},{1,5},{2,6},{3,7},{4,0},{5,1},{6,2},{7,3},{8,12},{9,13},{10,... | collective-permute-start | bytes 196616 | tf_op jit(solution)/shard_map/ppermute | solution.py:20
  15.3 0.0 collective-permute-done.5.refs_2_
  15.4 0.0 collective-permute-done.6.refs_3_
  15.4 0.5 collective-permute-start.7
  15.9 2.5 %collective-permute-start.8 = (f32[32,512]{1,0:T(8,128)S(1)}, f32[32,512]{1,0:T(8,128)S(1)}, u32[]{:S(2)}, u32[]{:S(2)}) collective-permute-start(f32[32,512]{1,0:T(8,128)S(1)} %shard_map.132.refs_4_.refs_0_), channel_id=1, source_target_pairs={{0,4},{1,5},{2,6},{3,7},{4,0},{5,1},{6,2},{7,3},{8,12},{9,13},{10,... | collective-permute-start | bytes 196616 | tf_op jit(solution)/shard_map/ppermute | solution.py:20
  18.4 1.5 %collective-permute-start.9 = (f32[32,512]{1,0:T(8,128)S(1)}, f32[32,512]{1,0:T(8,128)S(1)}, u32[]{:S(2)}, u32[]{:S(2)}) collective-permute-start(f32[32,512]{1,0:T(8,128)S(1)} %shard_map.132.refs_4_.refs_0_), channel_id=1, source_target_pairs={{0,6},{1,7},{2,4},{3,5},{4,2},{5,3},{6,0},{7,1},{8,14},{9,15},{10,... | collective-permute-start | bytes 196616 | tf_op jit(solution)/shard_map/ppermute | solution.py:20
  19.9 2.4 %collective-permute-start.3 = (f32[32,512]{1,0:T(8,128)S(1)}, f32[32,512]{1,0:T(8,128)S(1)}, u32[]{:S(2)}, u32[]{:S(2)}) collective-permute-start(f32[32,512]{1,0:T(8,128)S(1)} %get-tuple-element.41), channel_id=1, source_target_pairs={{0,6},{1,7},{2,4},{3,5},{4,2},{5,3},{6,0},{7,1},{8,14},{9,15},{10,... | collective-permute-start | bytes 196616 | tf_op jit(solution)/shard_map/ppermute | solution.py:20
  22.2 0.5 collective-permute-start.11
  22.7 1.9 %collective-permute-done.8.refs_6_.refs_2_ = f32[32,512]{1,0:T(8,128)S(1)} collective-permute-done((f32[32,512]{1,0:T(8,128)S(1)}, f32[32,512]{1,0:T(8,128)S(1)}, u32[]{:S(2)}, u32[]{:S(2)}) %collective-permute-start.8) | collective-permute-done | bytes 65568 | tf_op jit(solution)/shard_map/ppermute | solution.py:20
  24.6 0.5 collective-permute-start.13
  25.2 0.9 %collective-permute-done.3.refs_3_ = f32[32,512]{1,0:T(8,128)S(1)} collective-permute-done((f32[32,512]{1,0:T(8,128)S(1)}, f32[32,512]{1,0:T(8,128)S(1)}, u32[]{:S(2)}, u32[]{:S(2)}) %collective-permute-start.3) | collective-permute-done | bytes 65568 | tf_op jit(solution)/shard_map/ppermute | solution.py:20
  26.0 0.0 collective-permute-done.13.refs_11_.refs_7_
  26.1 1.5 %shard_map.133 = (f32[128,512]{1,0:T(8,128)S(1)}, f32[128,512]{1,0:T(8,128)S(1)}, f32[256,512]{1,0:T(8,128)S(1)}, f32[256,512]{1,0:T(8,128)S(1)}, f32[256,512]{1...) custom-call(s32[256]{0:T(256)S(1)} %copy-done.9, s32[256]{0:T(256)S(1)} %copy-done.10, ...), custom_call_target="tpu_custom_call" | custom-call | bytes 3803136 | tf_op jit(solution)/shard_map/pallas_call | solution.py:26
  27.5 0.4 collective-permute-start.14
  28.0 1.1 %shard_map.134 = (f32[64,512]{1,0:T(8,128)S(1)}, f32[64,512]{1,0:T(8,128)S(1)}, f32[128,512]{1,0:T(8,128)S(1)}) custom-call(s32[256]{0:T(256)S(1)} %copy-done.9, s32[256]{0:T(256)S(1)} %copy-done.11, s32[256]{0:T(256)S(1)} %copy-done.10, f32[128,512]{1,0:T(8,128)S(1)} %copy-done, f32[256,512]{1,0:T(8,128)S(1)} %shard_map.129.after_ref.rot_ref, ...), custom_call_target="tpu_custom_call" | custom-call | bytes 3804160 | tf_op jit(solution)/shard_map/pallas_call | solution.py:26
  29.1 0.1 collective-permute-done.14.theirs
  29.1 0.1 shard_map.135
  29.2 1.1 %collective-permute-start.18 = (f32[64,512]{1,0:T(8,128)S(1)}, f32[64,512]{1,0:T(8,128)S(1)}, u32[]{:S(2)}, u32[]{:S(2)}) collective-permute-start(f32[64,512]{1,0:T(8,128)S(1)} %get-tuple-element.57), channel_id=1, source_target_pairs={{0,8},{8,0},{16,24},{24,16},{1,9},{9,1},{17,25},{25,17},{2,10},{10... | collective-permute-start | bytes 393224 | tf_op jit(solution)/shard_map/ppermute | solution.py:20
  30.3 1.3 %collective-permute-start.19 = (f32[64,512]{1,0:T(8,128)S(1)}, f32[64,512]{1,0:T(8,128)S(1)}, u32[]{:S(2)}, u32[]{:S(2)}) collective-permute-start(f32[64,512]{1,0:T(8,128)S(1)} %get-tuple-element.58), channel_id=1, source_target_pairs={{0,16},{8,24},{16,0},{24,8},{1,17},{9,25},{17,1},{25,9},{2,18},{10... | collective-permute-start | bytes 393224 | tf_op jit(solution)/shard_map/ppermute | solution.py:20
  31.6 2.2 %collective-permute-start.15 = (f32[64,512]{1,0:T(8,128)S(1)}, f32[64,512]{1,0:T(8,128)S(1)}, u32[]{:S(2)}, u32[]{:S(2)}) collective-permute-start(f32[64,512]{1,0:T(8,128)S(1)} %get-tuple-element.54), channel_id=1, source_target_pairs={{0,2},{1,3},{2,0},{3,1},{4,6},{5,7},{6,4},{7,5},{8,10},{9,11},{10,... | collective-permute-start | bytes 393224 | tf_op jit(solution)/shard_map/ppermute | solution.py:20
  33.8 0.9 %collective-permute-start.16 = (f32[64,512]{1,0:T(8,128)S(1)}, f32[64,512]{1,0:T(8,128)S(1)}, u32[]{:S(2)}, u32[]{:S(2)}) collective-permute-start(f32[64,512]{1,0:T(8,128)S(1)} %get-tuple-element.55), channel_id=1, source_target_pairs={{0,4},{1,5},{2,6},{3,7},{4,0},{5,1},{6,2},{7,3},{8,12},{9,13},{10,... | collective-permute-start | bytes 393224 | tf_op jit(solution)/shard_map/ppermute | solution.py:20
  34.7 1.5 %collective-permute-start.17 = (f32[64,512]{1,0:T(8,128)S(1)}, f32[64,512]{1,0:T(8,128)S(1)}, u32[]{:S(2)}, u32[]{:S(2)}) collective-permute-start(f32[64,512]{1,0:T(8,128)S(1)} %get-tuple-element.56), channel_id=1, source_target_pairs={{0,6},{1,7},{2,4},{3,5},{4,2},{5,3},{6,0},{7,1},{8,14},{9,15},{10,... | collective-permute-start | bytes 393224 | tf_op jit(solution)/shard_map/ppermute | solution.py:20
  36.2 0.8 %collective-permute-start.24 = (f32[64,512]{1,0:T(8,128)S(1)}, f32[64,512]{1,0:T(8,128)S(1)}, u32[]{:S(2)}, u32[]{:S(2)}) collective-permute-start(f32[64,512]{1,0:T(8,128)S(1)} %add.6.refs_4_.low_a), channel_id=1, source_target_pairs={{0,16},{8,24},{16,0},{24,8},{1,17},{9,25},{17,1},{25,9},{2,18},{10... | collective-permute-start | bytes 393224 | tf_op jit(solution)/shard_map/ppermute | solution.py:20
  37.1 1.1 %collective-permute-start.25 = (f32[64,512]{1,0:T(8,128)S(1)}, f32[64,512]{1,0:T(8,128)S(1)}, u32[]{:S(2)}, u32[]{:S(2)}) collective-permute-start(f32[64,512]{1,0:T(8,128)S(1)} %add.7.refs_5_.high_a), channel_id=1, source_target_pairs={{0,8},{8,0},{16,24},{24,16},{1,9},{9,1},{17,25},{25,17},{2,10},{10... | collective-permute-start | bytes 393224 | tf_op jit(solution)/shard_map/ppermute | solution.py:20
  38.1 0.3 collective-permute-done.15.refs_1_
  38.5 8.0 %collective-permute-done.16.refs_2_ = f32[64,512]{1,0:T(8,128)S(1)} collective-permute-done((f32[64,512]{1,0:T(8,128)S(1)}, f32[64,512]{1,0:T(8,128)S(1)}, u32[]{:S(2)}, u32[]{:S(2)}) %collective-permute-start.16) | collective-permute-done | bytes 131104 | tf_op jit(solution)/shard_map/ppermute | solution.py:20
  46.5 0.1 collective-permute-start.20
  46.6 0.0 copy-start.2
  46.6 0.0 copy-start.4
  46.6 1.4 %collective-permute-start.21 = (f32[32,512]{1,0:T(8,128)S(1)}, f32[32,512]{1,0:T(8,128)S(1)}, u32[]{:S(2)}, u32[]{:S(2)}) collective-permute-start(f32[32,512]{1,0:T(8,128)S(1)} %get-tuple-element.61.refs_0_), channel_id=1, source_target_pairs={{0,8},{8,0},{16,24},{24,16},{1,9},{9,1},{17,25},{25,17},{2,10},{10... | collective-permute-start | bytes 196616 | tf_op jit(solution)/shard_map/ppermute | solution.py:20
  48.0 0.3 collective-permute-start.22
  48.3 1.9 %collective-permute-start.23 = (f32[32,512]{1,0:T(8,128)S(1)}, f32[32,512]{1,0:T(8,128)S(1)}, u32[]{:S(2)}, u32[]{:S(2)}) collective-permute-start(f32[32,512]{1,0:T(8,128)S(1)} %get-tuple-element.61.refs_0_), channel_id=1, source_target_pairs={{0,24},{8,16},{16,8},{24,0},{1,25},{9,17},{17,9},{25,1},{2,26},{10... | collective-permute-start | bytes 196616 | tf_op jit(solution)/shard_map/ppermute | solution.py:20
  50.2 0.9 %shard_map.138 = (f32[128,512]{1,0:T(8,128)}, f32[128,512]{1,0:T(8,128)}) custom-call(f32[64,512]{1,0:T(8,128)S(1)} %add.6.refs_4_.low_a, f32[64,512]{1,0:T(8,128)S(1)} %collective-permute-done.24.low_b, f32[64,512]{1,0:T(8,128)S(1)} %add.7.refs_5_.high_a, f32[64,512]{1,0:T(8,128)S(1)} %collective-permute-done.25.high_b, f32[128,512]{1,0:T(8,128)S(1)} %copy-done, ...), custom_call_target="tpu_custom_call" | custom-call | bytes 1572864 | tf_op jit(solution)/shard_map/pallas_call | solution.py:26
  51.1 0.1 collective-permute-done.21.refs_1_
  51.1 2.5 %collective-permute-done.22.refs_2_ = f32[32,512]{1,0:T(8,128)S(1)} collective-permute-done((f32[32,512]{1,0:T(8,128)S(1)}, f32[32,512]{1,0:T(8,128)S(1)}, u32[]{:S(2)}, u32[]{:S(2)}) %collective-permute-start.22) | collective-permute-done | bytes 65568 | tf_op jit(solution)/shard_map/ppermute | solution.py:20
  53.7 1.1 %shard_map.137 = (f32[128,512]{1,0:T(8,128)}, f32[128,512]{1,0:T(8,128)}) custom-call(s32[1]{0:T(128)S(6)} %copy.14.part_ref, s32[1,8,16]{2,1,0:T(8,128)S(1)} %copy-done.6, s32[8,32]{1,0:T(8,128)S(1)} %copy-done.8, f32[128,512]{1,0:T(8,128)S(1)} %copy-done.2, f32[128,512]{1,0:T(8,128)S(1)} %copy-done.4, f32[64,512]{1,0:T(8,128)S(1)} %get-tuple-element.59.stay_ref, ...), custom_call_target="tpu_custom_call" | custom-call | bytes 1574404 | tf_op jit(solution)/shard_map/pallas_call | solution.py:26
  (40 shorter events, 0.2 us)
Async XLA Ops:
  0.6 10.2 %copy-start = (f32[128,512]{1,0:T(8,128)S(1)}, f32[128,512]{1,0:T(8,128)}, u32[]{:S(2)}) copy-start(f32[128,512]{1,0:T(8,128)} %relation_ref.5) | copy-start | bytes 786436
  0.6 1.0 %copy-start.1 = (f32[128,512]{1,0:T(8,128)S(1)}, f32[128,512]{1,0:T(8,128)}, u32[]{:S(2)}) copy-start(f32[128,512]{1,0:T(8,128)} %entity_ref.3) | copy-start | bytes 786436
  1.6 0.7 %copy-start.5 = (s32[1,8,16]{2,1,0:T(8,128)S(1)}, s32[1,8,16]{2,1,0:T(8,128)}, u32[]{:S(2)}) copy-start(s32[1,8,16]{2,1,0:T(8,128)} %send_ref.3) | copy-start | bytes 1540
  2.3 0.7 %copy-start.7 = (s32[8,32]{1,0:T(8,128)S(1)}, s32[8,32]{1,0:T(8,128)}, u32[]{:S(2)}) copy-start(s32[8,32]{1,0:T(8,128)} %neg_ref.3) | copy-start | bytes 3076
  4.3 3.1 %collective-permute-start = (f32[64,512]{1,0:T(8,128)S(1)}, f32[64,512]{1,0:T(8,128)S(1)}, u32[]{:S(2)}, u32[]{:S(2)}) collective-permute-start(f32[64,512]{1,0:T(8,128)S(1)} %get-tuple-element.37), channel_id=1, source_target_pairs={{0,1},{1,0},{2,3},{3,2},{4,5},{5,4},{6,7},{7,6},{8,9},{9,8},{10,11... | collective-permute-start | bytes 393224 | tf_op jit(solution)/shard_map/ppermute | solution.py:20
  4.8 10.6 %collective-permute-start.4 = (f32[32,512]{1,0:T(8,128)S(1)}, f32[32,512]{1,0:T(8,128)S(1)}, u32[]{:S(2)}, u32[]{:S(2)}) collective-permute-start(f32[32,512]{1,0:T(8,128)S(1)} %get-tuple-element.35.own_ref), channel_id=1, source_target_pairs={{0,8},{8,0},{16,24},{24,16},{1,9},{9,1},{17,25},{25,17},{2,10},{10... | collective-permute-start | bytes 196616 | tf_op jit(solution)/shard_map/ppermute | solution.py:20
  7.4 3.5 %copy-start.11 = (s32[256]{0:T(256)S(1)}, s32[256]{0:T(256)}, u32[]{:S(2)}) copy-start(s32[256]{0:T(256)} %rel_index_ref.3) | copy-start | bytes 3076
  7.4 8.0 %collective-permute-start.5 = (f32[32,512]{1,0:T(8,128)S(1)}, f32[32,512]{1,0:T(8,128)S(1)}, u32[]{:S(2)}, u32[]{:S(2)}) collective-permute-start(f32[32,512]{1,0:T(8,128)S(1)} %get-tuple-element.42.refs_0_), channel_id=1, source_target_pairs={{0,16},{8,24},{16,0},{24,8},{1,17},{9,25},{17,1},{25,9},{2,18},{10... | collective-permute-start | bytes 196616 | tf_op jit(solution)/shard_map/ppermute | solution.py:20
  9.0 6.4 %collective-permute-start.6 = (f32[32,512]{1,0:T(8,128)S(1)}, f32[32,512]{1,0:T(8,128)S(1)}, u32[]{:S(2)}, u32[]{:S(2)}) collective-permute-start(f32[32,512]{1,0:T(8,128)S(1)} %get-tuple-element.42.refs_0_), channel_id=1, source_target_pairs={{0,24},{8,16},{16,8},{24,0},{1,25},{9,17},{17,9},{25,1},{2,26},{10... | collective-permute-start | bytes 196616 | tf_op jit(solution)/shard_map/ppermute | solution.py:20
  11.1 8.7 %collective-permute-start.1 = (f32[32,512]{1,0:T(8,128)S(1)}, f32[32,512]{1,0:T(8,128)S(1)}, u32[]{:S(2)}, u32[]{:S(2)}) collective-permute-start(f32[32,512]{1,0:T(8,128)S(1)} %get-tuple-element.39), channel_id=1, source_target_pairs={{0,2},{1,3},{2,0},{3,1},{4,6},{5,7},{6,4},{7,5},{8,10},{9,11},{10,... | collective-permute-start | bytes 196616 | tf_op jit(solution)/shard_map/ppermute | solution.py:20
  12.8 9.5 %collective-permute-start.2 = (f32[32,512]{1,0:T(8,128)S(1)}, f32[32,512]{1,0:T(8,128)S(1)}, u32[]{:S(2)}, u32[]{:S(2)}) collective-permute-start(f32[32,512]{1,0:T(8,128)S(1)} %get-tuple-element.40), channel_id=1, source_target_pairs={{0,4},{1,5},{2,6},{3,7},{4,0},{5,1},{6,2},{7,3},{8,12},{9,13},{10,... | collective-permute-start | bytes 196616 | tf_op jit(solution)/shard_map/ppermute | solution.py:20
  15.4 6.8 %collective-permute-start.7 = (f32[32,512]{1,0:T(8,128)S(1)}, f32[32,512]{1,0:T(8,128)S(1)}, u32[]{:S(2)}, u32[]{:S(2)}) collective-permute-start(f32[32,512]{1,0:T(8,128)S(1)} %shard_map.132.refs_4_.refs_0_), channel_id=1, source_target_pairs={{0,2},{1,3},{2,0},{3,1},{4,6},{5,7},{6,4},{7,5},{8,10},{9,11},{10,... | collective-permute-start | bytes 196616 | tf_op jit(solution)/shard_map/ppermute | solution.py:20
  15.9 8.7 %collective-permute-start.8 = (f32[32,512]{1,0:T(8,128)S(1)}, f32[32,512]{1,0:T(8,128)S(1)}, u32[]{:S(2)}, u32[]{:S(2)}) collective-permute-start(f32[32,512]{1,0:T(8,128)S(1)} %shard_map.132.refs_4_.refs_0_), channel_id=1, source_target_pairs={{0,4},{1,5},{2,6},{3,7},{4,0},{5,1},{6,2},{7,3},{8,12},{9,13},{10,... | collective-permute-start | bytes 196616 | tf_op jit(solution)/shard_map/ppermute | solution.py:20
  18.4 6.3 %collective-permute-start.9 = (f32[32,512]{1,0:T(8,128)S(1)}, f32[32,512]{1,0:T(8,128)S(1)}, u32[]{:S(2)}, u32[]{:S(2)}) collective-permute-start(f32[32,512]{1,0:T(8,128)S(1)} %shard_map.132.refs_4_.refs_0_), channel_id=1, source_target_pairs={{0,6},{1,7},{2,4},{3,5},{4,2},{5,3},{6,0},{7,1},{8,14},{9,15},{10,... | collective-permute-start | bytes 196616 | tf_op jit(solution)/shard_map/ppermute | solution.py:20
  19.8 6.2 %copy-start.10 = (s32[256]{0:T(256)S(1)}, s32[256]{0:T(256)}, u32[]{:S(2)}) copy-start(s32[256]{0:T(256)} %tail_ref.3) | copy-start | bytes 3076
  19.8 6.2 %copy-start.9 = (s32[256]{0:T(256)S(1)}, s32[256]{0:T(256)}, u32[]{:S(2)}) copy-start(s32[256]{0:T(256)} %head_ref.3) | copy-start | bytes 3076
  19.9 6.2 %collective-permute-start.3 = (f32[32,512]{1,0:T(8,128)S(1)}, f32[32,512]{1,0:T(8,128)S(1)}, u32[]{:S(2)}, u32[]{:S(2)}) collective-permute-start(f32[32,512]{1,0:T(8,128)S(1)} %get-tuple-element.41), channel_id=1, source_target_pairs={{0,6},{1,7},{2,4},{3,5},{4,2},{5,3},{6,0},{7,1},{8,14},{9,15},{10,... | collective-permute-start | bytes 196616 | tf_op jit(solution)/shard_map/ppermute | solution.py:20
  22.2 3.8 %collective-permute-start.10 = (f32[32,512]{1,0:T(8,128)S(1)}, f32[32,512]{1,0:T(8,128)S(1)}, u32[]{:S(2)}, u32[]{:S(2)}) collective-permute-start(f32[32,512]{1,0:T(8,128)S(1)} %shard_map.132.refs_4_.refs_0_), channel_id=1, source_target_pairs={{0,1},{1,0},{2,3},{3,2},{4,5},{5,4},{6,7},{7,6},{8,9},{9,8},{10,11... | collective-permute-start | bytes 196616 | tf_op jit(solution)/shard_map/ppermute | solution.py:20
  22.2 3.8 %collective-permute-start.11 = (f32[32,512]{1,0:T(8,128)S(1)}, f32[32,512]{1,0:T(8,128)S(1)}, u32[]{:S(2)}, u32[]{:S(2)}) collective-permute-start(f32[32,512]{1,0:T(8,128)S(1)} %collective-permute-done.7.refs_5_.refs_1_), channel_id=1, source_target_pairs={{0,1},{1,0},{2,3},{3,2},{4,5},{5,4},{6,7},{7,6},{8,9},{9,8},{10,11... | collective-permute-start | bytes 196616 | tf_op jit(solution)/shard_map/ppermute | solution.py:20
  24.6 1.4 %collective-permute-start.12 = (f32[32,512]{1,0:T(8,128)S(1)}, f32[32,512]{1,0:T(8,128)S(1)}, u32[]{:S(2)}, u32[]{:S(2)}) collective-permute-start(f32[32,512]{1,0:T(8,128)S(1)} %collective-permute-done.8.refs_6_.refs_2_), channel_id=1, source_target_pairs={{0,1},{1,0},{2,3},{3,2},{4,5},{5,4},{6,7},{7,6},{8,9},{9,8},{10,11... | collective-permute-start | bytes 196616 | tf_op jit(solution)/shard_map/ppermute | solution.py:20
  24.6 1.4 %collective-permute-start.13 = (f32[32,512]{1,0:T(8,128)S(1)}, f32[32,512]{1,0:T(8,128)S(1)}, u32[]{:S(2)}, u32[]{:S(2)}) collective-permute-start(f32[32,512]{1,0:T(8,128)S(1)} %collective-permute-done.9.refs_7_.refs_3_), channel_id=1, source_target_pairs={{0,1},{1,0},{2,3},{3,2},{4,5},{5,4},{6,7},{7,6},{8,9},{9,8},{10,11... | collective-permute-start | bytes 196616 | tf_op jit(solution)/shard_map/ppermute | solution.py:20
  27.5 1.6 %collective-permute-start.14 = (f32[128,512]{1,0:T(8,128)S(1)}, f32[128,512]{1,0:T(8,128)S(1)}, u32[]{:S(2)}, u32[]{:S(2)}) collective-permute-start(f32[128,512]{1,0:T(8,128)S(1)} %get-tuple-element.44), channel_id=1, source_target_pairs={{0,1},{1,0},{2,3},{3,2},{4,5},{5,4},{6,7},{7,6},{8,9},{9,8},{10,11... | collective-permute-start | bytes 786440 | tf_op jit(solution)/shard_map/ppermute | solution.py:20
  29.2 7.0 %collective-permute-start.18 = (f32[64,512]{1,0:T(8,128)S(1)}, f32[64,512]{1,0:T(8,128)S(1)}, u32[]{:S(2)}, u32[]{:S(2)}) collective-permute-start(f32[64,512]{1,0:T(8,128)S(1)} %get-tuple-element.57), channel_id=1, source_target_pairs={{0,8},{8,0},{16,24},{24,16},{1,9},{9,1},{17,25},{25,17},{2,10},{10... | collective-permute-start | bytes 393224 | tf_op jit(solution)/shard_map/ppermute | solution.py:20
  30.3 6.8 %collective-permute-start.19 = (f32[64,512]{1,0:T(8,128)S(1)}, f32[64,512]{1,0:T(8,128)S(1)}, u32[]{:S(2)}, u32[]{:S(2)}) collective-permute-start(f32[64,512]{1,0:T(8,128)S(1)} %get-tuple-element.58), channel_id=1, source_target_pairs={{0,16},{8,24},{16,0},{24,8},{1,17},{9,25},{17,1},{25,9},{2,18},{10... | collective-permute-start | bytes 393224 | tf_op jit(solution)/shard_map/ppermute | solution.py:20
  31.6 6.9 %collective-permute-start.15 = (f32[64,512]{1,0:T(8,128)S(1)}, f32[64,512]{1,0:T(8,128)S(1)}, u32[]{:S(2)}, u32[]{:S(2)}) collective-permute-start(f32[64,512]{1,0:T(8,128)S(1)} %get-tuple-element.54), channel_id=1, source_target_pairs={{0,2},{1,3},{2,0},{3,1},{4,6},{5,7},{6,4},{7,5},{8,10},{9,11},{10,... | collective-permute-start | bytes 393224 | tf_op jit(solution)/shard_map/ppermute | solution.py:20
  33.8 12.7 %collective-permute-start.16 = (f32[64,512]{1,0:T(8,128)S(1)}, f32[64,512]{1,0:T(8,128)S(1)}, u32[]{:S(2)}, u32[]{:S(2)}) collective-permute-start(f32[64,512]{1,0:T(8,128)S(1)} %get-tuple-element.55), channel_id=1, source_target_pairs={{0,4},{1,5},{2,6},{3,7},{4,0},{5,1},{6,2},{7,3},{8,12},{9,13},{10,... | collective-permute-start | bytes 393224 | tf_op jit(solution)/shard_map/ppermute | solution.py:20
  34.7 11.8 %collective-permute-start.17 = (f32[64,512]{1,0:T(8,128)S(1)}, f32[64,512]{1,0:T(8,128)S(1)}, u32[]{:S(2)}, u32[]{:S(2)}) collective-permute-start(f32[64,512]{1,0:T(8,128)S(1)} %get-tuple-element.56), channel_id=1, source_target_pairs={{0,6},{1,7},{2,4},{3,5},{4,2},{5,3},{6,0},{7,1},{8,14},{9,15},{10,... | collective-permute-start | bytes 393224 | tf_op jit(solution)/shard_map/ppermute | solution.py:20
  36.2 12.1 %collective-permute-start.24 = (f32[64,512]{1,0:T(8,128)S(1)}, f32[64,512]{1,0:T(8,128)S(1)}, u32[]{:S(2)}, u32[]{:S(2)}) collective-permute-start(f32[64,512]{1,0:T(8,128)S(1)} %add.6.refs_4_.low_a), channel_id=1, source_target_pairs={{0,16},{8,24},{16,0},{24,8},{1,17},{9,25},{17,1},{25,9},{2,18},{10... | collective-permute-start | bytes 393224 | tf_op jit(solution)/shard_map/ppermute | solution.py:20
  37.1 13.1 %collective-permute-start.25 = (f32[64,512]{1,0:T(8,128)S(1)}, f32[64,512]{1,0:T(8,128)S(1)}, u32[]{:S(2)}, u32[]{:S(2)}) collective-permute-start(f32[64,512]{1,0:T(8,128)S(1)} %add.7.refs_5_.high_a), channel_id=1, source_target_pairs={{0,8},{8,0},{16,24},{24,16},{1,9},{9,1},{17,25},{25,17},{2,10},{10... | collective-permute-start | bytes 393224 | tf_op jit(solution)/shard_map/ppermute | solution.py:20
  46.5 3.7 %copy-start.3 = (f32[128,512]{1,0:T(8,128)S(1)}, f32[128,512]{1,0:T(8,128)}, u32[]{:S(2)}) copy-start(f32[128,512]{1,0:T(8,128)} %acc_ref.3) | copy-start | bytes 786436
  46.5 7.1 %collective-permute-start.20 = (f32[64,512]{1,0:T(8,128)S(1)}, f32[64,512]{1,0:T(8,128)S(1)}, u32[]{:S(2)}, u32[]{:S(2)}) collective-permute-start(f32[64,512]{1,0:T(8,128)S(1)} %get-tuple-element.60), channel_id=1, source_target_pairs={{0,1},{1,0},{2,3},{3,2},{4,5},{5,4},{6,7},{7,6},{8,9},{9,8},{10,11... | collective-permute-start | bytes 393224 | tf_op jit(solution)/shard_map/ppermute | solution.py:20
  46.6 7.1 %copy-start.2 = (f32[128,512]{1,0:T(8,128)S(1)}, f32[128,512]{1,0:T(8,128)}, u32[]{:S(2)}) copy-start(f32[128,512]{1,0:T(8,128)} %entity_ref.3) | copy-start | bytes 786436
  46.6 7.1 %copy-start.4 = (f32[128,512]{1,0:T(8,128)S(1)}, f32[128,512]{1,0:T(8,128)}, u32[]{:S(2)}) copy-start(f32[128,512]{1,0:T(8,128)} %acc_ref.2) | copy-start | bytes 786436
  46.6 4.5 %collective-permute-start.21 = (f32[32,512]{1,0:T(8,128)S(1)}, f32[32,512]{1,0:T(8,128)S(1)}, u32[]{:S(2)}, u32[]{:S(2)}) collective-permute-start(f32[32,512]{1,0:T(8,128)S(1)} %get-tuple-element.61.refs_0_), channel_id=1, source_target_pairs={{0,8},{8,0},{16,24},{24,16},{1,9},{9,1},{17,25},{25,17},{2,10},{10... | collective-permute-start | bytes 196616 | tf_op jit(solution)/shard_map/ppermute | solution.py:20
  48.0 5.7 %collective-permute-start.22 = (f32[32,512]{1,0:T(8,128)S(1)}, f32[32,512]{1,0:T(8,128)S(1)}, u32[]{:S(2)}, u32[]{:S(2)}) collective-permute-start(f32[32,512]{1,0:T(8,128)S(1)} %get-tuple-element.61.refs_0_), channel_id=1, source_target_pairs={{0,16},{8,24},{16,0},{24,8},{1,17},{9,25},{17,1},{25,9},{2,18},{10... | collective-permute-start | bytes 196616 | tf_op jit(solution)/shard_map/ppermute | solution.py:20
  48.3 5.3 %collective-permute-start.23 = (f32[32,512]{1,0:T(8,128)S(1)}, f32[32,512]{1,0:T(8,128)S(1)}, u32[]{:S(2)}, u32[]{:S(2)}) collective-permute-start(f32[32,512]{1,0:T(8,128)S(1)} %get-tuple-element.61.refs_0_), channel_id=1, source_target_pairs={{0,24},{8,16},{16,8},{24,0},{1,25},{9,17},{17,9},{25,1},{2,26},{10... | collective-permute-start | bytes 196616 | tf_op jit(solution)/shard_map/ppermute | solution.py:20
  50.2 3.5 %copy-start.6 = (s32[1,8,16]{2,1,0:T(8,128)S(1)}, s32[1,8,16]{2,1,0:T(8,128)}, u32[]{:S(2)}) copy-start(s32[1,8,16]{2,1,0:T(8,128)} %send_ref.3) | copy-start | bytes 1540
  50.2 3.5 %copy-start.8 = (s32[8,32]{1,0:T(8,128)S(1)}, s32[8,32]{1,0:T(8,128)}, u32[]{:S(2)}) copy-start(s32[8,32]{1,0:T(8,128)} %neg_ref.3) | copy-start | bytes 3076

commit v3 on v2

--- a/solution.py
+++ b/solution.py
@@ -20,16 +20,16 @@
     return lax.ppermute(block, axis, [(i, i ^ step) for i in range(size)])
 
 
-def call(body, outs, specs, args, flops=0, scratch=()):
+def call(body, outs, specs, args, flops=0, scratch=(), limit=40, out_space=None):
     shapes = [jax.ShapeDtypeStruct(shape, jnp.float32) for shape in outs]
     moved = 4 * sum(int(a.size) for a in args) + 4 * sum(int(s.size) for s in shapes)
     return pl.pallas_call(
         body,
         out_shape=shapes,
         in_specs=specs,
-        out_specs=[VMEM] * len(shapes),
+        out_specs=[out_space or VMEM] * len(shapes),
         scratch_shapes=scratch,
-        compiler_params=pltpu.CompilerParams(vmem_limit_bytes=40 * 1024 * 1024),
+        compiler_params=pltpu.CompilerParams(vmem_limit_bytes=limit * 1024 * 1024),
         cost_estimate=pl.CostEstimate(flops=flops, bytes_accessed=moved, transcendentals=0),
     )(*args)
 
@@ -87,7 +87,10 @@
     return jnp.concatenate(parts, axis=-1)
 
 
-def gather_kernel(send_ref, neg_ref, entity_ref, negs_ref, keep_ref, give_ref, rows, sends, picks, sems):
+def gather_kernel(order, send_ref, neg_ref, entity_ref, negs_out, *refs):
+    count = len(order)
+    outs, (negs, *parcels) = refs[:count], refs[count : 2 * count + 1]
+    rows, sends, picks, sems = refs[2 * count + 1 :]
     copies = [
         pltpu.make_async_copy(source, target, sems.at[i])
         for i, (source, target) in enumerate(
@@ -100,21 +103,19 @@
         copy.wait()
     rel_here = lax.axis_index("rel")
     slots = send_ref.shape[2]
-
-    def neg_row(i, carry):
-        negs_ref[pl.ds(i, 1), :] = rows[pl.ds(picks[rel_here, i], 1), :]
-        return carry
-
-    lax.fori_loop(0, neg_ref.shape[1], neg_row, 0, unroll=8)
-
-    def chip(s, carry):
-        for core, out in ((0, keep_ref), (1, give_ref)):
+    for i in range(neg_ref.shape[1]):
+        negs[pl.ds(i, 1), :] = rows[pl.ds(picks[rel_here, i], 1), :]
+    copies = [pltpu.make_async_copy(negs, negs_out, sems.at[3])]
+    copies[0].start()
+    for s in order:
+        for core in range(2):
             peer = (2 * s + core) ^ rel_here
             for t in range(slots):
-                out[pl.ds(s * slots + t, 1), :] = rows[pl.ds(sends[0, peer, t], 1), :]
-        return carry
-
-    lax.fori_loop(0, send_ref.shape[1] // 2, chip, 0)
+                parcels[s][pl.ds(core * slots + t, 1), :] = rows[pl.ds(sends[0, peer, t], 1), :]
+        copies.append(pltpu.make_async_copy(parcels[s], outs[s], sems.at[4 + s]))
+        copies[-1].start()
+    for copy in copies:
+        copy.wait()
 
 
 def unit_parts(rows):
@@ -144,10 +145,14 @@
 def scores_kernel(
     slots, n_chip, head_ref, tail_ref, rot_ref, *refs
 ):
-    parcels, blocks = refs[:n_chip], refs[n_chip : 3 * n_chip]
-    mine_ref, theirs_ref, query_ref, head_out, tail_out, pull_ref, push_ref = refs[3 * n_chip :]
-    touched = jnp.concatenate([ref[...] for ref in parcels], axis=0)
-    negs = jnp.concatenate([ref[...] for ref in blocks], axis=0)
+    arrived, (stacked, swapped) = refs[:n_chip], refs[n_chip : n_chip + 2]
+    mine_ref, theirs_ref, query_ref, head_out, tail_out, pull_ref, push_ref = refs[n_chip + 2 :]
+    half = mine_ref.shape[0]
+    parts = []
+    for s in range(n_chip):
+        parts += [arrived[s][:slots], swapped[half + s * slots : half + (s + 1) * slots]]
+    touched = jnp.concatenate(parts, axis=0)
+    negs = jnp.concatenate([stacked[:half], swapped[:half]], axis=0)
     trips = head_ref.shape[0]
     rows = take(both_picks(head_ref, tail_ref, slots, touched.shape[0]), touched)
     head, tail = rows[:trips], rows[trips:]
@@ -167,11 +172,10 @@
     theirs_ref[...] = grad[middle:]
 
 
-def grad_kernel(slots, n_chip, head_ref, rel_index_ref, tail_ref, relation_ref, rot_ref, *refs):
-    blocks = refs[: 2 * n_chip]
-    query_ref, head_rows, tail_rows, pull_ref, push_ref = refs[2 * n_chip : 2 * n_chip + 5]
-    low_ref, high_ref, touched_ref = refs[2 * n_chip + 5 :]
-    negs = jnp.concatenate([ref[...] for ref in blocks], axis=0)
+def grad_kernel(slots, half, head_ref, rel_index_ref, tail_ref, relation_ref, rot_ref, *refs):
+    stacked, swapped, query_ref, head_rows, tail_rows, pull_ref, push_ref = refs[:7]
+    low_ref, high_ref, touched_ref = refs[7:]
+    negs = jnp.concatenate([stacked[:half], swapped[:half]], axis=0)
     p_high, p_low = halves(push_ref[...])
     n_high, n_low = halves(negs)
     pulled = dot(p_high, n_high, ROWS) + dot(p_low, n_high, ROWS) + dot(p_high, n_low, ROWS)
@@ -201,14 +205,6 @@
     out_ref[...] = picked
 
 
-def parcel_kernel(slots, own_ref, keep_ref, came_ref, copy_ref, *parcels):
-    copy_ref[...] = own_ref[...]
-    for s, ref in enumerate(parcels):
-        rows = pl.ds(s * slots, slots)
-        ref[:slots] = keep_ref[rows]
-        ref[slots:] = came_ref[rows]
-
-
 def pack_kernel(slots, n_neg, mine, theirs, touched, low, high, low_ref, high_ref, *back):
     low_ref[...] = low[...]
     high_ref[...] = high[...]
@@ -218,10 +214,20 @@
         ref[2 * slots :] = mine[block] + theirs[block]
 
 
-def unpack_kernel(slots, n_chip, *refs):
-    back, (neg_ref, stay_ref, cross_ref) = refs[:n_chip], refs[-3:]
+def stack_kernel(order, *refs):
+    count = len(order)
+    arrived, negs, out_ref = refs[:count], refs[count : 2 * count], refs[-1]
+    n_neg, slots = negs[0].shape[0], arrived[0].shape[0] // 2
+    for s, block, rows in zip(order, negs, arrived):
+        out_ref[s * n_neg : (s + 1) * n_neg] = block[...]
+        start = count * n_neg + s * slots
+        out_ref[start : start + slots] = rows[slots:]
+
+
+def unpack_kernel(slots, order, *refs):
+    back, (neg_ref, stay_ref, cross_ref) = refs[: len(order)], refs[-3:]
     neg_ref[...] = sum(ref[2 * slots :] for ref in back)
-    for s, ref in enumerate(back):
+    for s, ref in zip(order, back):
         rows = pl.ds(s * slots, slots)
         stay_ref[rows] = ref[:slots]
         cross_ref[rows] = ref[slots : 2 * slots]
@@ -277,28 +283,25 @@
     n_neg = neg_rows.shape[1]
     n_chip = n_rel // 2
 
-    own_negs, keep, give = call(
-        gather_kernel,
-        [(n_neg, width), (n_chip * slots, width), (n_chip * slots, width)],
+    order = [*range(2, n_chip), *range(min(n_chip, 2))]
+    own_negs, *parcels = call(
+        functools.partial(gather_kernel, order),
+        [(n_neg, width)] + [(2 * slots, width)] * n_chip,
         [HBM, HBM, HBM],
         (send_rows, neg_rows, entity),
-        scratch=[
+        limit=60,
+        out_space=HBM,
+        scratch=[pltpu.VMEM((n_neg, width), jnp.float32)]
+        + [pltpu.VMEM((2 * slots, width), jnp.float32)] * n_chip
+        + [
             pltpu.VMEM(entity.shape, jnp.float32),
             pltpu.SMEM(send_rows.shape, jnp.int32),
             pltpu.SMEM(neg_rows.shape, jnp.int32),
-            pltpu.SemaphoreType.DMA((3,)),
+            pltpu.SemaphoreType.DMA((4 + n_chip,)),
         ],
     )
-    came = exchange(give, "rel", n_rel, 1)
-    near = exchange(own_negs, "dom", n_dom, 1)
-    copied, *parcels = call(
-        functools.partial(parcel_kernel, slots),
-        [own_negs.shape] + [(2 * slots, width)] * n_chip,
-        [VMEM] * 3,
-        (own_negs, keep, came),
-    )
+    spread = [own_negs] + [exchange(own_negs, "dom", n_dom, s) for s in range(1, n_dom)]
     arrived = [parcels[0]] + [exchange(parcels[s], "rel", n_rel, 2 * s) for s in range(1, n_chip)]
-    spread = [copied, near] + [exchange(copied, "dom", n_dom, s) for s in range(2, n_dom)]
     (rot,) = call(rotation_kernel, [(trips, width)], [VMEM] * 2, (trip_rel, relation))
     (picked,) = call(
         select_kernel,
@@ -307,20 +310,26 @@
         (neg_part, rot, *spread),
     )
     negs = [picked] + [exchange(picked, "rel", n_rel, 2 * s) for s in range(1, n_chip)]
-    others = [exchange(block, "rel", n_rel, 1) for block in negs]
+    (stacked,) = call(
+        functools.partial(stack_kernel, order),
+        [(n_chip * (n_neg + slots), width)],
+        [VMEM] * (2 * n_chip),
+        (*[arrived[s] for s in order], *[negs[s] for s in order]),
+    )
+    swapped = exchange(stacked, "rel", n_rel, 1)
 
     mine, theirs, *saved = call(
         functools.partial(scores_kernel, slots, n_chip),
         [(n_chip * n_neg, width)] * 2 + [(trips, width)] * 3 + [(trips, 128), (trips, n_rel * n_neg)],
-        [VMEM] * (3 + 3 * n_chip),
-        (trip_head, trip_tail, rot, *arrived, *negs, *others),
+        [VMEM] * (5 + n_chip),
+        (trip_head, trip_tail, rot, *arrived, stacked, swapped),
     )
     theirs = exchange(theirs, "rel", n_rel, 1)
     low, high, touched = call(
-        functools.partial(grad_kernel, slots, n_chip),
+        functools.partial(grad_kernel, slots, n_chip * n_neg),
         [(rels // 2, width)] * 2 + [(n_rel * slots, width)],
-        [VMEM] * (10 + 2 * n_chip),
-        (trip_head, trip_rel, trip_tail, relation, rot, *negs, *others, *saved),
+        [VMEM] * 12,
+        (trip_head, trip_rel, trip_tail, relation, rot, stacked, swapped, *saved),
     )
 
     low, high, *back = call(
@@ -339,10 +348,10 @@
         sums[0].append(exchange(sums[0][0], "dom", n_dom, up))
         sums[1].append(exchange(sums[1][0], "dom", n_dom, down))
     neg_share, stay, cross = call(
-        functools.partial(unpack_kernel, slots, n_chip),
+        functools.partial(unpack_kernel, slots, order),
         [(n_neg, width)] + [(n_chip * slots, width)] * 2,
-        [VMEM] * (n_chip + len(first)),
-        (*back, *first),
+        [VMEM] * n_chip,
+        [back[s] for s in order],
     )
     neg_shares = [neg_share] + [exchange(neg_share, "dom", n_dom, s) for s in range(1, n_dom)]
     cross = exchange(cross, "rel", n_rel, 1)

time: 55.1 us -> 51.8 us (0.940)
  starting transfers between devices: 30.9 us -> 26.2 us
  waiting for transfers between devices: 13.9 us -> 16.2 us
  local copies, waits for them, and re-layouts: 2.4 us -> 0.6 us
  Pallas kernels: 6.19 us -> 6.97 us
    ppermute x26 -> x22, starting transfers between devices: 30.9 us -> 26.2 us  [exchange(): return lax.ppermute(block, axis, [(i, i ^ step) for i in range(size)])]
    ppermute x26 -> x22, waiting for transfers between devices: 13.9 us -> 16.2 us  [exchange(): return lax.ppermute(block, axis, [(i, i ^ step) for i in range(size)])]
    unnamed x24, local copies, waits for them, and re-layouts: 2.4 us -> 0.6 us
    pallas_call x10, Pallas kernels: 6.19 us -> 6.97 us  [call(): pl.pallas_call(body, out_shape=shapes, in_specs=specs, out_specs=[out_spa...]
  transfers between devices with their start and end apart: 26 -> 22, of which waited for: 7 -> 9; matrix products, arithmetic and copies ran while one was open for 0% -> 0% of each run, Pallas kernels for 4% -> 4%
where the time goes in v3:
time: 51.8 us; the launch traced here: 51.6 us
  starting transfers between devices  26.2 us (51%)
  waiting for transfers between devices  16.2 us (31%)
  Pallas kernels  6.97 us (13%)
  between operations  1.49 us (3%)
  local copies, waits for them, and re-layouts  0.6 us (1%)
    ppermute x22, starting transfers between devices, exchange(): return lax.ppermute(block, axis, [(i, i ^ step) for i in range(size)])  26.2 us
    ppermute x22, waiting for transfers between devices, exchange(): return lax.ppermute(block, axis, [(i, i ^ step) for i in range(size)])  16.2 us
    pallas_call x10, Pallas kernels, call(): pl.pallas_call(body, out_shape=shapes, in_specs=specs, out_specs=[out_spa...  6.97 us
  transfers between devices with their start and end apart: 22, of which 9 were waited for; matrix products, arithmetic and copies ran while one was open for 0% of the time, Pallas kernels for 4%

profile of v3, /device:TPU:0, one launch (start us, length us, event | category | flops | bytes accessed | tf_op | source)
XLA Modules:
  0.0 51.6 jit_solution(14266015931529816373)
XLA Ops:
  0.6 2.0 %shard_map.130 = (f32[32,512]{1,0:T(8,128)}, f32[32,512]{1,0:T(8,128)}, f32[32,512]{1,0:T(8,128)}, f32[32,512]{1,0:T(8,128)}, f32[32,512]{1,0:T(8,128)}) custom-call(s32[1,8,16]{2,1,0:T(8,128)} %send_ref.3, s32[8,32]{1,0:T(8,128)} %neg_ref.3, f32[128,512]{1,0:T(8,128)} %entity_ref.3), custom_call_target="tpu_custom_call" | custom-call | bytes 591360 | tf_op jit(solution)/shard_map/pallas_call | solution.py:26
  2.7 3.0 %collective-permute-start.3 = (f32[32,512]{1,0:T(8,128)}, f32[32,512]{1,0:T(8,128)S(1)}, u32[]{:S(2)}, u32[]{:S(2)}) collective-permute-start(f32[32,512]{1,0:T(8,128)} %get-tuple-element.36.refs_0_), channel_id=1, source_target_pairs={{0,8},{8,0},{16,24},{24,16},{1,9},{9,1},{17,25},{25,17},{2,10},{10... | collective-permute-start | bytes 196616 | tf_op jit(solution)/shard_map/ppermute | solution.py:20
  5.7 1.5 %collective-permute-start.4 = (f32[32,512]{1,0:T(8,128)}, f32[32,512]{1,0:T(8,128)S(1)}, u32[]{:S(2)}, u32[]{:S(2)}) collective-permute-start(f32[32,512]{1,0:T(8,128)} %get-tuple-element.36.refs_0_), channel_id=1, source_target_pairs={{0,16},{8,24},{16,0},{24,8},{1,17},{9,25},{17,1},{25,9},{2,18},{10... | collective-permute-start | bytes 196616 | tf_op jit(solution)/shard_map/ppermute | solution.py:20
  7.2 0.0 collective-permute-start.5
  7.2 2.0 %collective-permute-start = (f32[32,512]{1,0:T(8,128)}, f32[32,512]{1,0:T(8,128)S(1)}, u32[]{:S(2)}, u32[]{:S(2)}) collective-permute-start(f32[32,512]{1,0:T(8,128)} %get-tuple-element.33), channel_id=1, source_target_pairs={{0,2},{1,3},{2,0},{3,1},{4,6},{5,7},{6,4},{7,5},{8,10},{9,11},{10,... | collective-permute-start | bytes 196616 | tf_op jit(solution)/shard_map/ppermute | solution.py:20
  9.2 2.6 %collective-permute-start.1 = (f32[32,512]{1,0:T(8,128)}, f32[32,512]{1,0:T(8,128)S(1)}, u32[]{:S(2)}, u32[]{:S(2)}) collective-permute-start(f32[32,512]{1,0:T(8,128)} %get-tuple-element.34), channel_id=1, source_target_pairs={{0,4},{1,5},{2,6},{3,7},{4,0},{5,1},{6,2},{7,3},{8,12},{9,13},{10,... | collective-permute-start | bytes 196616 | tf_op jit(solution)/shard_map/ppermute | solution.py:20
  12.5 0.0 copy-start.5
  12.5 0.3 shard_map.129.after_ref.rot_ref
  12.8 0.5 %copy-done.11 = f32[32,512]{1,0:T(8,128)S(1)} copy-done((f32[32,512]{1,0:T(8,128)S(1)}, f32[32,512]{1,0:T(8,128)}, u32[]{:S(2)}) %copy-start.11) | copy-done | bytes 65560
  13.4 0.0 collective-permute-start.2
  13.4 0.0 collective-permute-done.5.refs_3_
  13.4 0.0 copy-done.5
  13.4 2.0 %collective-permute-start.6 = (f32[32,512]{1,0:T(8,128)S(1)}, f32[32,512]{1,0:T(8,128)S(1)}, u32[]{:S(2)}, u32[]{:S(2)}) collective-permute-start(f32[32,512]{1,0:T(8,128)S(1)} %shard_map.131.refs_6_), channel_id=1, source_target_pairs={{0,4},{1,5},{2,6},{3,7},{4,0},{5,1},{6,2},{7,3},{8,12},{9,13},{10,... | collective-permute-start | bytes 196616 | tf_op jit(solution)/shard_map/ppermute | solution.py:20
  15.4 2.0 %collective-permute-start.7 = (f32[32,512]{1,0:T(8,128)S(1)}, f32[32,512]{1,0:T(8,128)S(1)}, u32[]{:S(2)}, u32[]{:S(2)}) collective-permute-start(f32[32,512]{1,0:T(8,128)S(1)} %shard_map.131.refs_6_), channel_id=1, source_target_pairs={{0,6},{1,7},{2,4},{3,5},{4,2},{5,3},{6,0},{7,1},{8,14},{9,15},{10,... | collective-permute-start | bytes 196616 | tf_op jit(solution)/shard_map/ppermute | solution.py:20
  17.4 0.5 collective-permute-start.8
  17.9 0.0 collective-permute-done.1.refs_0_.refs_2_
  17.9 2.0 %collective-permute-done.2.refs_1_.refs_3_ = f32[32,512]{1,0:T(8,128)S(1)} collective-permute-done((f32[32,512]{1,0:T(8,128)S(1)}, f32[32,512]{1,0:T(8,128)S(1)}, u32[]{:S(2)}, u32[]{:S(2)}) %collective-permute-start.2) | collective-permute-done | bytes 65568 | tf_op jit(solution)/shard_map/ppermute | solution.py:20
  19.9 3.2 %collective-permute-done.6.refs_4_ = f32[32,512]{1,0:T(8,128)S(1)} collective-permute-done((f32[32,512]{1,0:T(8,128)S(1)}, f32[32,512]{1,0:T(8,128)S(1)}, u32[]{:S(2)}, u32[]{:S(2)}) %collective-permute-start.6) | collective-permute-done | bytes 65568 | tf_op jit(solution)/shard_map/ppermute | solution.py:20
  23.1 0.0 copy-start.8
  23.1 0.0 copy-start.9
  23.1 0.1 collective-permute-start.9
  23.2 1.7 %collective-permute-done.9.refs_5_.refs_1_ = f32[192,512]{1,0:T(8,128)S(1)} collective-permute-done((f32[192,512]{1,0:T(8,128)S(1)}, f32[192,512]{1,0:T(8,128)S(1)}, u32[]{:S(2)}, u32[]{:S(2)}) %collective-permute-start.9) | collective-permute-done | bytes 393248 | tf_op jit(solution)/shard_map/ppermute | solution.py:20
  24.9 1.5 %shard_map.133 = (f32[128,512]{1,0:T(8,128)S(1)}, f32[128,512]{1,0:T(8,128)S(1)}, f32[256,512]{1,0:T(8,128)S(1)}, f32[256,512]{1,0:T(8,128)S(1)}, f32[256,512]{1...) custom-call(s32[256]{0:T(256)S(1)} %copy-done.8, s32[256]{0:T(256)S(1)} %copy-done.9, ...), custom_call_target="tpu_custom_call" | custom-call | bytes 4065280 | tf_op jit(solution)/shard_map/pallas_call | solution.py:26
  26.4 0.2 collective-permute-start.10
  26.6 1.1 %shard_map.134 = (f32[64,512]{1,0:T(8,128)S(1)}, f32[64,512]{1,0:T(8,128)S(1)}, f32[128,512]{1,0:T(8,128)S(1)}) custom-call(s32[256]{0:T(256)S(1)} %copy-done.8, s32[256]{0:T(256)S(1)} %copy-done.10, s32[256]{0:T(256)S(1)} %copy-done.9, f32[128,512]{1,0:T(8,128)S(1)} %copy-done, f32[256,512]{1,0:T(8,128)S(1)} %shard_map.129.after_ref.rot_ref, ...), custom_call_target="tpu_custom_call" | custom-call | bytes 4066304 | tf_op jit(solution)/shard_map/pallas_call | solution.py:26
  27.7 0.3 collective-permute-done.10.theirs
  28.0 0.1 shard_map.135
  28.1 1.6 %collective-permute-start.18 = (f32[64,512]{1,0:T(8,128)S(1)}, f32[64,512]{1,0:T(8,128)S(1)}, u32[]{:S(2)}, u32[]{:S(2)}) collective-permute-start(f32[64,512]{1,0:T(8,128)S(1)} %get-tuple-element.56), channel_id=1, source_target_pairs={{0,8},{8,0},{16,24},{24,16},{1,9},{9,1},{17,25},{25,17},{2,10},{10... | collective-permute-start | bytes 393224 | tf_op jit(solution)/shard_map/ppermute | solution.py:20
  29.6 1.5 %collective-permute-start.20 = (f32[64,512]{1,0:T(8,128)S(1)}, f32[64,512]{1,0:T(8,128)S(1)}, u32[]{:S(2)}, u32[]{:S(2)}) collective-permute-start(f32[64,512]{1,0:T(8,128)S(1)} %get-tuple-element.57), channel_id=1, source_target_pairs={{0,16},{8,24},{16,0},{24,8},{1,17},{9,25},{17,1},{25,9},{2,18},{10... | collective-permute-start | bytes 393224 | tf_op jit(solution)/shard_map/ppermute | solution.py:20
  31.1 2.0 %collective-permute-start.11 = (f32[64,512]{1,0:T(8,128)S(1)}, f32[64,512]{1,0:T(8,128)S(1)}, u32[]{:S(2)}, u32[]{:S(2)}) collective-permute-start(f32[64,512]{1,0:T(8,128)S(1)} %get-tuple-element.47), channel_id=1, source_target_pairs={{0,4},{1,5},{2,6},{3,7},{4,0},{5,1},{6,2},{7,3},{8,12},{9,13},{10,... | collective-permute-start | bytes 393224 | tf_op jit(solution)/shard_map/ppermute | solution.py:20
  33.1 1.7 %collective-permute-start.12 = (f32[64,512]{1,0:T(8,128)S(1)}, f32[64,512]{1,0:T(8,128)S(1)}, u32[]{:S(2)}, u32[]{:S(2)}) collective-permute-start(f32[64,512]{1,0:T(8,128)S(1)} %get-tuple-element.48), channel_id=1, source_target_pairs={{0,6},{1,7},{2,4},{3,5},{4,2},{5,3},{6,0},{7,1},{8,14},{9,15},{10,... | collective-permute-start | bytes 393224 | tf_op jit(solution)/shard_map/ppermute | solution.py:20
  34.8 0.0 collective-permute-start.13
  34.8 0.0 collective-permute-done.18
  34.8 0.6 %collective-permute-start.19 = (f32[64,512]{1,0:T(8,128)S(1)}, f32[64,512]{1,0:T(8,128)S(1)}, u32[]{:S(2)}, u32[]{:S(2)}) collective-permute-start(f32[64,512]{1,0:T(8,128)S(1)} %add.6.low_a), channel_id=1, source_target_pairs={{0,16},{8,24},{16,0},{24,8},{1,17},{9,25},{17,1},{25,9},{2,18},{10... | collective-permute-start | bytes 393224 | tf_op jit(solution)/shard_map/ppermute | solution.py:20
  35.4 1.5 %collective-permute-start.21 = (f32[64,512]{1,0:T(8,128)S(1)}, f32[64,512]{1,0:T(8,128)S(1)}, u32[]{:S(2)}, u32[]{:S(2)}) collective-permute-start(f32[64,512]{1,0:T(8,128)S(1)} %add.7.high_a), channel_id=1, source_target_pairs={{0,8},{8,0},{16,24},{24,16},{1,9},{9,1},{17,25},{25,17},{2,10},{10... | collective-permute-start | bytes 393224 | tf_op jit(solution)/shard_map/ppermute | solution.py:20
  36.9 6.6 %collective-permute-done.11.refs_0_ = f32[64,512]{1,0:T(8,128)S(1)} collective-permute-done((f32[64,512]{1,0:T(8,128)S(1)}, f32[64,512]{1,0:T(8,128)S(1)}, u32[]{:S(2)}, u32[]{:S(2)}) %collective-permute-start.11) | collective-permute-done | bytes 131104 | tf_op jit(solution)/shard_map/ppermute | solution.py:20
  43.5 0.5 %collective-permute-done.13.refs_3_ = f32[64,512]{1,0:T(8,128)S(1)} collective-permute-done((f32[64,512]{1,0:T(8,128)S(1)}, f32[64,512]{1,0:T(8,128)S(1)}, u32[]{:S(2)}, u32[]{:S(2)}) %collective-permute-start.13) | collective-permute-done | bytes 131104 | tf_op jit(solution)/shard_map/ppermute | solution.py:20
  44.0 0.1 collective-permute-start.14
  44.1 0.0 copy-start.1
  44.1 0.0 copy-start.4
  44.1 0.6 %collective-permute-start.15 = (f32[32,512]{1,0:T(8,128)S(1)}, f32[32,512]{1,0:T(8,128)S(1)}, u32[]{:S(2)}, u32[]{:S(2)}) collective-permute-start(f32[32,512]{1,0:T(8,128)S(1)} %get-tuple-element.53.refs_0_), channel_id=1, source_target_pairs={{0,8},{8,0},{16,24},{24,16},{1,9},{9,1},{17,25},{25,17},{2,10},{10... | collective-permute-start | bytes 196616 | tf_op jit(solution)/shard_map/ppermute | solution.py:20
  44.7 0.5 collective-permute-start.16
  45.3 2.4 %collective-permute-start.17 = (f32[32,512]{1,0:T(8,128)S(1)}, f32[32,512]{1,0:T(8,128)S(1)}, u32[]{:S(2)}, u32[]{:S(2)}) collective-permute-start(f32[32,512]{1,0:T(8,128)S(1)} %get-tuple-element.53.refs_0_), channel_id=1, source_target_pairs={{0,24},{8,16},{16,8},{24,0},{1,25},{9,17},{17,9},{25,1},{2,26},{10... | collective-permute-start | bytes 196616 | tf_op jit(solution)/shard_map/ppermute | solution.py:20
  47.7 0.9 %shard_map.138 = (f32[128,512]{1,0:T(8,128)}, f32[128,512]{1,0:T(8,128)}) custom-call(f32[64,512]{1,0:T(8,128)S(1)} %add.6.low_a, f32[64,512]{1,0:T(8,128)S(1)} %collective-permute-done.19.low_b, f32[64,512]{1,0:T(8,128)S(1)} %add.7.high_a, f32[64,512]{1,0:T(8,128)S(1)} %collective-permute-done.21.high_b, f32[128,512]{1,0:T(8,128)S(1)} %copy-done, ...), custom_call_target="tpu_custom_call" | custom-call | bytes 1572864 | tf_op jit(solution)/shard_map/pallas_call | solution.py:26
  48.6 0.1 collective-permute-done.15.refs_1_
  48.6 1.1 %collective-permute-done.16.refs_2_ = f32[32,512]{1,0:T(8,128)S(1)} collective-permute-done((f32[32,512]{1,0:T(8,128)S(1)}, f32[32,512]{1,0:T(8,128)S(1)}, u32[]{:S(2)}, u32[]{:S(2)}) %collective-permute-start.16) | collective-permute-done | bytes 65568 | tf_op jit(solution)/shard_map/ppermute | solution.py:20
  49.7 0.7 %collective-permute-done.17.refs_3_ = f32[32,512]{1,0:T(8,128)S(1)} collective-permute-done((f32[32,512]{1,0:T(8,128)S(1)}, f32[32,512]{1,0:T(8,128)S(1)}, u32[]{:S(2)}, u32[]{:S(2)}) %collective-permute-start.17) | collective-permute-done | bytes 65568 | tf_op jit(solution)/shard_map/ppermute | solution.py:20
  50.4 1.1 %shard_map.137 = (f32[128,512]{1,0:T(8,128)}, f32[128,512]{1,0:T(8,128)}) custom-call(s32[1]{0:T(128)S(6)} %copy.14.part_ref, s32[1,8,16]{2,1,0:T(8,128)S(1)} %copy-done.6, s32[8,32]{1,0:T(8,128)S(1)} %copy-done.7, f32[128,512]{1,0:T(8,128)S(1)} %copy-done.1, f32[128,512]{1,0:T(8,128)S(1)} %copy-done.4, f32[64,512]{1,0:T(8,128)S(1)} %get-tuple-element.51.stay_ref, ...), custom_call_target="tpu_custom_call" | custom-call | bytes 1574404 | tf_op jit(solution)/shard_map/pallas_call | solution.py:26
  (32 shorter events, 0.2 us)
Async XLA Ops:
  0.6 11.9 %copy-start = (f32[128,512]{1,0:T(8,128)S(1)}, f32[128,512]{1,0:T(8,128)}, u32[]{:S(2)}) copy-start(f32[128,512]{1,0:T(8,128)} %relation_ref.5) | copy-start | bytes 786436
  2.7 10.1 %collective-permute-start.3 = (f32[32,512]{1,0:T(8,128)}, f32[32,512]{1,0:T(8,128)S(1)}, u32[]{:S(2)}, u32[]{:S(2)}) collective-permute-start(f32[32,512]{1,0:T(8,128)} %get-tuple-element.36.refs_0_), channel_id=1, source_target_pairs={{0,8},{8,0},{16,24},{24,16},{1,9},{9,1},{17,25},{25,17},{2,10},{10... | collective-permute-start | bytes 196616 | tf_op jit(solution)/shard_map/ppermute | solution.py:20
  5.7 7.7 %collective-permute-start.4 = (f32[32,512]{1,0:T(8,128)}, f32[32,512]{1,0:T(8,128)S(1)}, u32[]{:S(2)}, u32[]{:S(2)}) collective-permute-start(f32[32,512]{1,0:T(8,128)} %get-tuple-element.36.refs_0_), channel_id=1, source_target_pairs={{0,16},{8,24},{16,0},{24,8},{1,17},{9,25},{17,1},{25,9},{2,18},{10... | collective-permute-start | bytes 196616 | tf_op jit(solution)/shard_map/ppermute | solution.py:20
  7.2 6.2 %collective-permute-start.5 = (f32[32,512]{1,0:T(8,128)}, f32[32,512]{1,0:T(8,128)S(1)}, u32[]{:S(2)}, u32[]{:S(2)}) collective-permute-start(f32[32,512]{1,0:T(8,128)} %get-tuple-element.36.refs_0_), channel_id=1, source_target_pairs={{0,24},{8,16},{16,8},{24,0},{1,25},{9,17},{17,9},{25,1},{2,26},{10... | collective-permute-start | bytes 196616 | tf_op jit(solution)/shard_map/ppermute | solution.py:20
  7.2 10.2 %collective-permute-start = (f32[32,512]{1,0:T(8,128)}, f32[32,512]{1,0:T(8,128)S(1)}, u32[]{:S(2)}, u32[]{:S(2)}) collective-permute-start(f32[32,512]{1,0:T(8,128)} %get-tuple-element.33), channel_id=1, source_target_pairs={{0,2},{1,3},{2,0},{3,1},{4,6},{5,7},{6,4},{7,5},{8,10},{9,11},{10,... | collective-permute-start | bytes 196616 | tf_op jit(solution)/shard_map/ppermute | solution.py:20
  9.2 3.3 %copy-start.10 = (s32[256]{0:T(256)S(1)}, s32[256]{0:T(256)}, u32[]{:S(2)}) copy-start(s32[256]{0:T(256)} %rel_index_ref.3) | copy-start | bytes 3076
  9.2 8.6 %collective-permute-start.1 = (f32[32,512]{1,0:T(8,128)}, f32[32,512]{1,0:T(8,128)S(1)}, u32[]{:S(2)}, u32[]{:S(2)}) collective-permute-start(f32[32,512]{1,0:T(8,128)} %get-tuple-element.34), channel_id=1, source_target_pairs={{0,4},{1,5},{2,6},{3,7},{4,0},{5,1},{6,2},{7,3},{8,12},{9,13},{10,... | collective-permute-start | bytes 196616 | tf_op jit(solution)/shard_map/ppermute | solution.py:20
  12.5 0.8 %copy-start.11 = (f32[32,512]{1,0:T(8,128)S(1)}, f32[32,512]{1,0:T(8,128)}, u32[]{:S(2)}) copy-start(f32[32,512]{1,0:T(8,128)} %get-tuple-element.35) | copy-start | bytes 196612
  12.5 0.9 %copy-start.5 = (f32[32,512]{1,0:T(8,128)S(1)}, f32[32,512]{1,0:T(8,128)}, u32[]{:S(2)}) copy-start(f32[32,512]{1,0:T(8,128)} %get-tuple-element.36.refs_0_) | copy-start | bytes 196612
  13.3 9.7 %copy-start.2 = (f32[32,512]{1,0:T(8,128)S(1)}, f32[32,512]{1,0:T(8,128)}, u32[]{:S(2)}) copy-start(f32[32,512]{1,0:T(8,128)} %get-tuple-element.32.refs_2_.refs_0_) | copy-start | bytes 196612
  13.4 6.5 %collective-permute-start.2 = (f32[32,512]{1,0:T(8,128)S(1)}, f32[32,512]{1,0:T(8,128)S(1)}, u32[]{:S(2)}, u32[]{:S(2)}) collective-permute-start(f32[32,512]{1,0:T(8,128)S(1)} %copy-done.11), channel_id=1, source_target_pairs={{0,6},{1,7},{2,4},{3,5},{4,2},{5,3},{6,0},{7,1},{8,14},{9,15},{10,... | collective-permute-start | bytes 196616 | tf_op jit(solution)/shard_map/ppermute | solution.py:20
  13.4 9.6 %collective-permute-start.6 = (f32[32,512]{1,0:T(8,128)S(1)}, f32[32,512]{1,0:T(8,128)S(1)}, u32[]{:S(2)}, u32[]{:S(2)}) collective-permute-start(f32[32,512]{1,0:T(8,128)S(1)} %shard_map.131.refs_6_), channel_id=1, source_target_pairs={{0,4},{1,5},{2,6},{3,7},{4,0},{5,1},{6,2},{7,3},{8,12},{9,13},{10,... | collective-permute-start | bytes 196616 | tf_op jit(solution)/shard_map/ppermute | solution.py:20
  15.4 7.7 %collective-permute-start.7 = (f32[32,512]{1,0:T(8,128)S(1)}, f32[32,512]{1,0:T(8,128)S(1)}, u32[]{:S(2)}, u32[]{:S(2)}) collective-permute-start(f32[32,512]{1,0:T(8,128)S(1)} %shard_map.131.refs_6_), channel_id=1, source_target_pairs={{0,6},{1,7},{2,4},{3,5},{4,2},{5,3},{6,0},{7,1},{8,14},{9,15},{10,... | collective-permute-start | bytes 196616 | tf_op jit(solution)/shard_map/ppermute | solution.py:20
  17.4 5.7 %collective-permute-start.8 = (f32[32,512]{1,0:T(8,128)S(1)}, f32[32,512]{1,0:T(8,128)S(1)}, u32[]{:S(2)}, u32[]{:S(2)}) collective-permute-start(f32[32,512]{1,0:T(8,128)S(1)} %shard_map.131.refs_6_), channel_id=1, source_target_pairs={{0,2},{1,3},{2,0},{3,1},{4,6},{5,7},{6,4},{7,5},{8,10},{9,11},{10,... | collective-permute-start | bytes 196616 | tf_op jit(solution)/shard_map/ppermute | solution.py:20
  23.1 1.9 %copy-start.8 = (s32[256]{0:T(256)S(1)}, s32[256]{0:T(256)}, u32[]{:S(2)}) copy-start(s32[256]{0:T(256)} %head_ref.3) | copy-start | bytes 3076
  23.1 1.8 %copy-start.9 = (s32[256]{0:T(256)S(1)}, s32[256]{0:T(256)}, u32[]{:S(2)}) copy-start(s32[256]{0:T(256)} %tail_ref.3) | copy-start | bytes 3076
  23.1 1.8 %collective-permute-start.9 = (f32[192,512]{1,0:T(8,128)S(1)}, f32[192,512]{1,0:T(8,128)S(1)}, u32[]{:S(2)}, u32[]{:S(2)}) collective-permute-start(f32[192,512]{1,0:T(8,128)S(1)} %shard_map.132.refs_4_.refs_0_), channel_id=1, source_target_pairs={{0,1},{1,0},{2,3},{3,2},{4,5},{5,4},{6,7},{7,6},{8,9},{9,8},{10,11... | collective-permute-start | bytes 1179656 | tf_op jit(solution)/shard_map/ppermute | solution.py:20
  26.4 1.6 %collective-permute-start.10 = (f32[128,512]{1,0:T(8,128)S(1)}, f32[128,512]{1,0:T(8,128)S(1)}, u32[]{:S(2)}, u32[]{:S(2)}) collective-permute-start(f32[128,512]{1,0:T(8,128)S(1)} %get-tuple-element.38), channel_id=1, source_target_pairs={{0,1},{1,0},{2,3},{3,2},{4,5},{5,4},{6,7},{7,6},{8,9},{9,8},{10,11... | collective-permute-start | bytes 786440 | tf_op jit(solution)/shard_map/ppermute | solution.py:20
  28.1 6.7 %collective-permute-start.18 = (f32[64,512]{1,0:T(8,128)S(1)}, f32[64,512]{1,0:T(8,128)S(1)}, u32[]{:S(2)}, u32[]{:S(2)}) collective-permute-start(f32[64,512]{1,0:T(8,128)S(1)} %get-tuple-element.56), channel_id=1, source_target_pairs={{0,8},{8,0},{16,24},{24,16},{1,9},{9,1},{17,25},{25,17},{2,10},{10... | collective-permute-start | bytes 393224 | tf_op jit(solution)/shard_map/ppermute | solution.py:20
  29.6 5.7 %collective-permute-start.20 = (f32[64,512]{1,0:T(8,128)S(1)}, f32[64,512]{1,0:T(8,128)S(1)}, u32[]{:S(2)}, u32[]{:S(2)}) collective-permute-start(f32[64,512]{1,0:T(8,128)S(1)} %get-tuple-element.57), channel_id=1, source_target_pairs={{0,16},{8,24},{16,0},{24,8},{1,17},{9,25},{17,1},{25,9},{2,18},{10... | collective-permute-start | bytes 393224 | tf_op jit(solution)/shard_map/ppermute | solution.py:20
  31.1 12.3 %collective-permute-start.11 = (f32[64,512]{1,0:T(8,128)S(1)}, f32[64,512]{1,0:T(8,128)S(1)}, u32[]{:S(2)}, u32[]{:S(2)}) collective-permute-start(f32[64,512]{1,0:T(8,128)S(1)} %get-tuple-element.47), channel_id=1, source_target_pairs={{0,4},{1,5},{2,6},{3,7},{4,0},{5,1},{6,2},{7,3},{8,12},{9,13},{10,... | collective-permute-start | bytes 393224 | tf_op jit(solution)/shard_map/ppermute | solution.py:20
  33.1 10.4 %collective-permute-start.12 = (f32[64,512]{1,0:T(8,128)S(1)}, f32[64,512]{1,0:T(8,128)S(1)}, u32[]{:S(2)}, u32[]{:S(2)}) collective-permute-start(f32[64,512]{1,0:T(8,128)S(1)} %get-tuple-element.48), channel_id=1, source_target_pairs={{0,6},{1,7},{2,4},{3,5},{4,2},{5,3},{6,0},{7,1},{8,14},{9,15},{10,... | collective-permute-start | bytes 393224 | tf_op jit(solution)/shard_map/ppermute | solution.py:20
  34.8 9.2 %collective-permute-start.13 = (f32[64,512]{1,0:T(8,128)S(1)}, f32[64,512]{1,0:T(8,128)S(1)}, u32[]{:S(2)}, u32[]{:S(2)}) collective-permute-start(f32[64,512]{1,0:T(8,128)S(1)} %get-tuple-element.50), channel_id=1, source_target_pairs={{0,2},{1,3},{2,0},{3,1},{4,6},{5,7},{6,4},{7,5},{8,10},{9,11},{10,... | collective-permute-start | bytes 393224 | tf_op jit(solution)/shard_map/ppermute | solution.py:20
  34.8 10.5 %collective-permute-start.19 = (f32[64,512]{1,0:T(8,128)S(1)}, f32[64,512]{1,0:T(8,128)S(1)}, u32[]{:S(2)}, u32[]{:S(2)}) collective-permute-start(f32[64,512]{1,0:T(8,128)S(1)} %add.6.low_a), channel_id=1, source_target_pairs={{0,16},{8,24},{16,0},{24,8},{1,17},{9,25},{17,1},{25,9},{2,18},{10... | collective-permute-start | bytes 393224 | tf_op jit(solution)/shard_map/ppermute | solution.py:20
  35.4 12.3 %collective-permute-start.21 = (f32[64,512]{1,0:T(8,128)S(1)}, f32[64,512]{1,0:T(8,128)S(1)}, u32[]{:S(2)}, u32[]{:S(2)}) collective-permute-start(f32[64,512]{1,0:T(8,128)S(1)} %add.7.high_a), channel_id=1, source_target_pairs={{0,8},{8,0},{16,24},{24,16},{1,9},{9,1},{17,25},{25,17},{2,10},{10... | collective-permute-start | bytes 393224 | tf_op jit(solution)/shard_map/ppermute | solution.py:20
  44.0 3.7 %copy-start.3 = (f32[128,512]{1,0:T(8,128)S(1)}, f32[128,512]{1,0:T(8,128)}, u32[]{:S(2)}) copy-start(f32[128,512]{1,0:T(8,128)} %acc_ref.3) | copy-start | bytes 786436
  44.0 6.4 %collective-permute-start.14 = (f32[64,512]{1,0:T(8,128)S(1)}, f32[64,512]{1,0:T(8,128)S(1)}, u32[]{:S(2)}, u32[]{:S(2)}) collective-permute-start(f32[64,512]{1,0:T(8,128)S(1)} %get-tuple-element.52), channel_id=1, source_target_pairs={{0,1},{1,0},{2,3},{3,2},{4,5},{5,4},{6,7},{7,6},{8,9},{9,8},{10,11... | collective-permute-start | bytes 393224 | tf_op jit(solution)/shard_map/ppermute | solution.py:20
  44.1 6.3 %copy-start.1 = (f32[128,512]{1,0:T(8,128)S(1)}, f32[128,512]{1,0:T(8,128)}, u32[]{:S(2)}) copy-start(f32[128,512]{1,0:T(8,128)} %entity_ref.3) | copy-start | bytes 786436
  44.1 6.3 %copy-start.4 = (f32[128,512]{1,0:T(8,128)S(1)}, f32[128,512]{1,0:T(8,128)}, u32[]{:S(2)}) copy-start(f32[128,512]{1,0:T(8,128)} %acc_ref.2) | copy-start | bytes 786436
  44.1 4.5 %collective-permute-start.15 = (f32[32,512]{1,0:T(8,128)S(1)}, f32[32,512]{1,0:T(8,128)S(1)}, u32[]{:S(2)}, u32[]{:S(2)}) collective-permute-start(f32[32,512]{1,0:T(8,128)S(1)} %get-tuple-element.53.refs_0_), channel_id=1, source_target_pairs={{0,8},{8,0},{16,24},{24,16},{1,9},{9,1},{17,25},{25,17},{2,10},{10... | collective-permute-start | bytes 196616 | tf_op jit(solution)/shard_map/ppermute | solution.py:20
  44.7 5.0 %collective-permute-start.16 = (f32[32,512]{1,0:T(8,128)S(1)}, f32[32,512]{1,0:T(8,128)S(1)}, u32[]{:S(2)}, u32[]{:S(2)}) collective-permute-start(f32[32,512]{1,0:T(8,128)S(1)} %get-tuple-element.53.refs_0_), channel_id=1, source_target_pairs={{0,16},{8,24},{16,0},{24,8},{1,17},{9,25},{17,1},{25,9},{2,18},{10... | collective-permute-start | bytes 196616 | tf_op jit(solution)/shard_map/ppermute | solution.py:20
  45.3 5.2 %collective-permute-start.17 = (f32[32,512]{1,0:T(8,128)S(1)}, f32[32,512]{1,0:T(8,128)S(1)}, u32[]{:S(2)}, u32[]{:S(2)}) collective-permute-start(f32[32,512]{1,0:T(8,128)S(1)} %get-tuple-element.53.refs_0_), channel_id=1, source_target_pairs={{0,24},{8,16},{16,8},{24,0},{1,25},{9,17},{17,9},{25,1},{2,26},{10... | collective-permute-start | bytes 196616 | tf_op jit(solution)/shard_map/ppermute | solution.py:20
  47.7 2.7 %copy-start.6 = (s32[1,8,16]{2,1,0:T(8,128)S(1)}, s32[1,8,16]{2,1,0:T(8,128)}, u32[]{:S(2)}) copy-start(s32[1,8,16]{2,1,0:T(8,128)} %send_ref.3) | copy-start | bytes 1540
  47.7 2.7 %copy-start.7 = (s32[8,32]{1,0:T(8,128)S(1)}, s32[8,32]{1,0:T(8,128)}, u32[]{:S(2)}) copy-start(s32[8,32]{1,0:T(8,128)} %neg_ref.3) | copy-start | bytes 3076

commit v4 on v3

--- a/solution.py
+++ b/solution.py
@@ -20,16 +20,16 @@
     return lax.ppermute(block, axis, [(i, i ^ step) for i in range(size)])
 
 
-def call(body, outs, specs, args, flops=0, scratch=(), limit=40, out_space=None):
+def call(body, outs, specs, args, flops=0, scratch=(), limit=40 * 1024):
     shapes = [jax.ShapeDtypeStruct(shape, jnp.float32) for shape in outs]
     moved = 4 * sum(int(a.size) for a in args) + 4 * sum(int(s.size) for s in shapes)
     return pl.pallas_call(
         body,
         out_shape=shapes,
         in_specs=specs,
-        out_specs=[out_space or VMEM] * len(shapes),
+        out_specs=[VMEM] * len(shapes),
         scratch_shapes=scratch,
-        compiler_params=pltpu.CompilerParams(vmem_limit_bytes=limit * 1024 * 1024),
+        compiler_params=pltpu.CompilerParams(vmem_limit_bytes=limit * 1024),
         cost_estimate=pl.CostEstimate(flops=flops, bytes_accessed=moved, transcendentals=0),
     )(*args)
 
@@ -87,10 +87,8 @@
     return jnp.concatenate(parts, axis=-1)
 
 
-def gather_kernel(order, send_ref, neg_ref, entity_ref, negs_out, *refs):
-    count = len(order)
-    outs, (negs, *parcels) = refs[:count], refs[count : 2 * count + 1]
-    rows, sends, picks, sems = refs[2 * count + 1 :]
+def gather_kernel(send_ref, neg_ref, entity_ref, negs, *refs):
+    *parcels, rows, sends, picks, sems = refs
     copies = [
         pltpu.make_async_copy(source, target, sems.at[i])
         for i, (source, target) in enumerate(
@@ -105,17 +103,11 @@
     slots = send_ref.shape[2]
     for i in range(neg_ref.shape[1]):
         negs[pl.ds(i, 1), :] = rows[pl.ds(picks[rel_here, i], 1), :]
-    copies = [pltpu.make_async_copy(negs, negs_out, sems.at[3])]
-    copies[0].start()
-    for s in order:
+    for s, ref in enumerate(parcels):
         for core in range(2):
             peer = (2 * s + core) ^ rel_here
             for t in range(slots):
-                parcels[s][pl.ds(core * slots + t, 1), :] = rows[pl.ds(sends[0, peer, t], 1), :]
-        copies.append(pltpu.make_async_copy(parcels[s], outs[s], sems.at[4 + s]))
-        copies[-1].start()
-    for copy in copies:
-        copy.wait()
+                ref[pl.ds(core * slots + t, 1), :] = rows[pl.ds(sends[0, peer, t], 1), :]
 
 
 def unit_parts(rows):
@@ -162,11 +154,19 @@
     query_ref[...], head_out[...], tail_out[...] = query, head, tail
     q_high, q_low = halves(query)
     n_high, n_low = halves(negs)
-    scores = dot(q_high, n_high, COLS) + dot(q_high, n_low, COLS) + dot(q_low, n_high, COLS)
+    scores = dot(
+        jnp.concatenate([n_high, n_low, n_high], axis=1),
+        jnp.concatenate([q_high, q_high, q_low], axis=1),
+        COLS,
+    )
     push = jax.nn.sigmoid(scores) * (1.0 / negs.shape[0])
     push_ref[...] = push
     p_high, p_low = halves(push)
-    grad = dot(p_high, q_high, LEFT) + dot(p_low, q_high, LEFT) + dot(p_high, q_low, LEFT)
+    grad = dot(
+        jnp.concatenate([p_high, p_low, p_high], axis=1),
+        jnp.concatenate([q_high, q_high, q_low], axis=0),
+        ROWS,
+    )
     middle = mine_ref.shape[0]
     mine_ref[...] = grad[:middle]
     theirs_ref[...] = grad[middle:]
@@ -178,7 +178,7 @@
     negs = jnp.concatenate([stacked[:half], swapped[:half]], axis=0)
     p_high, p_low = halves(push_ref[...])
     n_high, n_low = halves(negs)
-    pulled = dot(p_high, n_high, ROWS) + dot(p_low, n_high, ROWS) + dot(p_high, n_low, ROWS)
+    pulled = dot(p_high, n_high, LEFT) + dot(p_low, n_high, LEFT) + dot(p_high, n_low, LEFT)
     pull = pull_ref[:, :1]
     grad_query = quarters(pulled + pull * tail_rows[...])
     grad_head = join(hamilton(grad_query, conjugate(quarters(rot_ref[...]))))
@@ -285,19 +285,16 @@
 
     order = [*range(2, n_chip), *range(min(n_chip, 2))]
     own_negs, *parcels = call(
-        functools.partial(gather_kernel, order),
+        gather_kernel,
         [(n_neg, width)] + [(2 * slots, width)] * n_chip,
         [HBM, HBM, HBM],
         (send_rows, neg_rows, entity),
-        limit=60,
-        out_space=HBM,
-        scratch=[pltpu.VMEM((n_neg, width), jnp.float32)]
-        + [pltpu.VMEM((2 * slots, width), jnp.float32)] * n_chip
-        + [
+        limit=60 * 1024,
+        scratch=[
             pltpu.VMEM(entity.shape, jnp.float32),
             pltpu.SMEM(send_rows.shape, jnp.int32),
             pltpu.SMEM(neg_rows.shape, jnp.int32),
-            pltpu.SemaphoreType.DMA((4 + n_chip,)),
+            pltpu.SemaphoreType.DMA((3,)),
         ],
     )
     spread = [own_negs] + [exchange(own_negs, "dom", n_dom, s) for s in range(1, n_dom)]
@@ -320,7 +317,7 @@
 
     mine, theirs, *saved = call(
         functools.partial(scores_kernel, slots, n_chip),
-        [(n_chip * n_neg, width)] * 2 + [(trips, width)] * 3 + [(trips, 128), (trips, n_rel * n_neg)],
+        [(n_chip * n_neg, width)] * 2 + [(trips, width)] * 3 + [(trips, 128), (n_rel * n_neg, trips)],
         [VMEM] * (5 + n_chip),
         (trip_head, trip_tail, rot, *arrived, stacked, swapped),
     )
@@ -347,11 +344,12 @@
         first = first or ([sums[0][0], sums[1][0]] if len(bits) > 1 and up != bits[0] else [])
         sums[0].append(exchange(sums[0][0], "dom", n_dom, up))
         sums[1].append(exchange(sums[1][0], "dom", n_dom, down))
+    back_order = [*range(2, n_chip, 2), *range(min(n_chip, 2))[::-1], *range(3, n_chip, 2)]
     neg_share, stay, cross = call(
-        functools.partial(unpack_kernel, slots, order),
+        functools.partial(unpack_kernel, slots, back_order),
         [(n_neg, width)] + [(n_chip * slots, width)] * 2,
         [VMEM] * n_chip,
-        [back[s] for s in order],
+        [back[s] for s in back_order],
     )
     neg_shares = [neg_share] + [exchange(neg_share, "dom", n_dom, s) for s in range(1, n_dom)]
     cross = exchange(cross, "rel", n_rel, 1)

time: 51.8 us -> 51.2 us (0.988)
  waiting for transfers between devices: 16.2 us -> 15.6 us
    ppermute x22, waiting for transfers between devices: 16.2 us -> 15.6 us  [exchange(): return lax.ppermute(block, axis, [(i, i ^ step) for i in range(size)])]
  transfers between devices with their start and end apart: 22 -> 22, of which waited for: 9 -> 8; matrix products, arithmetic and copies ran while one was open for 0% -> 0% of each run, Pallas kernels for 4% -> 5%
where the time goes in v4:
time: 51.2 us; the launch traced here: 51 us
  starting transfers between devices  26.2 us (51%)
  waiting for transfers between devices  15.6 us (30%)
  Pallas kernels  6.98 us (14%)
  between operations  1.51 us (3%)
  local copies, waits for them, and re-layouts  0.6 us (1%)
    ppermute x22, starting transfers between devices, exchange(): return lax.ppermute(block, axis, [(i, i ^ step) for i in range(size)])  26.2 us
    ppermute x22, waiting for transfers between devices, exchange(): return lax.ppermute(block, axis, [(i, i ^ step) for i in range(size)])  15.6 us
    pallas_call x10, Pallas kernels, call(): pl.pallas_call(body, out_shape=shapes, in_specs=specs, out_specs=[VMEM] *...  6.98 us
  transfers between devices with their start and end apart: 22, of which 8 were waited for; matrix products, arithmetic and copies ran while one was open for 0% of the time, Pallas kernels for 5%

profile of v4, /device:TPU:0, one launch (start us, length us, event | category | flops | bytes accessed | tf_op | source)
XLA Modules:
  0.0 51.0 jit_solution(2417573453294240217)
XLA Ops:
  0.6 2.0 %shard_map.130 = (f32[32,512]{1,0:T(8,128)}, f32[32,512]{1,0:T(8,128)}, f32[32,512]{1,0:T(8,128)}, f32[32,512]{1,0:T(8,128)}, f32[32,512]{1,0:T(8,128)}) custom-call(s32[1,8,16]{2,1,0:T(8,128)} %send_ref.3, s32[8,32]{1,0:T(8,128)} %neg_ref.3, f32[128,512]{1,0:T(8,128)} %entity_ref.3), custom_call_target="tpu_custom_call" | custom-call | bytes 591360 | tf_op jit(solution)/shard_map/pallas_call | solution.py:26
  2.7 3.0 %collective-permute-start.3 = (f32[32,512]{1,0:T(8,128)}, f32[32,512]{1,0:T(8,128)S(1)}, u32[]{:S(2)}, u32[]{:S(2)}) collective-permute-start(f32[32,512]{1,0:T(8,128)} %get-tuple-element.36.refs_0_), channel_id=1, source_target_pairs={{0,8},{8,0},{16,24},{24,16},{1,9},{9,1},{17,25},{25,17},{2,10},{10... | collective-permute-start | bytes 196616 | tf_op jit(solution)/shard_map/ppermute | solution.py:20
  5.7 1.5 %collective-permute-start.4 = (f32[32,512]{1,0:T(8,128)}, f32[32,512]{1,0:T(8,128)S(1)}, u32[]{:S(2)}, u32[]{:S(2)}) collective-permute-start(f32[32,512]{1,0:T(8,128)} %get-tuple-element.36.refs_0_), channel_id=1, source_target_pairs={{0,16},{8,24},{16,0},{24,8},{1,17},{9,25},{17,1},{25,9},{2,18},{10... | collective-permute-start | bytes 196616 | tf_op jit(solution)/shard_map/ppermute | solution.py:20
  7.2 0.0 collective-permute-start.5
  7.2 2.0 %collective-permute-start = (f32[32,512]{1,0:T(8,128)}, f32[32,512]{1,0:T(8,128)S(1)}, u32[]{:S(2)}, u32[]{:S(2)}) collective-permute-start(f32[32,512]{1,0:T(8,128)} %get-tuple-element.33), channel_id=1, source_target_pairs={{0,2},{1,3},{2,0},{3,1},{4,6},{5,7},{6,4},{7,5},{8,10},{9,11},{10,... | collective-permute-start | bytes 196616 | tf_op jit(solution)/shard_map/ppermute | solution.py:20
  9.3 2.6 %collective-permute-start.1 = (f32[32,512]{1,0:T(8,128)}, f32[32,512]{1,0:T(8,128)S(1)}, u32[]{:S(2)}, u32[]{:S(2)}) collective-permute-start(f32[32,512]{1,0:T(8,128)} %get-tuple-element.34), channel_id=1, source_target_pairs={{0,4},{1,5},{2,6},{3,7},{4,0},{5,1},{6,2},{7,3},{8,12},{9,13},{10,... | collective-permute-start | bytes 196616 | tf_op jit(solution)/shard_map/ppermute | solution.py:20
  12.5 0.0 copy-start.5
  12.6 0.3 shard_map.129.after_ref.rot_ref
  12.8 0.5 %copy-done.11 = f32[32,512]{1,0:T(8,128)S(1)} copy-done((f32[32,512]{1,0:T(8,128)S(1)}, f32[32,512]{1,0:T(8,128)}, u32[]{:S(2)}) %copy-start.11) | copy-done | bytes 65560
  13.4 0.0 collective-permute-start.2
  13.4 0.0 collective-permute-done.4.refs_2_
  13.4 0.0 copy-done.5
  13.4 2.0 %collective-permute-start.6 = (f32[32,512]{1,0:T(8,128)S(1)}, f32[32,512]{1,0:T(8,128)S(1)}, u32[]{:S(2)}, u32[]{:S(2)}) collective-permute-start(f32[32,512]{1,0:T(8,128)S(1)} %shard_map.131.refs_6_), channel_id=1, source_target_pairs={{0,4},{1,5},{2,6},{3,7},{4,0},{5,1},{6,2},{7,3},{8,12},{9,13},{10,... | collective-permute-start | bytes 196616 | tf_op jit(solution)/shard_map/ppermute | solution.py:20
  15.4 2.0 %collective-permute-start.7 = (f32[32,512]{1,0:T(8,128)S(1)}, f32[32,512]{1,0:T(8,128)S(1)}, u32[]{:S(2)}, u32[]{:S(2)}) collective-permute-start(f32[32,512]{1,0:T(8,128)S(1)} %shard_map.131.refs_6_), channel_id=1, source_target_pairs={{0,6},{1,7},{2,4},{3,5},{4,2},{5,3},{6,0},{7,1},{8,14},{9,15},{10,... | collective-permute-start | bytes 196616 | tf_op jit(solution)/shard_map/ppermute | solution.py:20
  17.4 0.5 collective-permute-start.8
  17.9 0.0 collective-permute-done.1.refs_0_.refs_2_
  17.9 2.0 %collective-permute-done.2.refs_1_.refs_3_ = f32[32,512]{1,0:T(8,128)S(1)} collective-permute-done((f32[32,512]{1,0:T(8,128)S(1)}, f32[32,512]{1,0:T(8,128)S(1)}, u32[]{:S(2)}, u32[]{:S(2)}) %collective-permute-start.2) | collective-permute-done | bytes 65568 | tf_op jit(solution)/shard_map/ppermute | solution.py:20
  19.9 3.2 %collective-permute-done.6.refs_4_ = f32[32,512]{1,0:T(8,128)S(1)} collective-permute-done((f32[32,512]{1,0:T(8,128)S(1)}, f32[32,512]{1,0:T(8,128)S(1)}, u32[]{:S(2)}, u32[]{:S(2)}) %collective-permute-start.6) | collective-permute-done | bytes 65568 | tf_op jit(solution)/shard_map/ppermute | solution.py:20
  23.1 0.0 collective-permute-done.7.refs_5_
  23.1 0.0 copy-start.8
  23.1 0.0 copy-start.9
  23.1 0.1 collective-permute-start.9
  23.2 1.7 %collective-permute-done.9.refs_5_.refs_1_ = f32[192,512]{1,0:T(8,128)S(1)} collective-permute-done((f32[192,512]{1,0:T(8,128)S(1)}, f32[192,512]{1,0:T(8,128)S(1)}, u32[]{:S(2)}, u32[]{:S(2)}) %collective-permute-start.9) | collective-permute-done | bytes 393248 | tf_op jit(solution)/shard_map/ppermute | solution.py:20
  24.9 1.4 %shard_map.133 = (f32[128,512]{1,0:T(8,128)S(1)}, f32[128,512]{1,0:T(8,128)S(1)}, f32[256,512]{1,0:T(8,128)S(1)}, f32[256,512]{1,0:T(8,128)S(1)}, f32[256,512]{1...) custom-call(s32[256]{0:T(256)S(1)} %copy-done.8, s32[256]{0:T(256)S(1)} %copy-done.9, ...), custom_call_target="tpu_custom_call" | custom-call | bytes 4065280 | tf_op jit(solution)/shard_map/pallas_call | solution.py:26
  26.3 0.2 collective-permute-start.10
  26.5 1.1 %shard_map.134 = (f32[64,512]{1,0:T(8,128)S(1)}, f32[64,512]{1,0:T(8,128)S(1)}, f32[128,512]{1,0:T(8,128)S(1)}) custom-call(s32[256]{0:T(256)S(1)} %copy-done.8, s32[256]{0:T(256)S(1)} %copy-done.10, s32[256]{0:T(256)S(1)} %copy-done.9, f32[128,512]{1,0:T(8,128)S(1)} %copy-done, f32[256,512]{1,0:T(8,128)S(1)} %shard_map.129.after_ref.rot_ref, ...), custom_call_target="tpu_custom_call" | custom-call | bytes 4066304 | tf_op jit(solution)/shard_map/pallas_call | solution.py:26
  27.7 0.3 collective-permute-done.10.theirs
  27.9 0.1 shard_map.135
  28.0 1.6 %collective-permute-start.18 = (f32[64,512]{1,0:T(8,128)S(1)}, f32[64,512]{1,0:T(8,128)S(1)}, u32[]{:S(2)}, u32[]{:S(2)}) collective-permute-start(f32[64,512]{1,0:T(8,128)S(1)} %get-tuple-element.56), channel_id=1, source_target_pairs={{0,8},{8,0},{16,24},{24,16},{1,9},{9,1},{17,25},{25,17},{2,10},{10... | collective-permute-start | bytes 393224 | tf_op jit(solution)/shard_map/ppermute | solution.py:20
  29.6 1.5 %collective-permute-start.20 = (f32[64,512]{1,0:T(8,128)S(1)}, f32[64,512]{1,0:T(8,128)S(1)}, u32[]{:S(2)}, u32[]{:S(2)}) collective-permute-start(f32[64,512]{1,0:T(8,128)S(1)} %get-tuple-element.57), channel_id=1, source_target_pairs={{0,16},{8,24},{16,0},{24,8},{1,17},{9,25},{17,1},{25,9},{2,18},{10... | collective-permute-start | bytes 393224 | tf_op jit(solution)/shard_map/ppermute | solution.py:20
  31.1 2.0 %collective-permute-start.11 = (f32[64,512]{1,0:T(8,128)S(1)}, f32[64,512]{1,0:T(8,128)S(1)}, u32[]{:S(2)}, u32[]{:S(2)}) collective-permute-start(f32[64,512]{1,0:T(8,128)S(1)} %get-tuple-element.47), channel_id=1, source_target_pairs={{0,4},{1,5},{2,6},{3,7},{4,0},{5,1},{6,2},{7,3},{8,12},{9,13},{10,... | collective-permute-start | bytes 393224 | tf_op jit(solution)/shard_map/ppermute | solution.py:20
  33.1 0.8 %collective-permute-start.12 = (f32[64,512]{1,0:T(8,128)S(1)}, f32[64,512]{1,0:T(8,128)S(1)}, u32[]{:S(2)}, u32[]{:S(2)}) collective-permute-start(f32[64,512]{1,0:T(8,128)S(1)} %get-tuple-element.48), channel_id=1, source_target_pairs={{0,2},{1,3},{2,0},{3,1},{4,6},{5,7},{6,4},{7,5},{8,10},{9,11},{10,... | collective-permute-start | bytes 393224 | tf_op jit(solution)/shard_map/ppermute | solution.py:20
  33.8 1.7 %collective-permute-start.13 = (f32[64,512]{1,0:T(8,128)S(1)}, f32[64,512]{1,0:T(8,128)S(1)}, u32[]{:S(2)}, u32[]{:S(2)}) collective-permute-start(f32[64,512]{1,0:T(8,128)S(1)} %get-tuple-element.50), channel_id=1, source_target_pairs={{0,6},{1,7},{2,4},{3,5},{4,2},{5,3},{6,0},{7,1},{8,14},{9,15},{10,... | collective-permute-start | bytes 393224 | tf_op jit(solution)/shard_map/ppermute | solution.py:20
  35.5 0.0 collective-permute-done.18
  35.5 0.6 %collective-permute-start.19 = (f32[64,512]{1,0:T(8,128)S(1)}, f32[64,512]{1,0:T(8,128)S(1)}, u32[]{:S(2)}, u32[]{:S(2)}) collective-permute-start(f32[64,512]{1,0:T(8,128)S(1)} %add.6.low_a), channel_id=1, source_target_pairs={{0,16},{8,24},{16,0},{24,8},{1,17},{9,25},{17,1},{25,9},{2,18},{10... | collective-permute-start | bytes 393224 | tf_op jit(solution)/shard_map/ppermute | solution.py:20
  36.1 0.7 %collective-permute-start.21 = (f32[64,512]{1,0:T(8,128)S(1)}, f32[64,512]{1,0:T(8,128)S(1)}, u32[]{:S(2)}, u32[]{:S(2)}) collective-permute-start(f32[64,512]{1,0:T(8,128)S(1)} %add.7.high_a), channel_id=1, source_target_pairs={{0,8},{8,0},{16,24},{24,16},{1,9},{9,1},{17,25},{25,17},{2,10},{10... | collective-permute-start | bytes 393224 | tf_op jit(solution)/shard_map/ppermute | solution.py:20
  36.8 6.6 %collective-permute-done.11.refs_0_ = f32[64,512]{1,0:T(8,128)S(1)} collective-permute-done((f32[64,512]{1,0:T(8,128)S(1)}, f32[64,512]{1,0:T(8,128)S(1)}, u32[]{:S(2)}, u32[]{:S(2)}) %collective-permute-start.11) | collective-permute-done | bytes 131104 | tf_op jit(solution)/shard_map/ppermute | solution.py:20
  43.5 0.1 collective-permute-start.14
  43.6 0.0 copy-start.1
  43.6 0.0 copy-start.4
  43.6 0.6 %collective-permute-start.15 = (f32[32,512]{1,0:T(8,128)S(1)}, f32[32,512]{1,0:T(8,128)S(1)}, u32[]{:S(2)}, u32[]{:S(2)}) collective-permute-start(f32[32,512]{1,0:T(8,128)S(1)} %get-tuple-element.53.refs_0_), channel_id=1, source_target_pairs={{0,8},{8,0},{16,24},{24,16},{1,9},{9,1},{17,25},{25,17},{2,10},{10... | collective-permute-start | bytes 196616 | tf_op jit(solution)/shard_map/ppermute | solution.py:20
  44.2 0.5 collective-permute-start.16
  44.7 2.4 %collective-permute-start.17 = (f32[32,512]{1,0:T(8,128)S(1)}, f32[32,512]{1,0:T(8,128)S(1)}, u32[]{:S(2)}, u32[]{:S(2)}) collective-permute-start(f32[32,512]{1,0:T(8,128)S(1)} %get-tuple-element.53.refs_0_), channel_id=1, source_target_pairs={{0,24},{8,16},{16,8},{24,0},{1,25},{9,17},{17,9},{25,1},{2,26},{10... | collective-permute-start | bytes 196616 | tf_op jit(solution)/shard_map/ppermute | solution.py:20
  47.2 0.9 %shard_map.138 = (f32[128,512]{1,0:T(8,128)}, f32[128,512]{1,0:T(8,128)}) custom-call(f32[64,512]{1,0:T(8,128)S(1)} %add.6.low_a, f32[64,512]{1,0:T(8,128)S(1)} %collective-permute-done.19.low_b, f32[64,512]{1,0:T(8,128)S(1)} %add.7.high_a, f32[64,512]{1,0:T(8,128)S(1)} %collective-permute-done.21.high_b, f32[128,512]{1,0:T(8,128)S(1)} %copy-done, ...), custom_call_target="tpu_custom_call" | custom-call | bytes 1572864 | tf_op jit(solution)/shard_map/pallas_call | solution.py:26
  48.0 0.1 collective-permute-done.15.refs_1_
  48.1 1.1 %collective-permute-done.16.refs_2_ = f32[32,512]{1,0:T(8,128)S(1)} collective-permute-done((f32[32,512]{1,0:T(8,128)S(1)}, f32[32,512]{1,0:T(8,128)S(1)}, u32[]{:S(2)}, u32[]{:S(2)}) %collective-permute-start.16) | collective-permute-done | bytes 65568 | tf_op jit(solution)/shard_map/ppermute | solution.py:20
  49.2 0.7 %collective-permute-done.17.refs_3_ = f32[32,512]{1,0:T(8,128)S(1)} collective-permute-done((f32[32,512]{1,0:T(8,128)S(1)}, f32[32,512]{1,0:T(8,128)S(1)}, u32[]{:S(2)}, u32[]{:S(2)}) %collective-permute-start.17) | collective-permute-done | bytes 65568 | tf_op jit(solution)/shard_map/ppermute | solution.py:20
  49.9 1.1 %shard_map.137 = (f32[128,512]{1,0:T(8,128)}, f32[128,512]{1,0:T(8,128)}) custom-call(s32[1]{0:T(128)S(6)} %copy.14.part_ref, s32[1,8,16]{2,1,0:T(8,128)S(1)} %copy-done.6, s32[8,32]{1,0:T(8,128)S(1)} %copy-done.7, f32[128,512]{1,0:T(8,128)S(1)} %copy-done.1, f32[128,512]{1,0:T(8,128)S(1)} %copy-done.4, f32[64,512]{1,0:T(8,128)S(1)} %get-tuple-element.51.stay_ref, ...), custom_call_target="tpu_custom_call" | custom-call | bytes 1574404 | tf_op jit(solution)/shard_map/pallas_call | solution.py:26
  (32 shorter events, 0.2 us)
Async XLA Ops:
  0.6 11.9 %copy-start = (f32[128,512]{1,0:T(8,128)S(1)}, f32[128,512]{1,0:T(8,128)}, u32[]{:S(2)}) copy-start(f32[128,512]{1,0:T(8,128)} %relation_ref.5) | copy-start | bytes 786436
  2.7 10.1 %collective-permute-start.3 = (f32[32,512]{1,0:T(8,128)}, f32[32,512]{1,0:T(8,128)S(1)}, u32[]{:S(2)}, u32[]{:S(2)}) collective-permute-start(f32[32,512]{1,0:T(8,128)} %get-tuple-element.36.refs_0_), channel_id=1, source_target_pairs={{0,8},{8,0},{16,24},{24,16},{1,9},{9,1},{17,25},{25,17},{2,10},{10... | collective-permute-start | bytes 196616 | tf_op jit(solution)/shard_map/ppermute | solution.py:20
  5.7 7.7 %collective-permute-start.4 = (f32[32,512]{1,0:T(8,128)}, f32[32,512]{1,0:T(8,128)S(1)}, u32[]{:S(2)}, u32[]{:S(2)}) collective-permute-start(f32[32,512]{1,0:T(8,128)} %get-tuple-element.36.refs_0_), channel_id=1, source_target_pairs={{0,16},{8,24},{16,0},{24,8},{1,17},{9,25},{17,1},{25,9},{2,18},{10... | collective-permute-start | bytes 196616 | tf_op jit(solution)/shard_map/ppermute | solution.py:20
  7.2 6.2 %collective-permute-start.5 = (f32[32,512]{1,0:T(8,128)}, f32[32,512]{1,0:T(8,128)S(1)}, u32[]{:S(2)}, u32[]{:S(2)}) collective-permute-start(f32[32,512]{1,0:T(8,128)} %get-tuple-element.36.refs_0_), channel_id=1, source_target_pairs={{0,24},{8,16},{16,8},{24,0},{1,25},{9,17},{17,9},{25,1},{2,26},{10... | collective-permute-start | bytes 196616 | tf_op jit(solution)/shard_map/ppermute | solution.py:20
  7.2 10.2 %collective-permute-start = (f32[32,512]{1,0:T(8,128)}, f32[32,512]{1,0:T(8,128)S(1)}, u32[]{:S(2)}, u32[]{:S(2)}) collective-permute-start(f32[32,512]{1,0:T(8,128)} %get-tuple-element.33), channel_id=1, source_target_pairs={{0,2},{1,3},{2,0},{3,1},{4,6},{5,7},{6,4},{7,5},{8,10},{9,11},{10,... | collective-permute-start | bytes 196616 | tf_op jit(solution)/shard_map/ppermute | solution.py:20
  9.3 3.3 %copy-start.10 = (s32[256]{0:T(256)S(1)}, s32[256]{0:T(256)}, u32[]{:S(2)}) copy-start(s32[256]{0:T(256)} %rel_index_ref.3) | copy-start | bytes 3076
  9.3 8.6 %collective-permute-start.1 = (f32[32,512]{1,0:T(8,128)}, f32[32,512]{1,0:T(8,128)S(1)}, u32[]{:S(2)}, u32[]{:S(2)}) collective-permute-start(f32[32,512]{1,0:T(8,128)} %get-tuple-element.34), channel_id=1, source_target_pairs={{0,4},{1,5},{2,6},{3,7},{4,0},{5,1},{6,2},{7,3},{8,12},{9,13},{10,... | collective-permute-start | bytes 196616 | tf_op jit(solution)/shard_map/ppermute | solution.py:20
  12.5 0.8 %copy-start.11 = (f32[32,512]{1,0:T(8,128)S(1)}, f32[32,512]{1,0:T(8,128)}, u32[]{:S(2)}) copy-start(f32[32,512]{1,0:T(8,128)} %get-tuple-element.35) | copy-start | bytes 196612
  12.5 0.9 %copy-start.5 = (f32[32,512]{1,0:T(8,128)S(1)}, f32[32,512]{1,0:T(8,128)}, u32[]{:S(2)}) copy-start(f32[32,512]{1,0:T(8,128)} %get-tuple-element.36.refs_0_) | copy-start | bytes 196612
  13.4 9.7 %copy-start.2 = (f32[32,512]{1,0:T(8,128)S(1)}, f32[32,512]{1,0:T(8,128)}, u32[]{:S(2)}) copy-start(f32[32,512]{1,0:T(8,128)} %get-tuple-element.32.refs_2_.refs_0_) | copy-start | bytes 196612
  13.4 6.5 %collective-permute-start.2 = (f32[32,512]{1,0:T(8,128)S(1)}, f32[32,512]{1,0:T(8,128)S(1)}, u32[]{:S(2)}, u32[]{:S(2)}) collective-permute-start(f32[32,512]{1,0:T(8,128)S(1)} %copy-done.11), channel_id=1, source_target_pairs={{0,6},{1,7},{2,4},{3,5},{4,2},{5,3},{6,0},{7,1},{8,14},{9,15},{10,... | collective-permute-start | bytes 196616 | tf_op jit(solution)/shard_map/ppermute | solution.py:20
  13.4 9.6 %collective-permute-start.6 = (f32[32,512]{1,0:T(8,128)S(1)}, f32[32,512]{1,0:T(8,128)S(1)}, u32[]{:S(2)}, u32[]{:S(2)}) collective-permute-start(f32[32,512]{1,0:T(8,128)S(1)} %shard_map.131.refs_6_), channel_id=1, source_target_pairs={{0,4},{1,5},{2,6},{3,7},{4,0},{5,1},{6,2},{7,3},{8,12},{9,13},{10,... | collective-permute-start | bytes 196616 | tf_op jit(solution)/shard_map/ppermute | solution.py:20
  15.4 7.7 %collective-permute-start.7 = (f32[32,512]{1,0:T(8,128)S(1)}, f32[32,512]{1,0:T(8,128)S(1)}, u32[]{:S(2)}, u32[]{:S(2)}) collective-permute-start(f32[32,512]{1,0:T(8,128)S(1)} %shard_map.131.refs_6_), channel_id=1, source_target_pairs={{0,6},{1,7},{2,4},{3,5},{4,2},{5,3},{6,0},{7,1},{8,14},{9,15},{10,... | collective-permute-start | bytes 196616 | tf_op jit(solution)/shard_map/ppermute | solution.py:20
  17.4 5.7 %collective-permute-start.8 = (f32[32,512]{1,0:T(8,128)S(1)}, f32[32,512]{1,0:T(8,128)S(1)}, u32[]{:S(2)}, u32[]{:S(2)}) collective-permute-start(f32[32,512]{1,0:T(8,128)S(1)} %shard_map.131.refs_6_), channel_id=1, source_target_pairs={{0,2},{1,3},{2,0},{3,1},{4,6},{5,7},{6,4},{7,5},{8,10},{9,11},{10,... | collective-permute-start | bytes 196616 | tf_op jit(solution)/shard_map/ppermute | solution.py:20
  23.1 1.9 %copy-start.8 = (s32[256]{0:T(256)S(1)}, s32[256]{0:T(256)}, u32[]{:S(2)}) copy-start(s32[256]{0:T(256)} %head_ref.3) | copy-start | bytes 3076
  23.1 1.8 %copy-start.9 = (s32[256]{0:T(256)S(1)}, s32[256]{0:T(256)}, u32[]{:S(2)}) copy-start(s32[256]{0:T(256)} %tail_ref.3) | copy-start | bytes 3076
  23.1 1.8 %collective-permute-start.9 = (f32[192,512]{1,0:T(8,128)S(1)}, f32[192,512]{1,0:T(8,128)S(1)}, u32[]{:S(2)}, u32[]{:S(2)}) collective-permute-start(f32[192,512]{1,0:T(8,128)S(1)} %shard_map.132.refs_4_.refs_0_), channel_id=1, source_target_pairs={{0,1},{1,0},{2,3},{3,2},{4,5},{5,4},{6,7},{7,6},{8,9},{9,8},{10,11... | collective-permute-start | bytes 1179656 | tf_op jit(solution)/shard_map/ppermute | solution.py:20
  26.3 1.6 %collective-permute-start.10 = (f32[128,512]{1,0:T(8,128)S(1)}, f32[128,512]{1,0:T(8,128)S(1)}, u32[]{:S(2)}, u32[]{:S(2)}) collective-permute-start(f32[128,512]{1,0:T(8,128)S(1)} %get-tuple-element.38), channel_id=1, source_target_pairs={{0,1},{1,0},{2,3},{3,2},{4,5},{5,4},{6,7},{7,6},{8,9},{9,8},{10,11... | collective-permute-start | bytes 786440 | tf_op jit(solution)/shard_map/ppermute | solution.py:20
  28.0 7.5 %collective-permute-start.18 = (f32[64,512]{1,0:T(8,128)S(1)}, f32[64,512]{1,0:T(8,128)S(1)}, u32[]{:S(2)}, u32[]{:S(2)}) collective-permute-start(f32[64,512]{1,0:T(8,128)S(1)} %get-tuple-element.56), channel_id=1, source_target_pairs={{0,8},{8,0},{16,24},{24,16},{1,9},{9,1},{17,25},{25,17},{2,10},{10... | collective-permute-start | bytes 393224 | tf_op jit(solution)/shard_map/ppermute | solution.py:20
  29.6 6.5 %collective-permute-start.20 = (f32[64,512]{1,0:T(8,128)S(1)}, f32[64,512]{1,0:T(8,128)S(1)}, u32[]{:S(2)}, u32[]{:S(2)}) collective-permute-start(f32[64,512]{1,0:T(8,128)S(1)} %get-tuple-element.57), channel_id=1, source_target_pairs={{0,16},{8,24},{16,0},{24,8},{1,17},{9,25},{17,1},{25,9},{2,18},{10... | collective-permute-start | bytes 393224 | tf_op jit(solution)/shard_map/ppermute | solution.py:20
  31.1 12.3 %collective-permute-start.11 = (f32[64,512]{1,0:T(8,128)S(1)}, f32[64,512]{1,0:T(8,128)S(1)}, u32[]{:S(2)}, u32[]{:S(2)}) collective-permute-start(f32[64,512]{1,0:T(8,128)S(1)} %get-tuple-element.47), channel_id=1, source_target_pairs={{0,4},{1,5},{2,6},{3,7},{4,0},{5,1},{6,2},{7,3},{8,12},{9,13},{10,... | collective-permute-start | bytes 393224 | tf_op jit(solution)/shard_map/ppermute | solution.py:20
  33.1 10.4 %collective-permute-start.12 = (f32[64,512]{1,0:T(8,128)S(1)}, f32[64,512]{1,0:T(8,128)S(1)}, u32[]{:S(2)}, u32[]{:S(2)}) collective-permute-start(f32[64,512]{1,0:T(8,128)S(1)} %get-tuple-element.48), channel_id=1, source_target_pairs={{0,2},{1,3},{2,0},{3,1},{4,6},{5,7},{6,4},{7,5},{8,10},{9,11},{10,... | collective-permute-start | bytes 393224 | tf_op jit(solution)/shard_map/ppermute | solution.py:20
  33.8 9.6 %collective-permute-start.13 = (f32[64,512]{1,0:T(8,128)S(1)}, f32[64,512]{1,0:T(8,128)S(1)}, u32[]{:S(2)}, u32[]{:S(2)}) collective-permute-start(f32[64,512]{1,0:T(8,128)S(1)} %get-tuple-element.50), channel_id=1, source_target_pairs={{0,6},{1,7},{2,4},{3,5},{4,2},{5,3},{6,0},{7,1},{8,14},{9,15},{10,... | collective-permute-start | bytes 393224 | tf_op jit(solution)/shard_map/ppermute | solution.py:20
  35.5 9.2 %collective-permute-start.19 = (f32[64,512]{1,0:T(8,128)S(1)}, f32[64,512]{1,0:T(8,128)S(1)}, u32[]{:S(2)}, u32[]{:S(2)}) collective-permute-start(f32[64,512]{1,0:T(8,128)S(1)} %add.6.low_a), channel_id=1, source_target_pairs={{0,16},{8,24},{16,0},{24,8},{1,17},{9,25},{17,1},{25,9},{2,18},{10... | collective-permute-start | bytes 393224 | tf_op jit(solution)/shard_map/ppermute | solution.py:20
  36.1 11.0 %collective-permute-start.21 = (f32[64,512]{1,0:T(8,128)S(1)}, f32[64,512]{1,0:T(8,128)S(1)}, u32[]{:S(2)}, u32[]{:S(2)}) collective-permute-start(f32[64,512]{1,0:T(8,128)S(1)} %add.7.high_a), channel_id=1, source_target_pairs={{0,8},{8,0},{16,24},{24,16},{1,9},{9,1},{17,25},{25,17},{2,10},{10... | collective-permute-start | bytes 393224 | tf_op jit(solution)/shard_map/ppermute | solution.py:20
  43.4 3.7 %copy-start.3 = (f32[128,512]{1,0:T(8,128)S(1)}, f32[128,512]{1,0:T(8,128)}, u32[]{:S(2)}) copy-start(f32[128,512]{1,0:T(8,128)} %acc_ref.3) | copy-start | bytes 786436
  43.5 6.4 %collective-permute-start.14 = (f32[64,512]{1,0:T(8,128)S(1)}, f32[64,512]{1,0:T(8,128)S(1)}, u32[]{:S(2)}, u32[]{:S(2)}) collective-permute-start(f32[64,512]{1,0:T(8,128)S(1)} %get-tuple-element.52), channel_id=1, source_target_pairs={{0,1},{1,0},{2,3},{3,2},{4,5},{5,4},{6,7},{7,6},{8,9},{9,8},{10,11... | collective-permute-start | bytes 393224 | tf_op jit(solution)/shard_map/ppermute | solution.py:20
  43.6 6.3 %copy-start.1 = (f32[128,512]{1,0:T(8,128)S(1)}, f32[128,512]{1,0:T(8,128)}, u32[]{:S(2)}) copy-start(f32[128,512]{1,0:T(8,128)} %entity_ref.3) | copy-start | bytes 786436
  43.6 6.3 %copy-start.4 = (f32[128,512]{1,0:T(8,128)S(1)}, f32[128,512]{1,0:T(8,128)}, u32[]{:S(2)}) copy-start(f32[128,512]{1,0:T(8,128)} %acc_ref.2) | copy-start | bytes 786436
  43.6 4.5 %collective-permute-start.15 = (f32[32,512]{1,0:T(8,128)S(1)}, f32[32,512]{1,0:T(8,128)S(1)}, u32[]{:S(2)}, u32[]{:S(2)}) collective-permute-start(f32[32,512]{1,0:T(8,128)S(1)} %get-tuple-element.53.refs_0_), channel_id=1, source_target_pairs={{0,8},{8,0},{16,24},{24,16},{1,9},{9,1},{17,25},{25,17},{2,10},{10... | collective-permute-start | bytes 196616 | tf_op jit(solution)/shard_map/ppermute | solution.py:20
  44.2 5.0 %collective-permute-start.16 = (f32[32,512]{1,0:T(8,128)S(1)}, f32[32,512]{1,0:T(8,128)S(1)}, u32[]{:S(2)}, u32[]{:S(2)}) collective-permute-start(f32[32,512]{1,0:T(8,128)S(1)} %get-tuple-element.53.refs_0_), channel_id=1, source_target_pairs={{0,16},{8,24},{16,0},{24,8},{1,17},{9,25},{17,1},{25,9},{2,18},{10... | collective-permute-start | bytes 196616 | tf_op jit(solution)/shard_map/ppermute | solution.py:20
  44.7 5.2 %collective-permute-start.17 = (f32[32,512]{1,0:T(8,128)S(1)}, f32[32,512]{1,0:T(8,128)S(1)}, u32[]{:S(2)}, u32[]{:S(2)}) collective-permute-start(f32[32,512]{1,0:T(8,128)S(1)} %get-tuple-element.53.refs_0_), channel_id=1, source_target_pairs={{0,24},{8,16},{16,8},{24,0},{1,25},{9,17},{17,9},{25,1},{2,26},{10... | collective-permute-start | bytes 196616 | tf_op jit(solution)/shard_map/ppermute | solution.py:20
  47.2 2.7 %copy-start.6 = (s32[1,8,16]{2,1,0:T(8,128)S(1)}, s32[1,8,16]{2,1,0:T(8,128)}, u32[]{:S(2)}) copy-start(s32[1,8,16]{2,1,0:T(8,128)} %send_ref.3) | copy-start | bytes 1540
  47.2 2.7 %copy-start.7 = (s32[8,32]{1,0:T(8,128)S(1)}, s32[8,32]{1,0:T(8,128)}, u32[]{:S(2)}) copy-start(s32[8,32]{1,0:T(8,128)} %neg_ref.3) | copy-start | bytes 3076

commit v5 on v4

--- a/solution.py
+++ b/solution.py
@@ -197,7 +197,7 @@
 
 
 def select_kernel(part_ref, after_ref, *refs):
-    *blocks, out_ref = refs
+    blocks, out_ref = refs[: lax.axis_size("dom")], refs[-1]
     source = lax.axis_index("dom") ^ part_ref[0]
     picked = blocks[0][...]
     for s, ref in enumerate(blocks):
@@ -214,12 +214,13 @@
         ref[2 * slots :] = mine[block] + theirs[block]
 
 
-def stack_kernel(order, *refs):
+def stack_kernel(order, neg_order, *refs):
     count = len(order)
     arrived, negs, out_ref = refs[:count], refs[count : 2 * count], refs[-1]
     n_neg, slots = negs[0].shape[0], arrived[0].shape[0] // 2
-    for s, block, rows in zip(order, negs, arrived):
+    for s, block in zip(neg_order, negs):
         out_ref[s * n_neg : (s + 1) * n_neg] = block[...]
+    for s, rows in zip(order, arrived):
         start = count * n_neg + s * slots
         out_ref[start : start + slots] = rows[slots:]
 
@@ -303,15 +304,16 @@
     (picked,) = call(
         select_kernel,
         [own_negs.shape],
-        [SMEM, VMEM] + [VMEM] * n_dom,
-        (neg_part, rot, *spread),
+        [SMEM, VMEM] + [VMEM] * (n_dom + len(arrived[1:2])),
+        (neg_part, rot, *spread, *arrived[1:2]),
     )
     negs = [picked] + [exchange(picked, "rel", n_rel, 2 * s) for s in range(1, n_chip)]
+    neg_order = [*range(2, n_chip)][::-1] + [*range(min(n_chip, 2))]
     (stacked,) = call(
-        functools.partial(stack_kernel, order),
+        functools.partial(stack_kernel, order, neg_order),
         [(n_chip * (n_neg + slots), width)],
         [VMEM] * (2 * n_chip),
-        (*[arrived[s] for s in order], *[negs[s] for s in order]),
+        (*[arrived[s] for s in order], *[negs[s] for s in neg_order]),
     )
     swapped = exchange(stacked, "rel", n_rel, 1)
 

time: 51.2 us -> 50.7 us (level)
  waiting for transfers between devices: 15.6 us -> 14.9 us
    ppermute x22, waiting for transfers between devices: 15.6 us -> 14.9 us  [exchange(): return lax.ppermute(block, axis, [(i, i ^ step) for i in range(size)])]
  transfers between devices with their start and end apart: 22 -> 22, of which waited for: 8 -> 11; matrix products, arithmetic and copies ran while one was open for 0% -> 0% of each run, Pallas kernels for 5% -> 5%
where the time goes in v5:
time: 50.7 us; the launch traced here: 50.5 us
  starting transfers between devices  26.5 us (52%)
  waiting for transfers between devices  14.9 us (29%)
  Pallas kernels  6.98 us (14%)
  between operations  1.49 us (3%)
  local copies, waits for them, and re-layouts  0.59 us (1%)
    ppermute x22, starting transfers between devices, exchange(): return lax.ppermute(block, axis, [(i, i ^ step) for i in range(size)])  26.5 us
    ppermute x22, waiting for transfers between devices, exchange(): return lax.ppermute(block, axis, [(i, i ^ step) for i in range(size)])  14.9 us
    pallas_call x10, Pallas kernels, call(): pl.pallas_call(body, out_shape=shapes, in_specs=specs, out_specs=[VMEM] *...  6.98 us
  transfers between devices with their start and end apart: 22, of which 11 were waited for; matrix products, arithmetic and copies ran while one was open for 0% of the time, Pallas kernels for 5%

profile of v5, /device:TPU:0, one launch (start us, length us, event | category | flops | bytes accessed | tf_op | source)
XLA Modules:
  0.0 50.5 jit_solution(11133196010303407379)
XLA Ops:
  0.6 2.0 %shard_map.130 = (f32[32,512]{1,0:T(8,128)}, f32[32,512]{1,0:T(8,128)}, f32[32,512]{1,0:T(8,128)}, f32[32,512]{1,0:T(8,128)}, f32[32,512]{1,0:T(8,128)}) custom-call(s32[1,8,16]{2,1,0:T(8,128)} %send_ref.3, s32[8,32]{1,0:T(8,128)} %neg_ref.3, f32[128,512]{1,0:T(8,128)} %entity_ref.3), custom_call_target="tpu_custom_call" | custom-call | bytes 591360 | tf_op jit(solution)/shard_map/pallas_call | solution.py:26
  2.7 3.1 %collective-permute-start = (f32[32,512]{1,0:T(8,128)}, f32[32,512]{1,0:T(8,128)S(1)}, u32[]{:S(2)}, u32[]{:S(2)}) collective-permute-start(f32[32,512]{1,0:T(8,128)} %get-tuple-element.33), channel_id=1, source_target_pairs={{0,2},{1,3},{2,0},{3,1},{4,6},{5,7},{6,4},{7,5},{8,10},{9,11},{10,... | collective-permute-start | bytes 196616 | tf_op jit(solution)/shard_map/ppermute | solution.py:20
  5.8 1.5 %collective-permute-start.3 = (f32[32,512]{1,0:T(8,128)}, f32[32,512]{1,0:T(8,128)S(1)}, u32[]{:S(2)}, u32[]{:S(2)}) collective-permute-start(f32[32,512]{1,0:T(8,128)} %get-tuple-element.36.refs_0_), channel_id=1, source_target_pairs={{0,8},{8,0},{16,24},{24,16},{1,9},{9,1},{17,25},{25,17},{2,10},{10... | collective-permute-start | bytes 196616 | tf_op jit(solution)/shard_map/ppermute | solution.py:20
  7.3 1.5 %collective-permute-start.4 = (f32[32,512]{1,0:T(8,128)}, f32[32,512]{1,0:T(8,128)S(1)}, u32[]{:S(2)}, u32[]{:S(2)}) collective-permute-start(f32[32,512]{1,0:T(8,128)} %get-tuple-element.36.refs_0_), channel_id=1, source_target_pairs={{0,16},{8,24},{16,0},{24,8},{1,17},{9,25},{17,1},{25,9},{2,18},{10... | collective-permute-start | bytes 196616 | tf_op jit(solution)/shard_map/ppermute | solution.py:20
  8.8 0.5 collective-permute-start.5
  9.3 2.6 %collective-permute-start.1 = (f32[32,512]{1,0:T(8,128)}, f32[32,512]{1,0:T(8,128)S(1)}, u32[]{:S(2)}, u32[]{:S(2)}) collective-permute-start(f32[32,512]{1,0:T(8,128)} %get-tuple-element.34), channel_id=1, source_target_pairs={{0,4},{1,5},{2,6},{3,7},{4,0},{5,1},{6,2},{7,3},{8,12},{9,13},{10,... | collective-permute-start | bytes 196616 | tf_op jit(solution)/shard_map/ppermute | solution.py:20
  12.5 0.0 copy-start.5
  12.6 0.3 shard_map.129.after_ref.rot_ref
  12.8 0.0 collective-permute-done.refs_4_.refs_3_.refs_1_
  12.8 0.5 %copy-done.11 = f32[32,512]{1,0:T(8,128)S(1)} copy-done((f32[32,512]{1,0:T(8,128)S(1)}, f32[32,512]{1,0:T(8,128)}, u32[]{:S(2)}) %copy-start.11) | copy-done | bytes 65560
  13.4 0.0 collective-permute-done.4.refs_2_
  13.4 0.8 %collective-permute-done.5.refs_3_ = f32[32,512]{1,0:T(8,128)S(1)} collective-permute-done((f32[32,512]{1,0:T(8,128)}, f32[32,512]{1,0:T(8,128)S(1)}, u32[]{:S(2)}, u32[]{:S(2)}) %collective-permute-start.5) | collective-permute-done | bytes 65568 | tf_op jit(solution)/shard_map/ppermute | solution.py:20
  14.2 3.1 %collective-permute-start.6 = (f32[32,512]{1,0:T(8,128)S(1)}, f32[32,512]{1,0:T(8,128)S(1)}, u32[]{:S(2)}, u32[]{:S(2)}) collective-permute-start(f32[32,512]{1,0:T(8,128)S(1)} %shard_map.131.refs_6_), channel_id=1, source_target_pairs={{0,6},{1,7},{2,4},{3,5},{4,2},{5,3},{6,0},{7,1},{8,14},{9,15},{10,... | collective-permute-start | bytes 196616 | tf_op jit(solution)/shard_map/ppermute | solution.py:20
  17.3 0.0 collective-permute-start.7
  17.3 1.3 %collective-permute-start.8 = (f32[32,512]{1,0:T(8,128)S(1)}, f32[32,512]{1,0:T(8,128)S(1)}, u32[]{:S(2)}, u32[]{:S(2)}) collective-permute-start(f32[32,512]{1,0:T(8,128)S(1)} %shard_map.131.refs_6_), channel_id=1, source_target_pairs={{0,2},{1,3},{2,0},{3,1},{4,6},{5,7},{6,4},{7,5},{8,10},{9,11},{10,... | collective-permute-start | bytes 196616 | tf_op jit(solution)/shard_map/ppermute | solution.py:20
  18.7 0.0 collective-permute-done.1.refs_0_.refs_2_
  18.7 0.8 %collective-permute-done.2.refs_1_.refs_3_ = f32[32,512]{1,0:T(8,128)S(1)} collective-permute-done((f32[32,512]{1,0:T(8,128)S(1)}, f32[32,512]{1,0:T(8,128)S(1)}, u32[]{:S(2)}, u32[]{:S(2)}) %collective-permute-start.2) | collective-permute-done | bytes 65568 | tf_op jit(solution)/shard_map/ppermute | solution.py:20
  19.5 1.3 %collective-permute-done.6.refs_4_ = f32[32,512]{1,0:T(8,128)S(1)} collective-permute-done((f32[32,512]{1,0:T(8,128)S(1)}, f32[32,512]{1,0:T(8,128)S(1)}, u32[]{:S(2)}, u32[]{:S(2)}) %collective-permute-start.6) | collective-permute-done | bytes 65568 | tf_op jit(solution)/shard_map/ppermute | solution.py:20
  20.8 2.6 %collective-permute-done.7.refs_5_ = f32[32,512]{1,0:T(8,128)S(1)} collective-permute-done((f32[32,512]{1,0:T(8,128)S(1)}, f32[32,512]{1,0:T(8,128)S(1)}, u32[]{:S(2)}, u32[]{:S(2)}) %collective-permute-start.7) | collective-permute-done | bytes 65568 | tf_op jit(solution)/shard_map/ppermute | solution.py:20
  23.4 0.0 collective-permute-done.8.refs_7_
  23.4 0.0 copy-start.9
  23.4 0.1 collective-permute-start.9
  23.5 1.7 %collective-permute-done.9.refs_5_.refs_1_ = f32[192,512]{1,0:T(8,128)S(1)} collective-permute-done((f32[192,512]{1,0:T(8,128)S(1)}, f32[192,512]{1,0:T(8,128)S(1)}, u32[]{:S(2)}, u32[]{:S(2)}) %collective-permute-start.9) | collective-permute-done | bytes 393248 | tf_op jit(solution)/shard_map/ppermute | solution.py:20
  25.2 1.4 %shard_map.133 = (f32[128,512]{1,0:T(8,128)S(1)}, f32[128,512]{1,0:T(8,128)S(1)}, f32[256,512]{1,0:T(8,128)S(1)}, f32[256,512]{1,0:T(8,128)S(1)}, f32[256,512]{1...) custom-call(s32[256]{0:T(256)S(1)} %copy-done.8, s32[256]{0:T(256)S(1)} %copy-done.9, ...), custom_call_target="tpu_custom_call" | custom-call | bytes 4065280 | tf_op jit(solution)/shard_map/pallas_call | solution.py:26
  26.6 0.2 collective-permute-start.10
  26.8 1.1 %shard_map.134 = (f32[64,512]{1,0:T(8,128)S(1)}, f32[64,512]{1,0:T(8,128)S(1)}, f32[128,512]{1,0:T(8,128)S(1)}) custom-call(s32[256]{0:T(256)S(1)} %copy-done.8, s32[256]{0:T(256)S(1)} %copy-done.10, s32[256]{0:T(256)S(1)} %copy-done.9, f32[128,512]{1,0:T(8,128)S(1)} %copy-done, f32[256,512]{1,0:T(8,128)S(1)} %shard_map.129.after_ref.rot_ref, ...), custom_call_target="tpu_custom_call" | custom-call | bytes 4066304 | tf_op jit(solution)/shard_map/pallas_call | solution.py:26
  28.0 0.3 collective-permute-done.10.theirs
  28.2 0.1 shard_map.135
  28.3 1.8 %collective-permute-start.18 = (f32[64,512]{1,0:T(8,128)S(1)}, f32[64,512]{1,0:T(8,128)S(1)}, u32[]{:S(2)}, u32[]{:S(2)}) collective-permute-start(f32[64,512]{1,0:T(8,128)S(1)} %get-tuple-element.56), channel_id=1, source_target_pairs={{0,8},{8,0},{16,24},{24,16},{1,9},{9,1},{17,25},{25,17},{2,10},{10... | collective-permute-start | bytes 393224 | tf_op jit(solution)/shard_map/ppermute | solution.py:20
  30.2 1.5 %collective-permute-start.20 = (f32[64,512]{1,0:T(8,128)S(1)}, f32[64,512]{1,0:T(8,128)S(1)}, u32[]{:S(2)}, u32[]{:S(2)}) collective-permute-start(f32[64,512]{1,0:T(8,128)S(1)} %get-tuple-element.57), channel_id=1, source_target_pairs={{0,16},{8,24},{16,0},{24,8},{1,17},{9,25},{17,1},{25,9},{2,18},{10... | collective-permute-start | bytes 393224 | tf_op jit(solution)/shard_map/ppermute | solution.py:20
  31.7 0.8 %collective-permute-start.11 = (f32[64,512]{1,0:T(8,128)S(1)}, f32[64,512]{1,0:T(8,128)S(1)}, u32[]{:S(2)}, u32[]{:S(2)}) collective-permute-start(f32[64,512]{1,0:T(8,128)S(1)} %get-tuple-element.47), channel_id=1, source_target_pairs={{0,4},{1,5},{2,6},{3,7},{4,0},{5,1},{6,2},{7,3},{8,12},{9,13},{10,... | collective-permute-start | bytes 393224 | tf_op jit(solution)/shard_map/ppermute | solution.py:20
  32.5 1.8 %collective-permute-start.12 = (f32[64,512]{1,0:T(8,128)S(1)}, f32[64,512]{1,0:T(8,128)S(1)}, u32[]{:S(2)}, u32[]{:S(2)}) collective-permute-start(f32[64,512]{1,0:T(8,128)S(1)} %get-tuple-element.48), channel_id=1, source_target_pairs={{0,2},{1,3},{2,0},{3,1},{4,6},{5,7},{6,4},{7,5},{8,10},{9,11},{10,... | collective-permute-start | bytes 393224 | tf_op jit(solution)/shard_map/ppermute | solution.py:20
  34.3 1.8 %collective-permute-start.13 = (f32[64,512]{1,0:T(8,128)S(1)}, f32[64,512]{1,0:T(8,128)S(1)}, u32[]{:S(2)}, u32[]{:S(2)}) collective-permute-start(f32[64,512]{1,0:T(8,128)S(1)} %get-tuple-element.50), channel_id=1, source_target_pairs={{0,6},{1,7},{2,4},{3,5},{4,2},{5,3},{6,0},{7,1},{8,14},{9,15},{10,... | collective-permute-start | bytes 393224 | tf_op jit(solution)/shard_map/ppermute | solution.py:20
  36.1 0.6 %collective-permute-start.19 = (f32[64,512]{1,0:T(8,128)S(1)}, f32[64,512]{1,0:T(8,128)S(1)}, u32[]{:S(2)}, u32[]{:S(2)}) collective-permute-start(f32[64,512]{1,0:T(8,128)S(1)} %add.6.low_a), channel_id=1, source_target_pairs={{0,16},{8,24},{16,0},{24,8},{1,17},{9,25},{17,1},{25,9},{2,18},{10... | collective-permute-start | bytes 393224 | tf_op jit(solution)/shard_map/ppermute | solution.py:20
  36.7 0.7 %collective-permute-start.21 = (f32[64,512]{1,0:T(8,128)S(1)}, f32[64,512]{1,0:T(8,128)S(1)}, u32[]{:S(2)}, u32[]{:S(2)}) collective-permute-start(f32[64,512]{1,0:T(8,128)S(1)} %add.7.high_a), channel_id=1, source_target_pairs={{0,8},{8,0},{16,24},{24,16},{1,9},{9,1},{17,25},{25,17},{2,10},{10... | collective-permute-start | bytes 393224 | tf_op jit(solution)/shard_map/ppermute | solution.py:20
  37.4 5.4 %collective-permute-done.11.refs_0_ = f32[64,512]{1,0:T(8,128)S(1)} collective-permute-done((f32[64,512]{1,0:T(8,128)S(1)}, f32[64,512]{1,0:T(8,128)S(1)}, u32[]{:S(2)}, u32[]{:S(2)}) %collective-permute-start.11) | collective-permute-done | bytes 131104 | tf_op jit(solution)/shard_map/ppermute | solution.py:20
  42.8 0.2 collective-permute-done.12.refs_1_
  43.0 0.1 collective-permute-start.14
  43.1 0.0 copy-start.1
  43.1 0.0 copy-start.4
  43.1 0.6 %collective-permute-start.15 = (f32[32,512]{1,0:T(8,128)S(1)}, f32[32,512]{1,0:T(8,128)S(1)}, u32[]{:S(2)}, u32[]{:S(2)}) collective-permute-start(f32[32,512]{1,0:T(8,128)S(1)} %get-tuple-element.53.refs_0_), channel_id=1, source_target_pairs={{0,8},{8,0},{16,24},{24,16},{1,9},{9,1},{17,25},{25,17},{2,10},{10... | collective-permute-start | bytes 196616 | tf_op jit(solution)/shard_map/ppermute | solution.py:20
  43.7 0.5 collective-permute-start.16
  44.2 2.5 %collective-permute-start.17 = (f32[32,512]{1,0:T(8,128)S(1)}, f32[32,512]{1,0:T(8,128)S(1)}, u32[]{:S(2)}, u32[]{:S(2)}) collective-permute-start(f32[32,512]{1,0:T(8,128)S(1)} %get-tuple-element.53.refs_0_), channel_id=1, source_target_pairs={{0,24},{8,16},{16,8},{24,0},{1,25},{9,17},{17,9},{25,1},{2,26},{10... | collective-permute-start | bytes 196616 | tf_op jit(solution)/shard_map/ppermute | solution.py:20
  46.7 0.9 %shard_map.138 = (f32[128,512]{1,0:T(8,128)}, f32[128,512]{1,0:T(8,128)}) custom-call(f32[64,512]{1,0:T(8,128)S(1)} %add.6.low_a, f32[64,512]{1,0:T(8,128)S(1)} %collective-permute-done.19.low_b, f32[64,512]{1,0:T(8,128)S(1)} %add.7.high_a, f32[64,512]{1,0:T(8,128)S(1)} %collective-permute-done.21.high_b, f32[128,512]{1,0:T(8,128)S(1)} %copy-done, ...), custom_call_target="tpu_custom_call" | custom-call | bytes 1572864 | tf_op jit(solution)/shard_map/pallas_call | solution.py:26
  47.6 0.1 collective-permute-done.15.refs_1_
  47.6 1.1 %collective-permute-done.16.refs_2_ = f32[32,512]{1,0:T(8,128)S(1)} collective-permute-done((f32[32,512]{1,0:T(8,128)S(1)}, f32[32,512]{1,0:T(8,128)S(1)}, u32[]{:S(2)}, u32[]{:S(2)}) %collective-permute-start.16) | collective-permute-done | bytes 65568 | tf_op jit(solution)/shard_map/ppermute | solution.py:20
  48.7 0.7 %collective-permute-done.17.refs_3_ = f32[32,512]{1,0:T(8,128)S(1)} collective-permute-done((f32[32,512]{1,0:T(8,128)S(1)}, f32[32,512]{1,0:T(8,128)S(1)}, u32[]{:S(2)}, u32[]{:S(2)}) %collective-permute-start.17) | collective-permute-done | bytes 65568 | tf_op jit(solution)/shard_map/ppermute | solution.py:20
  49.4 1.1 %shard_map.137 = (f32[128,512]{1,0:T(8,128)}, f32[128,512]{1,0:T(8,128)}) custom-call(s32[1]{0:T(128)S(6)} %copy.14.part_ref, s32[1,8,16]{2,1,0:T(8,128)S(1)} %copy-done.6, s32[8,32]{1,0:T(8,128)S(1)} %copy-done.7, f32[128,512]{1,0:T(8,128)S(1)} %copy-done.1, f32[128,512]{1,0:T(8,128)S(1)} %copy-done.4, f32[64,512]{1,0:T(8,128)S(1)} %get-tuple-element.51.stay_ref, ...), custom_call_target="tpu_custom_call" | custom-call | bytes 1574404 | tf_op jit(solution)/shard_map/pallas_call | solution.py:26
  (32 shorter events, 0.2 us)
Async XLA Ops:
  0.6 11.9 %copy-start = (f32[128,512]{1,0:T(8,128)S(1)}, f32[128,512]{1,0:T(8,128)}, u32[]{:S(2)}) copy-start(f32[128,512]{1,0:T(8,128)} %relation_ref.5) | copy-start | bytes 786436
  2.7 10.1 %collective-permute-start = (f32[32,512]{1,0:T(8,128)}, f32[32,512]{1,0:T(8,128)S(1)}, u32[]{:S(2)}, u32[]{:S(2)}) collective-permute-start(f32[32,512]{1,0:T(8,128)} %get-tuple-element.33), channel_id=1, source_target_pairs={{0,2},{1,3},{2,0},{3,1},{4,6},{5,7},{6,4},{7,5},{8,10},{9,11},{10,... | collective-permute-start | bytes 196616 | tf_op jit(solution)/shard_map/ppermute | solution.py:20
  5.8 7.6 %collective-permute-start.3 = (f32[32,512]{1,0:T(8,128)}, f32[32,512]{1,0:T(8,128)S(1)}, u32[]{:S(2)}, u32[]{:S(2)}) collective-permute-start(f32[32,512]{1,0:T(8,128)} %get-tuple-element.36.refs_0_), channel_id=1, source_target_pairs={{0,8},{8,0},{16,24},{24,16},{1,9},{9,1},{17,25},{25,17},{2,10},{10... | collective-permute-start | bytes 196616 | tf_op jit(solution)/shard_map/ppermute | solution.py:20
  7.3 6.1 %collective-permute-start.4 = (f32[32,512]{1,0:T(8,128)}, f32[32,512]{1,0:T(8,128)S(1)}, u32[]{:S(2)}, u32[]{:S(2)}) collective-permute-start(f32[32,512]{1,0:T(8,128)} %get-tuple-element.36.refs_0_), channel_id=1, source_target_pairs={{0,16},{8,24},{16,0},{24,8},{1,17},{9,25},{17,1},{25,9},{2,18},{10... | collective-permute-start | bytes 196616 | tf_op jit(solution)/shard_map/ppermute | solution.py:20
  8.8 5.4 %collective-permute-start.5 = (f32[32,512]{1,0:T(8,128)}, f32[32,512]{1,0:T(8,128)S(1)}, u32[]{:S(2)}, u32[]{:S(2)}) collective-permute-start(f32[32,512]{1,0:T(8,128)} %get-tuple-element.36.refs_0_), channel_id=1, source_target_pairs={{0,24},{8,16},{16,8},{24,0},{1,25},{9,17},{17,9},{25,1},{2,26},{10... | collective-permute-start | bytes 196616 | tf_op jit(solution)/shard_map/ppermute | solution.py:20
  9.3 3.3 %copy-start.10 = (s32[256]{0:T(256)S(1)}, s32[256]{0:T(256)}, u32[]{:S(2)}) copy-start(s32[256]{0:T(256)} %rel_index_ref.3) | copy-start | bytes 3076
  9.3 9.4 %collective-permute-start.1 = (f32[32,512]{1,0:T(8,128)}, f32[32,512]{1,0:T(8,128)S(1)}, u32[]{:S(2)}, u32[]{:S(2)}) collective-permute-start(f32[32,512]{1,0:T(8,128)} %get-tuple-element.34), channel_id=1, source_target_pairs={{0,4},{1,5},{2,6},{3,7},{4,0},{5,1},{6,2},{7,3},{8,12},{9,13},{10,... | collective-permute-start | bytes 196616 | tf_op jit(solution)/shard_map/ppermute | solution.py:20
  12.5 0.8 %copy-start.11 = (f32[32,512]{1,0:T(8,128)S(1)}, f32[32,512]{1,0:T(8,128)}, u32[]{:S(2)}) copy-start(f32[32,512]{1,0:T(8,128)} %get-tuple-element.35) | copy-start | bytes 196612
  12.5 1.6 %copy-start.5 = (f32[32,512]{1,0:T(8,128)S(1)}, f32[32,512]{1,0:T(8,128)}, u32[]{:S(2)}) copy-start(f32[32,512]{1,0:T(8,128)} %get-tuple-element.36.refs_0_) | copy-start | bytes 196612
  13.4 10.0 %copy-start.2 = (f32[32,512]{1,0:T(8,128)S(1)}, f32[32,512]{1,0:T(8,128)}, u32[]{:S(2)}) copy-start(f32[32,512]{1,0:T(8,128)} %get-tuple-element.32.refs_2_.refs_0_) | copy-start | bytes 196612
  13.4 6.1 %collective-permute-start.2 = (f32[32,512]{1,0:T(8,128)S(1)}, f32[32,512]{1,0:T(8,128)S(1)}, u32[]{:S(2)}, u32[]{:S(2)}) collective-permute-start(f32[32,512]{1,0:T(8,128)S(1)} %copy-done.11), channel_id=1, source_target_pairs={{0,6},{1,7},{2,4},{3,5},{4,2},{5,3},{6,0},{7,1},{8,14},{9,15},{10,... | collective-permute-start | bytes 196616 | tf_op jit(solution)/shard_map/ppermute | solution.py:20
  14.2 6.6 %collective-permute-start.6 = (f32[32,512]{1,0:T(8,128)S(1)}, f32[32,512]{1,0:T(8,128)S(1)}, u32[]{:S(2)}, u32[]{:S(2)}) collective-permute-start(f32[32,512]{1,0:T(8,128)S(1)} %shard_map.131.refs_6_), channel_id=1, source_target_pairs={{0,6},{1,7},{2,4},{3,5},{4,2},{5,3},{6,0},{7,1},{8,14},{9,15},{10,... | collective-permute-start | bytes 196616 | tf_op jit(solution)/shard_map/ppermute | solution.py:20
  17.3 6.1 %collective-permute-start.7 = (f32[32,512]{1,0:T(8,128)S(1)}, f32[32,512]{1,0:T(8,128)S(1)}, u32[]{:S(2)}, u32[]{:S(2)}) collective-permute-start(f32[32,512]{1,0:T(8,128)S(1)} %shard_map.131.refs_6_), channel_id=1, source_target_pairs={{0,4},{1,5},{2,6},{3,7},{4,0},{5,1},{6,2},{7,3},{8,12},{9,13},{10,... | collective-permute-start | bytes 196616 | tf_op jit(solution)/shard_map/ppermute | solution.py:20
  17.3 6.1 %collective-permute-start.8 = (f32[32,512]{1,0:T(8,128)S(1)}, f32[32,512]{1,0:T(8,128)S(1)}, u32[]{:S(2)}, u32[]{:S(2)}) collective-permute-start(f32[32,512]{1,0:T(8,128)S(1)} %shard_map.131.refs_6_), channel_id=1, source_target_pairs={{0,2},{1,3},{2,0},{3,1},{4,6},{5,7},{6,4},{7,5},{8,10},{9,11},{10,... | collective-permute-start | bytes 196616 | tf_op jit(solution)/shard_map/ppermute | solution.py:20
  23.4 1.8 %copy-start.8 = (s32[256]{0:T(256)S(1)}, s32[256]{0:T(256)}, u32[]{:S(2)}) copy-start(s32[256]{0:T(256)} %head_ref.3) | copy-start | bytes 3076
  23.4 1.8 %copy-start.9 = (s32[256]{0:T(256)S(1)}, s32[256]{0:T(256)}, u32[]{:S(2)}) copy-start(s32[256]{0:T(256)} %tail_ref.3) | copy-start | bytes 3076
  23.4 1.8 %collective-permute-start.9 = (f32[192,512]{1,0:T(8,128)S(1)}, f32[192,512]{1,0:T(8,128)S(1)}, u32[]{:S(2)}, u32[]{:S(2)}) collective-permute-start(f32[192,512]{1,0:T(8,128)S(1)} %shard_map.132.refs_4_.refs_0_), channel_id=1, source_target_pairs={{0,1},{1,0},{2,3},{3,2},{4,5},{5,4},{6,7},{7,6},{8,9},{9,8},{10,11... | collective-permute-start | bytes 1179656 | tf_op jit(solution)/shard_map/ppermute | solution.py:20
  26.6 1.6 %collective-permute-start.10 = (f32[128,512]{1,0:T(8,128)S(1)}, f32[128,512]{1,0:T(8,128)S(1)}, u32[]{:S(2)}, u32[]{:S(2)}) collective-permute-start(f32[128,512]{1,0:T(8,128)S(1)} %get-tuple-element.38), channel_id=1, source_target_pairs={{0,1},{1,0},{2,3},{3,2},{4,5},{5,4},{6,7},{7,6},{8,9},{9,8},{10,11... | collective-permute-start | bytes 786440 | tf_op jit(solution)/shard_map/ppermute | solution.py:20
  28.3 7.7 %collective-permute-start.18 = (f32[64,512]{1,0:T(8,128)S(1)}, f32[64,512]{1,0:T(8,128)S(1)}, u32[]{:S(2)}, u32[]{:S(2)}) collective-permute-start(f32[64,512]{1,0:T(8,128)S(1)} %get-tuple-element.56), channel_id=1, source_target_pairs={{0,8},{8,0},{16,24},{24,16},{1,9},{9,1},{17,25},{25,17},{2,10},{10... | collective-permute-start | bytes 393224 | tf_op jit(solution)/shard_map/ppermute | solution.py:20
  30.2 6.5 %collective-permute-start.20 = (f32[64,512]{1,0:T(8,128)S(1)}, f32[64,512]{1,0:T(8,128)S(1)}, u32[]{:S(2)}, u32[]{:S(2)}) collective-permute-start(f32[64,512]{1,0:T(8,128)S(1)} %get-tuple-element.57), channel_id=1, source_target_pairs={{0,16},{8,24},{16,0},{24,8},{1,17},{9,25},{17,1},{25,9},{2,18},{10... | collective-permute-start | bytes 393224 | tf_op jit(solution)/shard_map/ppermute | solution.py:20
  31.7 11.1 %collective-permute-start.11 = (f32[64,512]{1,0:T(8,128)S(1)}, f32[64,512]{1,0:T(8,128)S(1)}, u32[]{:S(2)}, u32[]{:S(2)}) collective-permute-start(f32[64,512]{1,0:T(8,128)S(1)} %get-tuple-element.47), channel_id=1, source_target_pairs={{0,4},{1,5},{2,6},{3,7},{4,0},{5,1},{6,2},{7,3},{8,12},{9,13},{10,... | collective-permute-start | bytes 393224 | tf_op jit(solution)/shard_map/ppermute | solution.py:20
  32.5 10.5 %collective-permute-start.12 = (f32[64,512]{1,0:T(8,128)S(1)}, f32[64,512]{1,0:T(8,128)S(1)}, u32[]{:S(2)}, u32[]{:S(2)}) collective-permute-start(f32[64,512]{1,0:T(8,128)S(1)} %get-tuple-element.48), channel_id=1, source_target_pairs={{0,2},{1,3},{2,0},{3,1},{4,6},{5,7},{6,4},{7,5},{8,10},{9,11},{10,... | collective-permute-start | bytes 393224 | tf_op jit(solution)/shard_map/ppermute | solution.py:20
  34.3 8.7 %collective-permute-start.13 = (f32[64,512]{1,0:T(8,128)S(1)}, f32[64,512]{1,0:T(8,128)S(1)}, u32[]{:S(2)}, u32[]{:S(2)}) collective-permute-start(f32[64,512]{1,0:T(8,128)S(1)} %get-tuple-element.50), channel_id=1, source_target_pairs={{0,6},{1,7},{2,4},{3,5},{4,2},{5,3},{6,0},{7,1},{8,14},{9,15},{10,... | collective-permute-start | bytes 393224 | tf_op jit(solution)/shard_map/ppermute | solution.py:20
  36.1 8.1 %collective-permute-start.19 = (f32[64,512]{1,0:T(8,128)S(1)}, f32[64,512]{1,0:T(8,128)S(1)}, u32[]{:S(2)}, u32[]{:S(2)}) collective-permute-start(f32[64,512]{1,0:T(8,128)S(1)} %add.6.low_a), channel_id=1, source_target_pairs={{0,16},{8,24},{16,0},{24,8},{1,17},{9,25},{17,1},{25,9},{2,18},{10... | collective-permute-start | bytes 393224 | tf_op jit(solution)/shard_map/ppermute | solution.py:20
  36.7 10.0 %collective-permute-start.21 = (f32[64,512]{1,0:T(8,128)S(1)}, f32[64,512]{1,0:T(8,128)S(1)}, u32[]{:S(2)}, u32[]{:S(2)}) collective-permute-start(f32[64,512]{1,0:T(8,128)S(1)} %add.7.high_a), channel_id=1, source_target_pairs={{0,8},{8,0},{16,24},{24,16},{1,9},{9,1},{17,25},{25,17},{2,10},{10... | collective-permute-start | bytes 393224 | tf_op jit(solution)/shard_map/ppermute | solution.py:20
  43.0 3.7 %copy-start.3 = (f32[128,512]{1,0:T(8,128)S(1)}, f32[128,512]{1,0:T(8,128)}, u32[]{:S(2)}) copy-start(f32[128,512]{1,0:T(8,128)} %acc_ref.3) | copy-start | bytes 786436
  43.0 6.4 %collective-permute-start.14 = (f32[64,512]{1,0:T(8,128)S(1)}, f32[64,512]{1,0:T(8,128)S(1)}, u32[]{:S(2)}, u32[]{:S(2)}) collective-permute-start(f32[64,512]{1,0:T(8,128)S(1)} %get-tuple-element.52), channel_id=1, source_target_pairs={{0,1},{1,0},{2,3},{3,2},{4,5},{5,4},{6,7},{7,6},{8,9},{9,8},{10,11... | collective-permute-start | bytes 393224 | tf_op jit(solution)/shard_map/ppermute | solution.py:20
  43.1 6.3 %copy-start.1 = (f32[128,512]{1,0:T(8,128)S(1)}, f32[128,512]{1,0:T(8,128)}, u32[]{:S(2)}) copy-start(f32[128,512]{1,0:T(8,128)} %entity_ref.3) | copy-start | bytes 786436
  43.1 6.3 %copy-start.4 = (f32[128,512]{1,0:T(8,128)S(1)}, f32[128,512]{1,0:T(8,128)}, u32[]{:S(2)}) copy-start(f32[128,512]{1,0:T(8,128)} %acc_ref.2) | copy-start | bytes 786436
  43.1 4.5 %collective-permute-start.15 = (f32[32,512]{1,0:T(8,128)S(1)}, f32[32,512]{1,0:T(8,128)S(1)}, u32[]{:S(2)}, u32[]{:S(2)}) collective-permute-start(f32[32,512]{1,0:T(8,128)S(1)} %get-tuple-element.53.refs_0_), channel_id=1, source_target_pairs={{0,8},{8,0},{16,24},{24,16},{1,9},{9,1},{17,25},{25,17},{2,10},{10... | collective-permute-start | bytes 196616 | tf_op jit(solution)/shard_map/ppermute | solution.py:20
  43.7 5.0 %collective-permute-start.16 = (f32[32,512]{1,0:T(8,128)S(1)}, f32[32,512]{1,0:T(8,128)S(1)}, u32[]{:S(2)}, u32[]{:S(2)}) collective-permute-start(f32[32,512]{1,0:T(8,128)S(1)} %get-tuple-element.53.refs_0_), channel_id=1, source_target_pairs={{0,16},{8,24},{16,0},{24,8},{1,17},{9,25},{17,1},{25,9},{2,18},{10... | collective-permute-start | bytes 196616 | tf_op jit(solution)/shard_map/ppermute | solution.py:20
  44.2 5.2 %collective-permute-start.17 = (f32[32,512]{1,0:T(8,128)S(1)}, f32[32,512]{1,0:T(8,128)S(1)}, u32[]{:S(2)}, u32[]{:S(2)}) collective-permute-start(f32[32,512]{1,0:T(8,128)S(1)} %get-tuple-element.53.refs_0_), channel_id=1, source_target_pairs={{0,24},{8,16},{16,8},{24,0},{1,25},{9,17},{17,9},{25,1},{2,26},{10... | collective-permute-start | bytes 196616 | tf_op jit(solution)/shard_map/ppermute | solution.py:20
  46.7 2.7 %copy-start.6 = (s32[1,8,16]{2,1,0:T(8,128)S(1)}, s32[1,8,16]{2,1,0:T(8,128)}, u32[]{:S(2)}) copy-start(s32[1,8,16]{2,1,0:T(8,128)} %send_ref.3) | copy-start | bytes 1540
  46.7 2.7 %copy-start.7 = (s32[8,32]{1,0:T(8,128)S(1)}, s32[8,32]{1,0:T(8,128)}, u32[]{:S(2)}) copy-start(s32[8,32]{1,0:T(8,128)} %neg_ref.3) | copy-start | bytes 3076

commit v6 on v5

--- a/solution.py
+++ b/solution.py
@@ -18,6 +18,14 @@
 
 def exchange(block, axis, size, step):
     return lax.ppermute(block, axis, [(i, i ^ step) for i in range(size)])
+
+
+def cross_exchange(block, n_dom, n_rel, even, odd):
+    pairs = []
+    for i in range(n_dom):
+        for r in range(n_rel):
+            pairs.append((i * n_rel + r, (i ^ (odd if r % 2 else even)) * n_rel + r))
+    return lax.ppermute(block, ("dom", "rel"), pairs)
 
 
 def call(body, outs, specs, args, flops=0, scratch=(), limit=40 * 1024):
@@ -174,7 +182,7 @@
 
 def grad_kernel(slots, half, head_ref, rel_index_ref, tail_ref, relation_ref, rot_ref, *refs):
     stacked, swapped, query_ref, head_rows, tail_rows, pull_ref, push_ref = refs[:7]
-    low_ref, high_ref, touched_ref = refs[7:]
+    rel_ref, touched_ref = refs[7:]
     negs = jnp.concatenate([stacked[:half], swapped[:half]], axis=0)
     p_high, p_low = halves(push_ref[...])
     n_high, n_low = halves(negs)
@@ -190,10 +198,7 @@
     chosen = pick(rel_index_ref[...].reshape(1, -1), relation_ref.shape[0])
     grad_unit = quarters(put(chosen, grad_rot))
     along = sum(u * g for u, g in zip(unit, grad_unit))
-    rel_grad = join([inverse * (g - u * along) for u, g in zip(unit, grad_unit)])
-    middle = low_ref.shape[0]
-    low_ref[...] = rel_grad[:middle]
-    high_ref[...] = rel_grad[middle:]
+    rel_ref[...] = join([inverse * (g - u * along) for u, g in zip(unit, grad_unit)])
 
 
 def select_kernel(part_ref, after_ref, *refs):
@@ -205,9 +210,8 @@
     out_ref[...] = picked
 
 
-def pack_kernel(slots, n_neg, mine, theirs, touched, low, high, low_ref, high_ref, *back):
-    low_ref[...] = low[...]
-    high_ref[...] = high[...]
+def pack_kernel(slots, n_neg, mine, theirs, touched, rel, rel_ref, *back):
+    rel_ref[...] = rel[...]
     for s, ref in enumerate(back):
         block = pl.ds(s * n_neg, n_neg)
         ref[: 2 * slots] = touched[2 * s * slots : 2 * (s + 1) * slots]
@@ -257,9 +261,16 @@
     out_ref[...], acc_out[...] = adagrad(entity_ref[...], acc_ref[...], grad)
 
 
-def relation_kernel(low_a, low_b, high_a, high_b, relation_ref, acc_ref, out_ref, acc_out):
-    grad = jnp.concatenate([low_a[...] + low_b[...], high_a[...] + high_b[...]], axis=0)
+def relation_kernel(*refs):
+    *parts, relation_ref, acc_ref, out_ref, acc_out = refs
+    grad = sum(ref[...] for ref in parts)
     out_ref[...], acc_out[...] = adagrad(relation_ref[...], acc_ref[...], grad)
+
+
+def update_kernel(count, *refs):
+    new_rel, (new_ent, ins) = refs[-2:], (refs[-4:-2], refs[:-4])
+    relation_kernel(*ins[-2 - count :], *new_rel)
+    entity_kernel(*ins[: -2 - count], *new_ent)
 
 
 def shards(
@@ -324,28 +335,25 @@
         (trip_head, trip_tail, rot, *arrived, stacked, swapped),
     )
     theirs = exchange(theirs, "rel", n_rel, 1)
-    low, high, touched = call(
+    rel_grad, touched = call(
         functools.partial(grad_kernel, slots, n_chip * n_neg),
-        [(rels // 2, width)] * 2 + [(n_rel * slots, width)],
+        [relation.shape, (n_rel * slots, width)],
         [VMEM] * 12,
         (trip_head, trip_rel, trip_tail, relation, rot, stacked, swapped, *saved),
     )
 
-    low, high, *back = call(
+    rel_grad, *back = call(
         functools.partial(pack_kernel, slots, n_neg),
-        [low.shape, high.shape] + [(2 * slots + n_neg, width)] * n_chip,
-        [VMEM] * 5,
-        (mine, theirs, touched, low, high),
+        [relation.shape] + [(2 * slots + n_neg, width)] * n_chip,
+        [VMEM] * 4,
+        (mine, theirs, touched, rel_grad),
     )
     back = [back[0]] + [exchange(back[s], "rel", n_rel, 2 * s) for s in range(1, n_chip)]
     bits = [1 << b for b in range((n_dom - 1).bit_length())]
-    sums = [[low], [high]]
-    first = []
+    sums = [rel_grad]
     for up, down in zip(bits, bits[::-1]):
-        sums = [[sum(pair)] for pair in sums]
-        first = first or ([sums[0][0], sums[1][0]] if len(bits) > 1 and up != bits[0] else [])
-        sums[0].append(exchange(sums[0][0], "dom", n_dom, up))
-        sums[1].append(exchange(sums[1][0], "dom", n_dom, down))
+        total = sum(sums)
+        sums = [total, cross_exchange(total, n_dom, n_rel, up, down)]
     back_order = [*range(2, n_chip, 2), *range(min(n_chip, 2))[::-1], *range(3, n_chip, 2)]
     neg_share, stay, cross = call(
         functools.partial(unpack_kernel, slots, back_order),
@@ -356,18 +364,12 @@
     neg_shares = [neg_share] + [exchange(neg_share, "dom", n_dom, s) for s in range(1, n_dom)]
     cross = exchange(cross, "rel", n_rel, 1)
 
-    new_relation, new_relation_acc = call(
-        relation_kernel,
-        [relation.shape] * 2,
-        [VMEM] * 6,
-        (*sums[0], *sums[1], relation, relation_acc),
-    )
-
-    new_entity, new_entity_acc = call(
-        entity_kernel,
-        [entity.shape] * 2,
-        [SMEM] + [VMEM] * (6 + n_dom),
-        (neg_part, send_rows, neg_rows, entity, entity_acc, stay, cross, *neg_shares),
+    new_entity, new_entity_acc, new_relation, new_relation_acc = call(
+        functools.partial(update_kernel, len(sums)),
+        [entity.shape] * 2 + [relation.shape] * 2,
+        [SMEM] + [VMEM] * (8 + n_dom + len(sums)),
+        (neg_part, send_rows, neg_rows, entity, entity_acc, stay, cross)
+        + (*neg_shares, *sums, relation, relation_acc),
     )
     return (new_entity, new_entity_acc, new_relation, new_relation_acc)
 

time: 50.7 us -> 50.7 us (level)
  waiting for transfers between devices: 14.9 us -> 16.3 us
  starting transfers between devices: 26.5 us -> 25.6 us
  Pallas kernels: 6.98 us -> 6.32 us
    ppermute x22 -> x18, starting transfers between devices: 26.5 us -> 21.9 us  [exchange(): return lax.ppermute(block, axis, [(i, i ^ step) for i in range(size)])]
    ppermute x0 -> x2, starting transfers between devices: none -> 3.71 us  [cross_exchange(): return lax.ppermute(block, ('dom', 'rel'), pairs)]
    ppermute x22 -> x18, waiting for transfers between devices: 14.9 us -> 16.1 us  [exchange(): return lax.ppermute(block, axis, [(i, i ^ step) for i in range(size)])]
    pallas_call x10 -> x9, Pallas kernels: 6.98 us -> 6.32 us  [call(): pl.pallas_call(body, out_shape=shapes, in_specs=specs, out_specs=[VMEM] *...]
  transfers between devices with their start and end apart: 22 -> 20, of which waited for: 11 -> 12; matrix products, arithmetic and copies ran while one was open for 0% -> 0% of each run, Pallas kernels for 5% -> 3%
where the time goes in v6:
time: 50.7 us; the launch traced here: 50.4 us
  starting transfers between devices  25.6 us (50%)
  waiting for transfers between devices  16.3 us (32%)
  Pallas kernels  6.32 us (12%)
  between operations  1.49 us (3%)
  local copies, waits for them, and re-layouts  0.59 us (1%)
    ppermute x18, starting transfers between devices, exchange(): return lax.ppermute(block, axis, [(i, i ^ step) for i in range(size)])  21.9 us
    ppermute x18, waiting for transfers between devices, exchange(): return lax.ppermute(block, axis, [(i, i ^ step) for i in range(size)])  16.1 us
    pallas_call x9, Pallas kernels, call(): pl.pallas_call(body, out_shape=shapes, in_specs=specs, out_specs=[VMEM] *...  6.32 us
    ppermute x2, starting transfers between devices, cross_exchange(): return lax.ppermute(block, ('dom', 'rel'), pairs)  3.71 us
  transfers between devices with their start and end apart: 20, of which 12 were waited for; matrix products, arithmetic and copies ran while one was open for 0% of the time, Pallas kernels for 3%

profile of v6, /device:TPU:0, one launch (start us, length us, event | category | flops | bytes accessed | tf_op | source)
XLA Modules:
  0.0 50.4 jit_solution(4642056117325231114)
XLA Ops:
  0.6 2.1 %shard_map.130 = (f32[32,512]{1,0:T(8,128)}, f32[32,512]{1,0:T(8,128)}, f32[32,512]{1,0:T(8,128)}, f32[32,512]{1,0:T(8,128)}, f32[32,512]{1,0:T(8,128)}) custom-call(s32[1,8,16]{2,1,0:T(8,128)} %refs_1_.1, s32[8,32]{1,0:T(8,128)} %refs_2_.1, f32[128,512]{1,0:T(8,128)} %refs_3_.1), custom_call_target="tpu_custom_call" | custom-call | bytes 591360 | tf_op jit(solution)/shard_map/pallas_call | solution.py:34
  2.7 3.1 %collective-permute-start = (f32[32,512]{1,0:T(8,128)}, f32[32,512]{1,0:T(8,128)S(1)}, u32[]{:S(2)}, u32[]{:S(2)}) collective-permute-start(f32[32,512]{1,0:T(8,128)} %get-tuple-element.27), channel_id=1, source_target_pairs={{0,2},{1,3},{2,0},{3,1},{4,6},{5,7},{6,4},{7,5},{8,10},{9,11},{10,... | collective-permute-start | bytes 196616 | tf_op jit(solution)/shard_map/ppermute | solution.py:20
  5.8 1.5 %collective-permute-start.3 = (f32[32,512]{1,0:T(8,128)}, f32[32,512]{1,0:T(8,128)S(1)}, u32[]{:S(2)}, u32[]{:S(2)}) collective-permute-start(f32[32,512]{1,0:T(8,128)} %get-tuple-element.30.refs_0_), channel_id=1, source_target_pairs={{0,8},{8,0},{16,24},{24,16},{1,9},{9,1},{17,25},{25,17},{2,10},{10... | collective-permute-start | bytes 196616 | tf_op jit(solution)/shard_map/ppermute | solution.py:20
  7.3 1.5 %collective-permute-start.4 = (f32[32,512]{1,0:T(8,128)}, f32[32,512]{1,0:T(8,128)S(1)}, u32[]{:S(2)}, u32[]{:S(2)}) collective-permute-start(f32[32,512]{1,0:T(8,128)} %get-tuple-element.30.refs_0_), channel_id=1, source_target_pairs={{0,16},{8,24},{16,0},{24,8},{1,17},{9,25},{17,1},{25,9},{2,18},{10... | collective-permute-start | bytes 196616 | tf_op jit(solution)/shard_map/ppermute | solution.py:20
  8.8 0.5 collective-permute-start.5
  9.3 2.6 %collective-permute-start.1 = (f32[32,512]{1,0:T(8,128)}, f32[32,512]{1,0:T(8,128)S(1)}, u32[]{:S(2)}, u32[]{:S(2)}) collective-permute-start(f32[32,512]{1,0:T(8,128)} %get-tuple-element.28), channel_id=1, source_target_pairs={{0,4},{1,5},{2,6},{3,7},{4,0},{5,1},{6,2},{7,3},{8,12},{9,13},{10,... | collective-permute-start | bytes 196616 | tf_op jit(solution)/shard_map/ppermute | solution.py:20
  12.6 0.0 copy-start.5
  12.6 0.3 shard_map.129.after_ref.rot_ref
  12.8 0.0 collective-permute-done.refs_4_.refs_3_.refs_1_
  12.8 0.5 %copy-done.11 = f32[32,512]{1,0:T(8,128)S(1)} copy-done((f32[32,512]{1,0:T(8,128)S(1)}, f32[32,512]{1,0:T(8,128)}, u32[]{:S(2)}) %copy-start.11) | copy-done | bytes 65560
  13.4 0.0 collective-permute-start.2
  13.4 0.0 collective-permute-done.4.refs_2_
  13.4 0.8 %collective-permute-done.5.refs_3_ = f32[32,512]{1,0:T(8,128)S(1)} collective-permute-done((f32[32,512]{1,0:T(8,128)}, f32[32,512]{1,0:T(8,128)S(1)}, u32[]{:S(2)}, u32[]{:S(2)}) %collective-permute-start.5) | collective-permute-done | bytes 65568 | tf_op jit(solution)/shard_map/ppermute | solution.py:20
  14.2 3.1 %collective-permute-start.6 = (f32[32,512]{1,0:T(8,128)S(1)}, f32[32,512]{1,0:T(8,128)S(1)}, u32[]{:S(2)}, u32[]{:S(2)}) collective-permute-start(f32[32,512]{1,0:T(8,128)S(1)} %shard_map.131.refs_6_), channel_id=1, source_target_pairs={{0,6},{1,7},{2,4},{3,5},{4,2},{5,3},{6,0},{7,1},{8,14},{9,15},{10,... | collective-permute-start | bytes 196616 | tf_op jit(solution)/shard_map/ppermute | solution.py:20
  17.3 0.0 collective-permute-start.7
  17.3 1.3 %collective-permute-start.8 = (f32[32,512]{1,0:T(8,128)S(1)}, f32[32,512]{1,0:T(8,128)S(1)}, u32[]{:S(2)}, u32[]{:S(2)}) collective-permute-start(f32[32,512]{1,0:T(8,128)S(1)} %shard_map.131.refs_6_), channel_id=1, source_target_pairs={{0,2},{1,3},{2,0},{3,1},{4,6},{5,7},{6,4},{7,5},{8,10},{9,11},{10,... | collective-permute-start | bytes 196616 | tf_op jit(solution)/shard_map/ppermute | solution.py:20
  18.7 0.0 collective-permute-done.1.refs_0_.refs_2_
  18.7 0.8 %collective-permute-done.2.refs_1_.refs_3_ = f32[32,512]{1,0:T(8,128)S(1)} collective-permute-done((f32[32,512]{1,0:T(8,128)S(1)}, f32[32,512]{1,0:T(8,128)S(1)}, u32[]{:S(2)}, u32[]{:S(2)}) %collective-permute-start.2) | collective-permute-done | bytes 65568 | tf_op jit(solution)/shard_map/ppermute | solution.py:20
  19.5 1.3 %collective-permute-done.6.refs_4_ = f32[32,512]{1,0:T(8,128)S(1)} collective-permute-done((f32[32,512]{1,0:T(8,128)S(1)}, f32[32,512]{1,0:T(8,128)S(1)}, u32[]{:S(2)}, u32[]{:S(2)}) %collective-permute-start.6) | collective-permute-done | bytes 65568 | tf_op jit(solution)/shard_map/ppermute | solution.py:20
  20.8 2.6 %collective-permute-done.7.refs_5_ = f32[32,512]{1,0:T(8,128)S(1)} collective-permute-done((f32[32,512]{1,0:T(8,128)S(1)}, f32[32,512]{1,0:T(8,128)S(1)}, u32[]{:S(2)}, u32[]{:S(2)}) %collective-permute-start.7) | collective-permute-done | bytes 65568 | tf_op jit(solution)/shard_map/ppermute | solution.py:20
  23.4 0.0 collective-permute-done.8.refs_7_
  23.4 0.0 copy-start.9
  23.5 0.1 collective-permute-start.9
  23.5 1.7 %collective-permute-done.9.refs_5_.refs_1_ = f32[192,512]{1,0:T(8,128)S(1)} collective-permute-done((f32[192,512]{1,0:T(8,128)S(1)}, f32[192,512]{1,0:T(8,128)S(1)}, u32[]{:S(2)}, u32[]{:S(2)}) %collective-permute-start.9) | collective-permute-done | bytes 393248 | tf_op jit(solution)/shard_map/ppermute | solution.py:20
  25.2 1.4 %shard_map.133 = (f32[128,512]{1,0:T(8,128)S(1)}, f32[128,512]{1,0:T(8,128)S(1)}, f32[256,512]{1,0:T(8,128)S(1)}, f32[256,512]{1,0:T(8,128)S(1)}, f32[256,512]{1...) custom-call(s32[256]{0:T(256)S(1)} %copy-done.8, s32[256]{0:T(256)S(1)} %copy-done.9, ...), custom_call_target="tpu_custom_call" | custom-call | bytes 4065280 | tf_op jit(solution)/shard_map/pallas_call | solution.py:34
  26.7 0.2 collective-permute-start.10
  26.9 1.1 %shard_map.134 = (f32[128,512]{1,0:T(8,128)S(1)}, f32[128,512]{1,0:T(8,128)S(1)}) custom-call(s32[256]{0:T(256)S(1)} %copy-done.8, s32[256]{0:T(256)S(1)} %copy-done.10, s32[256]{0:T(256)S(1)} %copy-done.9, f32[128,512]{1,0:T(8,128)S(1)} %copy-done, f32[256,512]{1,0:T(8,128)S(1)} %shard_map.129.after_ref.rot_ref, f32[192,512]{1,0:T(8,128)S(1)} %shard_map.132.refs_4_.refs_0_, ...), custom_call_target="tpu_custom_call" | custom-call | bytes 4066304 | tf_op jit(solution)/shard_map/pallas_call | solution.py:34
  28.0 0.3 collective-permute-done.10.theirs
  28.3 0.1 shard_map.135
  28.3 1.8 %collective-permute-start.18 = (f32[128,512]{1,0:T(8,128)S(1)}, f32[128,512]{1,0:T(8,128)S(1)}, u32[]{:S(2)}, u32[]{:S(2)}) collective-permute-start(f32[128,512]{1,0:T(8,128)S(1)} %get-tuple-element.47), channel_id=1, source_target_pairs={{0,8},{1,17},{2,10},{3,19},{4,12},{5,21},{6,14},{7,23},{8,0},{9,25... | collective-permute-start | bytes 786440 | tf_op jit(solution)/shard_map/ppermute | solution.py:28
  30.2 0.8 %collective-permute-start.11 = (f32[64,512]{1,0:T(8,128)S(1)}, f32[64,512]{1,0:T(8,128)S(1)}, u32[]{:S(2)}, u32[]{:S(2)}) collective-permute-start(f32[64,512]{1,0:T(8,128)S(1)} %get-tuple-element.40), channel_id=1, source_target_pairs={{0,4},{1,5},{2,6},{3,7},{4,0},{5,1},{6,2},{7,3},{8,12},{9,13},{10,... | collective-permute-start | bytes 393224 | tf_op jit(solution)/shard_map/ppermute | solution.py:20
  31.0 1.8 %collective-permute-start.12 = (f32[64,512]{1,0:T(8,128)S(1)}, f32[64,512]{1,0:T(8,128)S(1)}, u32[]{:S(2)}, u32[]{:S(2)}) collective-permute-start(f32[64,512]{1,0:T(8,128)S(1)} %get-tuple-element.41), channel_id=1, source_target_pairs={{0,2},{1,3},{2,0},{3,1},{4,6},{5,7},{6,4},{7,5},{8,10},{9,11},{10,... | collective-permute-start | bytes 393224 | tf_op jit(solution)/shard_map/ppermute | solution.py:20
  32.8 1.8 %collective-permute-start.13 = (f32[64,512]{1,0:T(8,128)S(1)}, f32[64,512]{1,0:T(8,128)S(1)}, u32[]{:S(2)}, u32[]{:S(2)}) collective-permute-start(f32[64,512]{1,0:T(8,128)S(1)} %get-tuple-element.43), channel_id=1, source_target_pairs={{0,6},{1,7},{2,4},{3,5},{4,2},{5,3},{6,0},{7,1},{8,14},{9,15},{10,... | collective-permute-start | bytes 393224 | tf_op jit(solution)/shard_map/ppermute | solution.py:20
  34.6 0.2 collective-permute-done.18
  34.8 1.9 %collective-permute-start.19 = (f32[128,512]{1,0:T(8,128)S(1)}, f32[128,512]{1,0:T(8,128)S(1)}, u32[]{:S(2)}, u32[]{:S(2)}) collective-permute-start(f32[128,512]{1,0:T(8,128)S(1)} %add.3.refs_11_), channel_id=1, source_target_pairs={{0,16},{1,9},{2,18},{3,11},{4,20},{5,13},{6,22},{7,15},{8,24},{9,1... | collective-permute-start | bytes 786440 | tf_op jit(solution)/shard_map/ppermute | solution.py:28
  36.7 4.8 %collective-permute-done.11.refs_0_ = f32[64,512]{1,0:T(8,128)S(1)} collective-permute-done((f32[64,512]{1,0:T(8,128)S(1)}, f32[64,512]{1,0:T(8,128)S(1)}, u32[]{:S(2)}, u32[]{:S(2)}) %collective-permute-start.11) | collective-permute-done | bytes 131104 | tf_op jit(solution)/shard_map/ppermute | solution.py:20
  41.5 0.1 collective-permute-done.12.refs_1_
  41.7 0.0 copy-start.6
  41.7 0.1 collective-permute-start.14
  41.8 1.6 %collective-permute-start.15 = (f32[32,512]{1,0:T(8,128)S(1)}, f32[32,512]{1,0:T(8,128)S(1)}, u32[]{:S(2)}, u32[]{:S(2)}) collective-permute-start(f32[32,512]{1,0:T(8,128)S(1)} %get-tuple-element.46.refs_7_), channel_id=1, source_target_pairs={{0,8},{8,0},{16,24},{24,16},{1,9},{9,1},{17,25},{25,17},{2,10},{10... | collective-permute-start | bytes 196616 | tf_op jit(solution)/shard_map/ppermute | solution.py:20
  43.4 0.5 %collective-permute-start.16 = (f32[32,512]{1,0:T(8,128)S(1)}, f32[32,512]{1,0:T(8,128)S(1)}, u32[]{:S(2)}, u32[]{:S(2)}) collective-permute-start(f32[32,512]{1,0:T(8,128)S(1)} %get-tuple-element.46.refs_7_), channel_id=1, source_target_pairs={{0,16},{8,24},{16,0},{24,8},{1,17},{9,25},{17,1},{25,9},{2,18},{10... | collective-permute-start | bytes 196616 | tf_op jit(solution)/shard_map/ppermute | solution.py:20
  43.9 1.5 %collective-permute-start.17 = (f32[32,512]{1,0:T(8,128)S(1)}, f32[32,512]{1,0:T(8,128)S(1)}, u32[]{:S(2)}, u32[]{:S(2)}) collective-permute-start(f32[32,512]{1,0:T(8,128)S(1)} %get-tuple-element.46.refs_7_), channel_id=1, source_target_pairs={{0,24},{8,16},{16,8},{24,0},{1,25},{9,17},{17,9},{25,1},{2,26},{10... | collective-permute-start | bytes 196616 | tf_op jit(solution)/shard_map/ppermute | solution.py:20
  45.4 1.0 %collective-permute-done.15.refs_8_ = f32[32,512]{1,0:T(8,128)S(1)} collective-permute-done((f32[32,512]{1,0:T(8,128)S(1)}, f32[32,512]{1,0:T(8,128)S(1)}, u32[]{:S(2)}, u32[]{:S(2)}) %collective-permute-start.15) | collective-permute-done | bytes 65568 | tf_op jit(solution)/shard_map/ppermute | solution.py:20
  46.3 2.0 %collective-permute-done.16.refs_9_ = f32[32,512]{1,0:T(8,128)S(1)} collective-permute-done((f32[32,512]{1,0:T(8,128)S(1)}, f32[32,512]{1,0:T(8,128)S(1)}, u32[]{:S(2)}, u32[]{:S(2)}) %collective-permute-start.16) | collective-permute-done | bytes 65568 | tf_op jit(solution)/shard_map/ppermute | solution.py:20
  48.3 0.7 %collective-permute-done.17.refs_10_ = f32[32,512]{1,0:T(8,128)S(1)} collective-permute-done((f32[32,512]{1,0:T(8,128)S(1)}, f32[32,512]{1,0:T(8,128)S(1)}, u32[]{:S(2)}, u32[]{:S(2)}) %collective-permute-start.17) | collective-permute-done | bytes 65568 | tf_op jit(solution)/shard_map/ppermute | solution.py:20
  49.0 0.0 collective-permute-done.14.refs_6_
  49.0 0.0 collective-permute-done.19.refs_12_
  49.1 1.3 %shard_map.137 = (f32[128,512]{1,0:T(8,128)}, f32[128,512]{1,0:T(8,128)}, f32[128,512]{1,0:T(8,128)}, f32[128,512]{1,0:T(8,128)}) custom-call(s32[1]{0:T(128)S(6)} %copy.14.part_ref.refs_0_, s32[1,8,16]{2,1,0:T(8,128)S(1)} %copy-done.6, s32[8,32]{1,0:T(8,128)S(1)} %copy-done.7, f32[128,512]{1,0:T(8,128)S(1)} %copy-done.1, f32[128,512]{1,0:T(8,128)S(1)} %copy-done.3, ...), custom_call_target="tpu_custom_call" | custom-call | bytes 3147268 | tf_op jit(solution)/shard_map/pallas_call | solution.py:34
  (26 shorter events, 0.2 us)
Async XLA Ops:
  0.6 11.9 %copy-start = (f32[128,512]{1,0:T(8,128)S(1)}, f32[128,512]{1,0:T(8,128)}, u32[]{:S(2)}) copy-start(f32[128,512]{1,0:T(8,128)} %refs_13_.1) | copy-start | bytes 786436
  2.7 10.1 %collective-permute-start = (f32[32,512]{1,0:T(8,128)}, f32[32,512]{1,0:T(8,128)S(1)}, u32[]{:S(2)}, u32[]{:S(2)}) collective-permute-start(f32[32,512]{1,0:T(8,128)} %get-tuple-element.27), channel_id=1, source_target_pairs={{0,2},{1,3},{2,0},{3,1},{4,6},{5,7},{6,4},{7,5},{8,10},{9,11},{10,... | collective-permute-start | bytes 196616 | tf_op jit(solution)/shard_map/ppermute | solution.py:20
  5.8 7.6 %collective-permute-start.3 = (f32[32,512]{1,0:T(8,128)}, f32[32,512]{1,0:T(8,128)S(1)}, u32[]{:S(2)}, u32[]{:S(2)}) collective-permute-start(f32[32,512]{1,0:T(8,128)} %get-tuple-element.30.refs_0_), channel_id=1, source_target_pairs={{0,8},{8,0},{16,24},{24,16},{1,9},{9,1},{17,25},{25,17},{2,10},{10... | collective-permute-start | bytes 196616 | tf_op jit(solution)/shard_map/ppermute | solution.py:20
  7.3 6.1 %collective-permute-start.4 = (f32[32,512]{1,0:T(8,128)}, f32[32,512]{1,0:T(8,128)S(1)}, u32[]{:S(2)}, u32[]{:S(2)}) collective-permute-start(f32[32,512]{1,0:T(8,128)} %get-tuple-element.30.refs_0_), channel_id=1, source_target_pairs={{0,16},{8,24},{16,0},{24,8},{1,17},{9,25},{17,1},{25,9},{2,18},{10... | collective-permute-start | bytes 196616 | tf_op jit(solution)/shard_map/ppermute | solution.py:20
  8.8 5.4 %collective-permute-start.5 = (f32[32,512]{1,0:T(8,128)}, f32[32,512]{1,0:T(8,128)S(1)}, u32[]{:S(2)}, u32[]{:S(2)}) collective-permute-start(f32[32,512]{1,0:T(8,128)} %get-tuple-element.30.refs_0_), channel_id=1, source_target_pairs={{0,24},{8,16},{16,8},{24,0},{1,25},{9,17},{17,9},{25,1},{2,26},{10... | collective-permute-start | bytes 196616 | tf_op jit(solution)/shard_map/ppermute | solution.py:20
  9.3 3.3 %copy-start.10 = (s32[256]{0:T(256)S(1)}, s32[256]{0:T(256)}, u32[]{:S(2)}) copy-start(s32[256]{0:T(256)} %rel_index_ref.3) | copy-start | bytes 3076
  9.3 9.4 %collective-permute-start.1 = (f32[32,512]{1,0:T(8,128)}, f32[32,512]{1,0:T(8,128)S(1)}, u32[]{:S(2)}, u32[]{:S(2)}) collective-permute-start(f32[32,512]{1,0:T(8,128)} %get-tuple-element.28), channel_id=1, source_target_pairs={{0,4},{1,5},{2,6},{3,7},{4,0},{5,1},{6,2},{7,3},{8,12},{9,13},{10,... | collective-permute-start | bytes 196616 | tf_op jit(solution)/shard_map/ppermute | solution.py:20
  12.5 0.8 %copy-start.11 = (f32[32,512]{1,0:T(8,128)S(1)}, f32[32,512]{1,0:T(8,128)}, u32[]{:S(2)}) copy-start(f32[32,512]{1,0:T(8,128)} %get-tuple-element.29) | copy-start | bytes 196612
  12.6 1.6 %copy-start.5 = (f32[32,512]{1,0:T(8,128)S(1)}, f32[32,512]{1,0:T(8,128)}, u32[]{:S(2)}) copy-start(f32[32,512]{1,0:T(8,128)} %get-tuple-element.30.refs_0_) | copy-start | bytes 196612
  13.4 10.0 %copy-start.2 = (f32[32,512]{1,0:T(8,128)S(1)}, f32[32,512]{1,0:T(8,128)}, u32[]{:S(2)}) copy-start(f32[32,512]{1,0:T(8,128)} %get-tuple-element.26.refs_2_.refs_0_) | copy-start | bytes 196612
  13.4 6.1 %collective-permute-start.2 = (f32[32,512]{1,0:T(8,128)S(1)}, f32[32,512]{1,0:T(8,128)S(1)}, u32[]{:S(2)}, u32[]{:S(2)}) collective-permute-start(f32[32,512]{1,0:T(8,128)S(1)} %copy-done.11), channel_id=1, source_target_pairs={{0,6},{1,7},{2,4},{3,5},{4,2},{5,3},{6,0},{7,1},{8,14},{9,15},{10,... | collective-permute-start | bytes 196616 | tf_op jit(solution)/shard_map/ppermute | solution.py:20
  14.2 6.6 %collective-permute-start.6 = (f32[32,512]{1,0:T(8,128)S(1)}, f32[32,512]{1,0:T(8,128)S(1)}, u32[]{:S(2)}, u32[]{:S(2)}) collective-permute-start(f32[32,512]{1,0:T(8,128)S(1)} %shard_map.131.refs_6_), channel_id=1, source_target_pairs={{0,6},{1,7},{2,4},{3,5},{4,2},{5,3},{6,0},{7,1},{8,14},{9,15},{10,... | collective-permute-start | bytes 196616 | tf_op jit(solution)/shard_map/ppermute | solution.py:20
  17.3 6.1 %collective-permute-start.7 = (f32[32,512]{1,0:T(8,128)S(1)}, f32[32,512]{1,0:T(8,128)S(1)}, u32[]{:S(2)}, u32[]{:S(2)}) collective-permute-start(f32[32,512]{1,0:T(8,128)S(1)} %shard_map.131.refs_6_), channel_id=1, source_target_pairs={{0,4},{1,5},{2,6},{3,7},{4,0},{5,1},{6,2},{7,3},{8,12},{9,13},{10,... | collective-permute-start | bytes 196616 | tf_op jit(solution)/shard_map/ppermute | solution.py:20
  17.3 6.1 %collective-permute-start.8 = (f32[32,512]{1,0:T(8,128)S(1)}, f32[32,512]{1,0:T(8,128)S(1)}, u32[]{:S(2)}, u32[]{:S(2)}) collective-permute-start(f32[32,512]{1,0:T(8,128)S(1)} %shard_map.131.refs_6_), channel_id=1, source_target_pairs={{0,2},{1,3},{2,0},{3,1},{4,6},{5,7},{6,4},{7,5},{8,10},{9,11},{10,... | collective-permute-start | bytes 196616 | tf_op jit(solution)/shard_map/ppermute | solution.py:20
  23.4 1.8 %copy-start.8 = (s32[256]{0:T(256)S(1)}, s32[256]{0:T(256)}, u32[]{:S(2)}) copy-start(s32[256]{0:T(256)} %head_ref.3) | copy-start | bytes 3076
  23.4 1.8 %copy-start.9 = (s32[256]{0:T(256)S(1)}, s32[256]{0:T(256)}, u32[]{:S(2)}) copy-start(s32[256]{0:T(256)} %tail_ref.3) | copy-start | bytes 3076
  23.5 1.8 %collective-permute-start.9 = (f32[192,512]{1,0:T(8,128)S(1)}, f32[192,512]{1,0:T(8,128)S(1)}, u32[]{:S(2)}, u32[]{:S(2)}) collective-permute-start(f32[192,512]{1,0:T(8,128)S(1)} %shard_map.132.refs_4_.refs_0_), channel_id=1, source_target_pairs={{0,1},{1,0},{2,3},{3,2},{4,5},{5,4},{6,7},{7,6},{8,9},{9,8},{10,11... | collective-permute-start | bytes 1179656 | tf_op jit(solution)/shard_map/ppermute | solution.py:20
  26.7 1.6 %collective-permute-start.10 = (f32[128,512]{1,0:T(8,128)S(1)}, f32[128,512]{1,0:T(8,128)S(1)}, u32[]{:S(2)}, u32[]{:S(2)}) collective-permute-start(f32[128,512]{1,0:T(8,128)S(1)} %get-tuple-element.32), channel_id=1, source_target_pairs={{0,1},{1,0},{2,3},{3,2},{4,5},{5,4},{6,7},{7,6},{8,9},{9,8},{10,11... | collective-permute-start | bytes 786440 | tf_op jit(solution)/shard_map/ppermute | solution.py:20
  28.3 6.4 %collective-permute-start.18 = (f32[128,512]{1,0:T(8,128)S(1)}, f32[128,512]{1,0:T(8,128)S(1)}, u32[]{:S(2)}, u32[]{:S(2)}) collective-permute-start(f32[128,512]{1,0:T(8,128)S(1)} %get-tuple-element.47), channel_id=1, source_target_pairs={{0,8},{1,17},{2,10},{3,19},{4,12},{5,21},{6,14},{7,23},{8,0},{9,25... | collective-permute-start | bytes 786440 | tf_op jit(solution)/shard_map/ppermute | solution.py:28
  30.2 11.4 %collective-permute-start.11 = (f32[64,512]{1,0:T(8,128)S(1)}, f32[64,512]{1,0:T(8,128)S(1)}, u32[]{:S(2)}, u32[]{:S(2)}) collective-permute-start(f32[64,512]{1,0:T(8,128)S(1)} %get-tuple-element.40), channel_id=1, source_target_pairs={{0,4},{1,5},{2,6},{3,7},{4,0},{5,1},{6,2},{7,3},{8,12},{9,13},{10,... | collective-permute-start | bytes 393224 | tf_op jit(solution)/shard_map/ppermute | solution.py:20
  31.0 10.7 %collective-permute-start.12 = (f32[64,512]{1,0:T(8,128)S(1)}, f32[64,512]{1,0:T(8,128)S(1)}, u32[]{:S(2)}, u32[]{:S(2)}) collective-permute-start(f32[64,512]{1,0:T(8,128)S(1)} %get-tuple-element.41), channel_id=1, source_target_pairs={{0,2},{1,3},{2,0},{3,1},{4,6},{5,7},{6,4},{7,5},{8,10},{9,11},{10,... | collective-permute-start | bytes 393224 | tf_op jit(solution)/shard_map/ppermute | solution.py:20
  32.8 8.9 %collective-permute-start.13 = (f32[64,512]{1,0:T(8,128)S(1)}, f32[64,512]{1,0:T(8,128)S(1)}, u32[]{:S(2)}, u32[]{:S(2)}) collective-permute-start(f32[64,512]{1,0:T(8,128)S(1)} %get-tuple-element.43), channel_id=1, source_target_pairs={{0,6},{1,7},{2,4},{3,5},{4,2},{5,3},{6,0},{7,1},{8,14},{9,15},{10,... | collective-permute-start | bytes 393224 | tf_op jit(solution)/shard_map/ppermute | solution.py:20
  34.8 14.3 %copy-start.4 = (f32[128,512]{1,0:T(8,128)S(1)}, f32[128,512]{1,0:T(8,128)}, u32[]{:S(2)}) copy-start(f32[128,512]{1,0:T(8,128)} %refs_14_.1) | copy-start | bytes 786436
  34.8 14.3 %copy-start.7 = (s32[8,32]{1,0:T(8,128)S(1)}, s32[8,32]{1,0:T(8,128)}, u32[]{:S(2)}) copy-start(s32[8,32]{1,0:T(8,128)} %refs_2_.1) | copy-start | bytes 3076
  34.8 14.2 %collective-permute-start.19 = (f32[128,512]{1,0:T(8,128)S(1)}, f32[128,512]{1,0:T(8,128)S(1)}, u32[]{:S(2)}, u32[]{:S(2)}) collective-permute-start(f32[128,512]{1,0:T(8,128)S(1)} %add.3.refs_11_), channel_id=1, source_target_pairs={{0,16},{1,9},{2,18},{3,11},{4,20},{5,13},{6,22},{7,15},{8,24},{9,1... | collective-permute-start | bytes 786440 | tf_op jit(solution)/shard_map/ppermute | solution.py:28
  41.7 7.4 %copy-start.1 = (f32[128,512]{1,0:T(8,128)S(1)}, f32[128,512]{1,0:T(8,128)}, u32[]{:S(2)}) copy-start(f32[128,512]{1,0:T(8,128)} %refs_3_.1) | copy-start | bytes 786436
  41.7 7.4 %copy-start.3 = (f32[128,512]{1,0:T(8,128)S(1)}, f32[128,512]{1,0:T(8,128)}, u32[]{:S(2)}) copy-start(f32[128,512]{1,0:T(8,128)} %refs_4_.1) | copy-start | bytes 786436
  41.7 7.4 %copy-start.6 = (s32[1,8,16]{2,1,0:T(8,128)S(1)}, s32[1,8,16]{2,1,0:T(8,128)}, u32[]{:S(2)}) copy-start(s32[1,8,16]{2,1,0:T(8,128)} %refs_1_.1) | copy-start | bytes 1540
  41.7 7.3 %collective-permute-start.14 = (f32[64,512]{1,0:T(8,128)S(1)}, f32[64,512]{1,0:T(8,128)S(1)}, u32[]{:S(2)}, u32[]{:S(2)}) collective-permute-start(f32[64,512]{1,0:T(8,128)S(1)} %get-tuple-element.45), channel_id=1, source_target_pairs={{0,1},{1,0},{2,3},{3,2},{4,5},{5,4},{6,7},{7,6},{8,9},{9,8},{10,11... | collective-permute-start | bytes 393224 | tf_op jit(solution)/shard_map/ppermute | solution.py:20
  41.8 4.5 %collective-permute-start.15 = (f32[32,512]{1,0:T(8,128)S(1)}, f32[32,512]{1,0:T(8,128)S(1)}, u32[]{:S(2)}, u32[]{:S(2)}) collective-permute-start(f32[32,512]{1,0:T(8,128)S(1)} %get-tuple-element.46.refs_7_), channel_id=1, source_target_pairs={{0,8},{8,0},{16,24},{24,16},{1,9},{9,1},{17,25},{25,17},{2,10},{10... | collective-permute-start | bytes 196616 | tf_op jit(solution)/shard_map/ppermute | solution.py:20
  43.4 5.0 %collective-permute-start.16 = (f32[32,512]{1,0:T(8,128)S(1)}, f32[32,512]{1,0:T(8,128)S(1)}, u32[]{:S(2)}, u32[]{:S(2)}) collective-permute-start(f32[32,512]{1,0:T(8,128)S(1)} %get-tuple-element.46.refs_7_), channel_id=1, source_target_pairs={{0,16},{8,24},{16,0},{24,8},{1,17},{9,25},{17,1},{25,9},{2,18},{10... | collective-permute-start | bytes 196616 | tf_op jit(solution)/shard_map/ppermute | solution.py:20
  43.9 5.2 %collective-permute-start.17 = (f32[32,512]{1,0:T(8,128)S(1)}, f32[32,512]{1,0:T(8,128)S(1)}, u32[]{:S(2)}, u32[]{:S(2)}) collective-permute-start(f32[32,512]{1,0:T(8,128)S(1)} %get-tuple-element.46.refs_7_), channel_id=1, source_target_pairs={{0,24},{8,16},{16,8},{24,0},{1,25},{9,17},{17,9},{25,1},{2,26},{10... | collective-permute-start | bytes 196616 | tf_op jit(solution)/shard_map/ppermute | solution.py:20

commit v7 on v6

--- a/solution.py
+++ b/solution.py
@@ -26,6 +26,10 @@
         for r in range(n_rel):
             pairs.append((i * n_rel + r, (i ^ (odd if r % 2 else even)) * n_rel + r))
     return lax.ppermute(block, ("dom", "rel"), pairs)
+
+
+def other_way(step):
+    return step ^ 3 if step % 4 in (1, 2) else step
 
 
 def call(body, outs, specs, args, flops=0, scratch=(), limit=40 * 1024):
@@ -201,12 +205,14 @@
     rel_ref[...] = join([inverse * (g - u * along) for u, g in zip(unit, grad_unit)])
 
 
-def select_kernel(part_ref, after_ref, *refs):
+def select_kernel(part_ref, *refs):
     blocks, out_ref = refs[: lax.axis_size("dom")], refs[-1]
     source = lax.axis_index("dom") ^ part_ref[0]
     picked = blocks[0][...]
+    first_core = lax.axis_index("rel") % 2 == 0
     for s, ref in enumerate(blocks):
-        picked = jnp.where(source == s, ref[...], picked)
+        step = jnp.where(first_core, s, other_way(s))
+        picked = jnp.where(source == step, ref[...], picked)
     out_ref[...] = picked
 
 
@@ -309,22 +315,24 @@
             pltpu.SemaphoreType.DMA((3,)),
         ],
     )
-    spread = [own_negs] + [exchange(own_negs, "dom", n_dom, s) for s in range(1, n_dom)]
+    spread = [own_negs] + [
+        cross_exchange(own_negs, n_dom, n_rel, s, other_way(s)) for s in range(1, n_dom)
+    ]
     arrived = [parcels[0]] + [exchange(parcels[s], "rel", n_rel, 2 * s) for s in range(1, n_chip)]
     (rot,) = call(rotation_kernel, [(trips, width)], [VMEM] * 2, (trip_rel, relation))
     (picked,) = call(
         select_kernel,
         [own_negs.shape],
-        [SMEM, VMEM] + [VMEM] * (n_dom + len(arrived[1:2])),
-        (neg_part, rot, *spread, *arrived[1:2]),
+        [SMEM] + [VMEM] * (n_dom + len(arrived[1:2])),
+        (neg_part, *spread, *arrived[1:2]),
     )
     negs = [picked] + [exchange(picked, "rel", n_rel, 2 * s) for s in range(1, n_chip)]
     neg_order = [*range(2, n_chip)][::-1] + [*range(min(n_chip, 2))]
     (stacked,) = call(
         functools.partial(stack_kernel, order, neg_order),
         [(n_chip * (n_neg + slots), width)],
-        [VMEM] * (2 * n_chip),
-        (*[arrived[s] for s in order], *[negs[s] for s in neg_order]),
+        [VMEM] * (2 * n_chip + 1),
+        (*[arrived[s] for s in order], *[negs[s] for s in neg_order], rot),
     )
     swapped = exchange(stacked, "rel", n_rel, 1)
 
@@ -361,7 +369,9 @@
         [VMEM] * n_chip,
         [back[s] for s in back_order],
     )
-    neg_shares = [neg_share] + [exchange(neg_share, "dom", n_dom, s) for s in range(1, n_dom)]
+    neg_shares = [neg_share] + [
+        cross_exchange(neg_share, n_dom, n_rel, s, other_way(s)) for s in range(n_dom - 1, 0, -1)
+    ]
     cross = exchange(cross, "rel", n_rel, 1)
 
     new_entity, new_entity_acc, new_relation, new_relation_acc = call(

time: 50.7 us -> 50.6 us (level)
    ppermute x18 -> x12, starting transfers between devices: 21.9 us -> 14.9 us  [exchange(): return lax.ppermute(block, axis, [(i, i ^ step) for i in range(size)])]
    ppermute x2 -> x8, starting transfers between devices: 3.71 us -> 10.3 us  [cross_exchange(): return lax.ppermute(block, ('dom', 'rel'), pairs)]
    ppermute x2 -> x8, waiting for transfers between devices: 0.21 us -> 5.69 us  [cross_exchange(): return lax.ppermute(block, ('dom', 'rel'), pairs)]
    ppermute x18 -> x12, waiting for transfers between devices: 16.1 us -> 10.8 us  [exchange(): return lax.ppermute(block, axis, [(i, i ^ step) for i in range(size)])]
  transfers between devices with their start and end apart: 20 -> 20, of which waited for: 12 -> 11; matrix products, arithmetic and copies ran while one was open for 0% -> 0% of each run, Pallas kernels for 3% -> 3%
where the time goes in v7:
time: 50.6 us; the launch traced here: 50.4 us
  starting transfers between devices  25.3 us (50%)
  waiting for transfers between devices  16.4 us (32%)
  Pallas kernels  6.27 us (12%)
  between operations  1.49 us (3%)
  local copies, waits for them, and re-layouts  0.89 us (2%)
    ppermute x12, starting transfers between devices, exchange(): return lax.ppermute(block, axis, [(i, i ^ step) for i in range(size)])  14.9 us
    ppermute x12, waiting for transfers between devices, exchange(): return lax.ppermute(block, axis, [(i, i ^ step) for i in range(size)])  10.8 us
    ppermute x8, starting transfers between devices, cross_exchange(): return lax.ppermute(block, ('dom', 'rel'), pairs)  10.3 us
    pallas_call x9, Pallas kernels, call(): pl.pallas_call(body, out_shape=shapes, in_specs=specs, out_specs=[VMEM] *...  6.27 us
    ppermute x8, waiting for transfers between devices, cross_exchange(): return lax.ppermute(block, ('dom', 'rel'), pairs)  5.69 us
  transfers between devices with their start and end apart: 20, of which 11 were waited for; matrix products, arithmetic and copies ran while one was open for 0% of the time, Pallas kernels for 3%

profile of v7, /device:TPU:0, one launch (start us, length us, event | category | flops | bytes accessed | tf_op | source)
XLA Modules:
  0.0 50.4 jit_solution(10994175165863259749)
XLA Ops:
  0.6 2.0 %shard_map.130 = (f32[32,512]{1,0:T(8,128)}, f32[32,512]{1,0:T(8,128)}, f32[32,512]{1,0:T(8,128)}, f32[32,512]{1,0:T(8,128)}, f32[32,512]{1,0:T(8,128)}) custom-call(s32[1,8,16]{2,1,0:T(8,128)} %refs_1_.1, s32[8,32]{1,0:T(8,128)} %refs_2_.1, f32[128,512]{1,0:T(8,128)} %refs_3_.1), custom_call_target="tpu_custom_call" | custom-call | bytes 591360 | tf_op jit(solution)/shard_map/pallas_call | solution.py:38
  2.6 0.0 copy-start
  2.7 3.1 %collective-permute-start = (f32[32,512]{1,0:T(8,128)}, f32[32,512]{1,0:T(8,128)S(1)}, u32[]{:S(2)}, u32[]{:S(2)}) collective-permute-start(f32[32,512]{1,0:T(8,128)} %get-tuple-element.27), channel_id=1, source_target_pairs={{0,2},{1,3},{2,0},{3,1},{4,6},{5,7},{6,4},{7,5},{8,10},{9,11},{10,... | collective-permute-start | bytes 196616 | tf_op jit(solution)/shard_map/ppermute | solution.py:20
  5.7 1.5 %collective-permute-start.3 = (f32[32,512]{1,0:T(8,128)}, f32[32,512]{1,0:T(8,128)S(1)}, u32[]{:S(2)}, u32[]{:S(2)}) collective-permute-start(f32[32,512]{1,0:T(8,128)} %get-tuple-element.30.refs_0_), channel_id=1, source_target_pairs={{0,8},{1,17},{2,10},{3,19},{4,12},{5,21},{6,14},{7,23},{8,0},{9,25... | collective-permute-start | bytes 196616 | tf_op jit(solution)/shard_map/ppermute | solution.py:28
  7.2 1.5 %collective-permute-start.4 = (f32[32,512]{1,0:T(8,128)}, f32[32,512]{1,0:T(8,128)S(1)}, u32[]{:S(2)}, u32[]{:S(2)}) collective-permute-start(f32[32,512]{1,0:T(8,128)} %get-tuple-element.30.refs_0_), channel_id=1, source_target_pairs={{0,16},{1,9},{2,18},{3,11},{4,20},{5,13},{6,22},{7,15},{8,24},{9,1... | collective-permute-start | bytes 196616 | tf_op jit(solution)/shard_map/ppermute | solution.py:28
  8.8 0.5 collective-permute-start.5
  9.2 2.6 %collective-permute-start.1 = (f32[32,512]{1,0:T(8,128)}, f32[32,512]{1,0:T(8,128)S(1)}, u32[]{:S(2)}, u32[]{:S(2)}) collective-permute-start(f32[32,512]{1,0:T(8,128)} %get-tuple-element.28), channel_id=1, source_target_pairs={{0,4},{1,5},{2,6},{3,7},{4,0},{5,1},{6,2},{7,3},{8,12},{9,13},{10,... | collective-permute-start | bytes 196616 | tf_op jit(solution)/shard_map/ppermute | solution.py:20
  12.5 0.1 collective-permute-start.2
  12.6 0.0 collective-permute-done.3.refs_1_
  12.6 0.0 collective-permute-done.4.refs_2_
  12.6 1.5 %collective-permute-done.5.refs_3_ = f32[32,512]{1,0:T(8,128)S(1)} collective-permute-done((f32[32,512]{1,0:T(8,128)}, f32[32,512]{1,0:T(8,128)S(1)}, u32[]{:S(2)}, u32[]{:S(2)}) %collective-permute-start.5) | collective-permute-done | bytes 65568 | tf_op jit(solution)/shard_map/ppermute | solution.py:28
  14.1 0.8 %copy-done.5 = f32[32,512]{1,0:T(8,128)S(1)} copy-done((f32[32,512]{1,0:T(8,128)S(1)}, f32[32,512]{1,0:T(8,128)}, u32[]{:S(2)}) %copy-start.5) | copy-done | bytes 65560
  15.0 0.0 copy-start.4
  15.0 2.5 %collective-permute-start.6 = (f32[32,512]{1,0:T(8,128)S(1)}, f32[32,512]{1,0:T(8,128)S(1)}, u32[]{:S(2)}, u32[]{:S(2)}) collective-permute-start(f32[32,512]{1,0:T(8,128)S(1)} %shard_map.131.refs_6_), channel_id=1, source_target_pairs={{0,6},{1,7},{2,4},{3,5},{4,2},{5,3},{6,0},{7,1},{8,14},{9,15},{10,... | collective-permute-start | bytes 196616 | tf_op jit(solution)/shard_map/ppermute | solution.py:20
  17.6 0.2 collective-permute-start.7
  17.7 1.7 %collective-permute-start.8 = (f32[32,512]{1,0:T(8,128)S(1)}, f32[32,512]{1,0:T(8,128)S(1)}, u32[]{:S(2)}, u32[]{:S(2)}) collective-permute-start(f32[32,512]{1,0:T(8,128)S(1)} %shard_map.131.refs_6_), channel_id=1, source_target_pairs={{0,2},{1,3},{2,0},{3,1},{4,6},{5,7},{6,4},{7,5},{8,10},{9,11},{10,... | collective-permute-start | bytes 196616 | tf_op jit(solution)/shard_map/ppermute | solution.py:20
  19.5 0.3 shard_map.129.refs_8_.rot_ref
  19.7 0.0 collective-permute-done.1.refs_0_.refs_2_
  19.8 0.0 collective-permute-done.2.refs_1_.refs_3_
  19.8 1.5 %collective-permute-done.6.refs_4_ = f32[32,512]{1,0:T(8,128)S(1)} collective-permute-done((f32[32,512]{1,0:T(8,128)S(1)}, f32[32,512]{1,0:T(8,128)S(1)}, u32[]{:S(2)}, u32[]{:S(2)}) %collective-permute-start.6) | collective-permute-done | bytes 65568 | tf_op jit(solution)/shard_map/ppermute | solution.py:20
  21.3 2.1 %collective-permute-done.7.refs_5_ = f32[32,512]{1,0:T(8,128)S(1)} collective-permute-done((f32[32,512]{1,0:T(8,128)S(1)}, f32[32,512]{1,0:T(8,128)S(1)}, u32[]{:S(2)}, u32[]{:S(2)}) %collective-permute-start.7) | collective-permute-done | bytes 65568 | tf_op jit(solution)/shard_map/ppermute | solution.py:20
  23.4 0.0 collective-permute-done.8.refs_7_
  23.4 0.0 copy-start.9
  23.5 0.1 collective-permute-start.9
  23.6 1.7 %collective-permute-done.9.refs_5_.refs_1_ = f32[192,512]{1,0:T(8,128)S(1)} collective-permute-done((f32[192,512]{1,0:T(8,128)S(1)}, f32[192,512]{1,0:T(8,128)S(1)}, u32[]{:S(2)}, u32[]{:S(2)}) %collective-permute-start.9) | collective-permute-done | bytes 393248 | tf_op jit(solution)/shard_map/ppermute | solution.py:20
  25.3 1.4 %shard_map.133 = (f32[128,512]{1,0:T(8,128)S(1)}, f32[128,512]{1,0:T(8,128)S(1)}, f32[256,512]{1,0:T(8,128)S(1)}, f32[256,512]{1,0:T(8,128)S(1)}, f32[256,512]{1...) custom-call(s32[256]{0:T(256)S(1)} %copy-done.8, s32[256]{0:T(256)S(1)} %copy-done.9, ...), custom_call_target="tpu_custom_call" | custom-call | bytes 4065280 | tf_op jit(solution)/shard_map/pallas_call | solution.py:38
  26.7 0.2 collective-permute-start.10
  26.9 1.1 %shard_map.134 = (f32[128,512]{1,0:T(8,128)S(1)}, f32[128,512]{1,0:T(8,128)S(1)}) custom-call(s32[256]{0:T(256)S(1)} %copy-done.8, s32[256]{0:T(256)S(1)} %copy-done.10, s32[256]{0:T(256)S(1)} %copy-done.9, f32[128,512]{1,0:T(8,128)S(1)} %copy-done, f32[256,512]{1,0:T(8,128)S(1)} %shard_map.129.refs_8_.rot_ref, f32[192,512]{1,0:T(8,128)S(1)} %shard_map.132.refs_4_.refs_0_, ...), custom_call_target="tpu_custom_call" | custom-call | bytes 4066304 | tf_op jit(solution)/shard_map/pallas_call | solution.py:38
  28.0 0.3 collective-permute-done.10.theirs
  28.3 0.1 shard_map.135
  28.4 1.6 %collective-permute-start.18 = (f32[128,512]{1,0:T(8,128)S(1)}, f32[128,512]{1,0:T(8,128)S(1)}, u32[]{:S(2)}, u32[]{:S(2)}) collective-permute-start(f32[128,512]{1,0:T(8,128)S(1)} %get-tuple-element.47), channel_id=1, source_target_pairs={{0,8},{1,17},{2,10},{3,19},{4,12},{5,21},{6,14},{7,23},{8,0},{9,25... | collective-permute-start | bytes 786440 | tf_op jit(solution)/shard_map/ppermute | solution.py:28
  30.0 1.0 %collective-permute-start.11 = (f32[64,512]{1,0:T(8,128)S(1)}, f32[64,512]{1,0:T(8,128)S(1)}, u32[]{:S(2)}, u32[]{:S(2)}) collective-permute-start(f32[64,512]{1,0:T(8,128)S(1)} %get-tuple-element.40), channel_id=1, source_target_pairs={{0,4},{1,5},{2,6},{3,7},{4,0},{5,1},{6,2},{7,3},{8,12},{9,13},{10,... | collective-permute-start | bytes 393224 | tf_op jit(solution)/shard_map/ppermute | solution.py:20
  31.0 1.6 %collective-permute-start.12 = (f32[64,512]{1,0:T(8,128)S(1)}, f32[64,512]{1,0:T(8,128)S(1)}, u32[]{:S(2)}, u32[]{:S(2)}) collective-permute-start(f32[64,512]{1,0:T(8,128)S(1)} %get-tuple-element.41), channel_id=1, source_target_pairs={{0,2},{1,3},{2,0},{3,1},{4,6},{5,7},{6,4},{7,5},{8,10},{9,11},{10,... | collective-permute-start | bytes 393224 | tf_op jit(solution)/shard_map/ppermute | solution.py:20
  32.6 1.8 %collective-permute-start.13 = (f32[64,512]{1,0:T(8,128)S(1)}, f32[64,512]{1,0:T(8,128)S(1)}, u32[]{:S(2)}, u32[]{:S(2)}) collective-permute-start(f32[64,512]{1,0:T(8,128)S(1)} %get-tuple-element.43), channel_id=1, source_target_pairs={{0,6},{1,7},{2,4},{3,5},{4,2},{5,3},{6,0},{7,1},{8,14},{9,15},{10,... | collective-permute-start | bytes 393224 | tf_op jit(solution)/shard_map/ppermute | solution.py:20
  34.4 0.4 collective-permute-done.18
  34.8 1.7 %collective-permute-start.19 = (f32[128,512]{1,0:T(8,128)S(1)}, f32[128,512]{1,0:T(8,128)S(1)}, u32[]{:S(2)}, u32[]{:S(2)}) collective-permute-start(f32[128,512]{1,0:T(8,128)S(1)} %add.3.refs_11_), channel_id=1, source_target_pairs={{0,16},{1,9},{2,18},{3,11},{4,20},{5,13},{6,22},{7,15},{8,24},{9,1... | collective-permute-start | bytes 786440 | tf_op jit(solution)/shard_map/ppermute | solution.py:28
  36.5 4.8 %collective-permute-done.11.refs_0_ = f32[64,512]{1,0:T(8,128)S(1)} collective-permute-done((f32[64,512]{1,0:T(8,128)S(1)}, f32[64,512]{1,0:T(8,128)S(1)}, u32[]{:S(2)}, u32[]{:S(2)}) %collective-permute-start.11) | collective-permute-done | bytes 131104 | tf_op jit(solution)/shard_map/ppermute | solution.py:20
  41.3 0.3 collective-permute-done.12.refs_1_
  41.6 0.0 collective-permute-done.13.refs_3_
  41.7 0.0 copy-start.6
  41.7 0.1 collective-permute-start.14
  41.8 1.5 %collective-permute-start.15 = (f32[32,512]{1,0:T(8,128)S(1)}, f32[32,512]{1,0:T(8,128)S(1)}, u32[]{:S(2)}, u32[]{:S(2)}) collective-permute-start(f32[32,512]{1,0:T(8,128)S(1)} %get-tuple-element.46.refs_7_), channel_id=1, source_target_pairs={{0,24},{1,25},{2,26},{3,27},{4,28},{5,29},{6,30},{7,31},{8,16},{9,... | collective-permute-start | bytes 196616 | tf_op jit(solution)/shard_map/ppermute | solution.py:28
  43.3 1.5 %collective-permute-start.16 = (f32[32,512]{1,0:T(8,128)S(1)}, f32[32,512]{1,0:T(8,128)S(1)}, u32[]{:S(2)}, u32[]{:S(2)}) collective-permute-start(f32[32,512]{1,0:T(8,128)S(1)} %get-tuple-element.46.refs_7_), channel_id=1, source_target_pairs={{0,16},{1,9},{2,18},{3,11},{4,20},{5,13},{6,22},{7,15},{8,24},{9,1... | collective-permute-start | bytes 196616 | tf_op jit(solution)/shard_map/ppermute | solution.py:28
  44.8 0.5 %collective-permute-start.17 = (f32[32,512]{1,0:T(8,128)S(1)}, f32[32,512]{1,0:T(8,128)S(1)}, u32[]{:S(2)}, u32[]{:S(2)}) collective-permute-start(f32[32,512]{1,0:T(8,128)S(1)} %get-tuple-element.46.refs_7_), channel_id=1, source_target_pairs={{0,8},{1,17},{2,10},{3,19},{4,12},{5,21},{6,14},{7,23},{8,0},{9,25... | collective-permute-start | bytes 196616 | tf_op jit(solution)/shard_map/ppermute | solution.py:28
  45.3 2.1 %collective-permute-done.15.refs_8_ = f32[32,512]{1,0:T(8,128)S(1)} collective-permute-done((f32[32,512]{1,0:T(8,128)S(1)}, f32[32,512]{1,0:T(8,128)S(1)}, u32[]{:S(2)}, u32[]{:S(2)}) %collective-permute-start.15) | collective-permute-done | bytes 65568 | tf_op jit(solution)/shard_map/ppermute | solution.py:28
  47.4 1.2 %collective-permute-done.16.refs_9_ = f32[32,512]{1,0:T(8,128)S(1)} collective-permute-done((f32[32,512]{1,0:T(8,128)S(1)}, f32[32,512]{1,0:T(8,128)S(1)}, u32[]{:S(2)}, u32[]{:S(2)}) %collective-permute-start.16) | collective-permute-done | bytes 65568 | tf_op jit(solution)/shard_map/ppermute | solution.py:28
  48.6 0.5 collective-permute-done.17.refs_10_
  49.1 1.3 %shard_map.137 = (f32[128,512]{1,0:T(8,128)}, f32[128,512]{1,0:T(8,128)}, f32[128,512]{1,0:T(8,128)}, f32[128,512]{1,0:T(8,128)}) custom-call(s32[1]{0:T(128)S(6)} %copy.14.part_ref.refs_0_, s32[1,8,16]{2,1,0:T(8,128)S(1)} %copy-done.6, s32[8,32]{1,0:T(8,128)S(1)} %copy-done.7, f32[128,512]{1,0:T(8,128)S(1)} %copy-done.1, f32[128,512]{1,0:T(8,128)S(1)} %copy-done.2, ...), custom_call_target="tpu_custom_call" | custom-call | bytes 3147268 | tf_op jit(solution)/shard_map/pallas_call | solution.py:38
  (24 shorter events, 0.2 us)
Async XLA Ops:
  2.6 16.8 %copy-start = (f32[128,512]{1,0:T(8,128)S(1)}, f32[128,512]{1,0:T(8,128)}, u32[]{:S(2)}) copy-start(f32[128,512]{1,0:T(8,128)} %refs_13_.1) | copy-start | bytes 786436
  2.7 9.8 %collective-permute-start = (f32[32,512]{1,0:T(8,128)}, f32[32,512]{1,0:T(8,128)S(1)}, u32[]{:S(2)}, u32[]{:S(2)}) collective-permute-start(f32[32,512]{1,0:T(8,128)} %get-tuple-element.27), channel_id=1, source_target_pairs={{0,2},{1,3},{2,0},{3,1},{4,6},{5,7},{6,4},{7,5},{8,10},{9,11},{10,... | collective-permute-start | bytes 196616 | tf_op jit(solution)/shard_map/ppermute | solution.py:20
  5.7 6.8 %collective-permute-start.3 = (f32[32,512]{1,0:T(8,128)}, f32[32,512]{1,0:T(8,128)S(1)}, u32[]{:S(2)}, u32[]{:S(2)}) collective-permute-start(f32[32,512]{1,0:T(8,128)} %get-tuple-element.30.refs_0_), channel_id=1, source_target_pairs={{0,8},{1,17},{2,10},{3,19},{4,12},{5,21},{6,14},{7,23},{8,0},{9,25... | collective-permute-start | bytes 196616 | tf_op jit(solution)/shard_map/ppermute | solution.py:28
  7.2 5.3 %collective-permute-start.4 = (f32[32,512]{1,0:T(8,128)}, f32[32,512]{1,0:T(8,128)S(1)}, u32[]{:S(2)}, u32[]{:S(2)}) collective-permute-start(f32[32,512]{1,0:T(8,128)} %get-tuple-element.30.refs_0_), channel_id=1, source_target_pairs={{0,16},{1,9},{2,18},{3,11},{4,20},{5,13},{6,22},{7,15},{8,24},{9,1... | collective-permute-start | bytes 196616 | tf_op jit(solution)/shard_map/ppermute | solution.py:28
  8.8 5.4 %collective-permute-start.5 = (f32[32,512]{1,0:T(8,128)}, f32[32,512]{1,0:T(8,128)S(1)}, u32[]{:S(2)}, u32[]{:S(2)}) collective-permute-start(f32[32,512]{1,0:T(8,128)} %get-tuple-element.30.refs_0_), channel_id=1, source_target_pairs={{0,24},{1,25},{2,26},{3,27},{4,28},{5,29},{6,30},{7,31},{8,16},{9,... | collective-permute-start | bytes 196616 | tf_op jit(solution)/shard_map/ppermute | solution.py:28
  9.2 10.5 %collective-permute-start.1 = (f32[32,512]{1,0:T(8,128)}, f32[32,512]{1,0:T(8,128)S(1)}, u32[]{:S(2)}, u32[]{:S(2)}) collective-permute-start(f32[32,512]{1,0:T(8,128)} %get-tuple-element.28), channel_id=1, source_target_pairs={{0,4},{1,5},{2,6},{3,7},{4,0},{5,1},{6,2},{7,3},{8,12},{9,13},{10,... | collective-permute-start | bytes 196616 | tf_op jit(solution)/shard_map/ppermute | solution.py:20
  12.5 7.3 %collective-permute-start.2 = (f32[32,512]{1,0:T(8,128)}, f32[32,512]{1,0:T(8,128)S(1)}, u32[]{:S(2)}, u32[]{:S(2)}) collective-permute-start(f32[32,512]{1,0:T(8,128)} %get-tuple-element.29), channel_id=1, source_target_pairs={{0,6},{1,7},{2,4},{3,5},{4,2},{5,3},{6,0},{7,1},{8,14},{9,15},{10,... | collective-permute-start | bytes 196616 | tf_op jit(solution)/shard_map/ppermute | solution.py:20
  14.1 0.8 %copy-start.5 = (f32[32,512]{1,0:T(8,128)S(1)}, f32[32,512]{1,0:T(8,128)}, u32[]{:S(2)}) copy-start(f32[32,512]{1,0:T(8,128)} %get-tuple-element.30.refs_0_) | copy-start | bytes 196612
  15.0 4.5 %copy-start.10 = (s32[256]{0:T(256)S(1)}, s32[256]{0:T(256)}, u32[]{:S(2)}) copy-start(s32[256]{0:T(256)} %rel_index_ref.3) | copy-start | bytes 3076
  15.0 8.4 %copy-start.4 = (f32[32,512]{1,0:T(8,128)S(1)}, f32[32,512]{1,0:T(8,128)}, u32[]{:S(2)}) copy-start(f32[32,512]{1,0:T(8,128)} %get-tuple-element.26.refs_2_.refs_0_) | copy-start | bytes 196612
  15.0 6.3 %collective-permute-start.6 = (f32[32,512]{1,0:T(8,128)S(1)}, f32[32,512]{1,0:T(8,128)S(1)}, u32[]{:S(2)}, u32[]{:S(2)}) collective-permute-start(f32[32,512]{1,0:T(8,128)S(1)} %shard_map.131.refs_6_), channel_id=1, source_target_pairs={{0,6},{1,7},{2,4},{3,5},{4,2},{5,3},{6,0},{7,1},{8,14},{9,15},{10,... | collective-permute-start | bytes 196616 | tf_op jit(solution)/shard_map/ppermute | solution.py:20
  17.6 5.9 %collective-permute-start.7 = (f32[32,512]{1,0:T(8,128)S(1)}, f32[32,512]{1,0:T(8,128)S(1)}, u32[]{:S(2)}, u32[]{:S(2)}) collective-permute-start(f32[32,512]{1,0:T(8,128)S(1)} %shard_map.131.refs_6_), channel_id=1, source_target_pairs={{0,4},{1,5},{2,6},{3,7},{4,0},{5,1},{6,2},{7,3},{8,12},{9,13},{10,... | collective-permute-start | bytes 196616 | tf_op jit(solution)/shard_map/ppermute | solution.py:20
  17.7 5.7 %collective-permute-start.8 = (f32[32,512]{1,0:T(8,128)S(1)}, f32[32,512]{1,0:T(8,128)S(1)}, u32[]{:S(2)}, u32[]{:S(2)}) collective-permute-start(f32[32,512]{1,0:T(8,128)S(1)} %shard_map.131.refs_6_), channel_id=1, source_target_pairs={{0,2},{1,3},{2,0},{3,1},{4,6},{5,7},{6,4},{7,5},{8,10},{9,11},{10,... | collective-permute-start | bytes 196616 | tf_op jit(solution)/shard_map/ppermute | solution.py:20
  23.4 1.8 %copy-start.8 = (s32[256]{0:T(256)S(1)}, s32[256]{0:T(256)}, u32[]{:S(2)}) copy-start(s32[256]{0:T(256)} %head_ref.3) | copy-start | bytes 3076
  23.4 1.8 %copy-start.9 = (s32[256]{0:T(256)S(1)}, s32[256]{0:T(256)}, u32[]{:S(2)}) copy-start(s32[256]{0:T(256)} %tail_ref.3) | copy-start | bytes 3076
  23.5 1.8 %collective-permute-start.9 = (f32[192,512]{1,0:T(8,128)S(1)}, f32[192,512]{1,0:T(8,128)S(1)}, u32[]{:S(2)}, u32[]{:S(2)}) collective-permute-start(f32[192,512]{1,0:T(8,128)S(1)} %shard_map.132.refs_4_.refs_0_), channel_id=1, source_target_pairs={{0,1},{1,0},{2,3},{3,2},{4,5},{5,4},{6,7},{7,6},{8,9},{9,8},{10,11... | collective-permute-start | bytes 1179656 | tf_op jit(solution)/shard_map/ppermute | solution.py:20
  26.7 1.6 %collective-permute-start.10 = (f32[128,512]{1,0:T(8,128)S(1)}, f32[128,512]{1,0:T(8,128)S(1)}, u32[]{:S(2)}, u32[]{:S(2)}) collective-permute-start(f32[128,512]{1,0:T(8,128)S(1)} %get-tuple-element.32), channel_id=1, source_target_pairs={{0,1},{1,0},{2,3},{3,2},{4,5},{5,4},{6,7},{7,6},{8,9},{9,8},{10,11... | collective-permute-start | bytes 786440 | tf_op jit(solution)/shard_map/ppermute | solution.py:20
  28.4 6.4 %collective-permute-start.18 = (f32[128,512]{1,0:T(8,128)S(1)}, f32[128,512]{1,0:T(8,128)S(1)}, u32[]{:S(2)}, u32[]{:S(2)}) collective-permute-start(f32[128,512]{1,0:T(8,128)S(1)} %get-tuple-element.47), channel_id=1, source_target_pairs={{0,8},{1,17},{2,10},{3,19},{4,12},{5,21},{6,14},{7,23},{8,0},{9,25... | collective-permute-start | bytes 786440 | tf_op jit(solution)/shard_map/ppermute | solution.py:28
  30.0 11.4 %collective-permute-start.11 = (f32[64,512]{1,0:T(8,128)S(1)}, f32[64,512]{1,0:T(8,128)S(1)}, u32[]{:S(2)}, u32[]{:S(2)}) collective-permute-start(f32[64,512]{1,0:T(8,128)S(1)} %get-tuple-element.40), channel_id=1, source_target_pairs={{0,4},{1,5},{2,6},{3,7},{4,0},{5,1},{6,2},{7,3},{8,12},{9,13},{10,... | collective-permute-start | bytes 393224 | tf_op jit(solution)/shard_map/ppermute | solution.py:20
  31.0 10.6 %collective-permute-start.12 = (f32[64,512]{1,0:T(8,128)S(1)}, f32[64,512]{1,0:T(8,128)S(1)}, u32[]{:S(2)}, u32[]{:S(2)}) collective-permute-start(f32[64,512]{1,0:T(8,128)S(1)} %get-tuple-element.41), channel_id=1, source_target_pairs={{0,2},{1,3},{2,0},{3,1},{4,6},{5,7},{6,4},{7,5},{8,10},{9,11},{10,... | collective-permute-start | bytes 393224 | tf_op jit(solution)/shard_map/ppermute | solution.py:20
  32.6 9.0 %collective-permute-start.13 = (f32[64,512]{1,0:T(8,128)S(1)}, f32[64,512]{1,0:T(8,128)S(1)}, u32[]{:S(2)}, u32[]{:S(2)}) collective-permute-start(f32[64,512]{1,0:T(8,128)S(1)} %get-tuple-element.43), channel_id=1, source_target_pairs={{0,6},{1,7},{2,4},{3,5},{4,2},{5,3},{6,0},{7,1},{8,14},{9,15},{10,... | collective-permute-start | bytes 393224 | tf_op jit(solution)/shard_map/ppermute | solution.py:20
  34.8 14.3 %copy-start.3 = (f32[128,512]{1,0:T(8,128)S(1)}, f32[128,512]{1,0:T(8,128)}, u32[]{:S(2)}) copy-start(f32[128,512]{1,0:T(8,128)} %refs_14_.1) | copy-start | bytes 786436
  34.8 14.3 %copy-start.7 = (s32[8,32]{1,0:T(8,128)S(1)}, s32[8,32]{1,0:T(8,128)}, u32[]{:S(2)}) copy-start(s32[8,32]{1,0:T(8,128)} %refs_2_.1) | copy-start | bytes 3076
  34.8 14.2 %collective-permute-start.19 = (f32[128,512]{1,0:T(8,128)S(1)}, f32[128,512]{1,0:T(8,128)S(1)}, u32[]{:S(2)}, u32[]{:S(2)}) collective-permute-start(f32[128,512]{1,0:T(8,128)S(1)} %add.3.refs_11_), channel_id=1, source_target_pairs={{0,16},{1,9},{2,18},{3,11},{4,20},{5,13},{6,22},{7,15},{8,24},{9,1... | collective-permute-start | bytes 786440 | tf_op jit(solution)/shard_map/ppermute | solution.py:28
  41.6 7.4 %copy-start.1 = (f32[128,512]{1,0:T(8,128)S(1)}, f32[128,512]{1,0:T(8,128)}, u32[]{:S(2)}) copy-start(f32[128,512]{1,0:T(8,128)} %refs_3_.1) | copy-start | bytes 786436
  41.6 7.4 %copy-start.2 = (f32[128,512]{1,0:T(8,128)S(1)}, f32[128,512]{1,0:T(8,128)}, u32[]{:S(2)}) copy-start(f32[128,512]{1,0:T(8,128)} %refs_4_.1) | copy-start | bytes 786436
  41.7 7.4 %copy-start.6 = (s32[1,8,16]{2,1,0:T(8,128)S(1)}, s32[1,8,16]{2,1,0:T(8,128)}, u32[]{:S(2)}) copy-start(s32[1,8,16]{2,1,0:T(8,128)} %refs_1_.1) | copy-start | bytes 1540
  41.7 7.4 %collective-permute-start.14 = (f32[64,512]{1,0:T(8,128)S(1)}, f32[64,512]{1,0:T(8,128)S(1)}, u32[]{:S(2)}, u32[]{:S(2)}) collective-permute-start(f32[64,512]{1,0:T(8,128)S(1)} %get-tuple-element.45), channel_id=1, source_target_pairs={{0,1},{1,0},{2,3},{3,2},{4,5},{5,4},{6,7},{7,6},{8,9},{9,8},{10,11... | collective-permute-start | bytes 393224 | tf_op jit(solution)/shard_map/ppermute | solution.py:20
  41.8 5.7 %collective-permute-start.15 = (f32[32,512]{1,0:T(8,128)S(1)}, f32[32,512]{1,0:T(8,128)S(1)}, u32[]{:S(2)}, u32[]{:S(2)}) collective-permute-start(f32[32,512]{1,0:T(8,128)S(1)} %get-tuple-element.46.refs_7_), channel_id=1, source_target_pairs={{0,24},{1,25},{2,26},{3,27},{4,28},{5,29},{6,30},{7,31},{8,16},{9,... | collective-permute-start | bytes 196616 | tf_op jit(solution)/shard_map/ppermute | solution.py:28
  43.3 5.3 %collective-permute-start.16 = (f32[32,512]{1,0:T(8,128)S(1)}, f32[32,512]{1,0:T(8,128)S(1)}, u32[]{:S(2)}, u32[]{:S(2)}) collective-permute-start(f32[32,512]{1,0:T(8,128)S(1)} %get-tuple-element.46.refs_7_), channel_id=1, source_target_pairs={{0,16},{1,9},{2,18},{3,11},{4,20},{5,13},{6,22},{7,15},{8,24},{9,1... | collective-permute-start | bytes 196616 | tf_op jit(solution)/shard_map/ppermute | solution.py:28
  44.8 4.3 %collective-permute-start.17 = (f32[32,512]{1,0:T(8,128)S(1)}, f32[32,512]{1,0:T(8,128)S(1)}, u32[]{:S(2)}, u32[]{:S(2)}) collective-permute-start(f32[32,512]{1,0:T(8,128)S(1)} %get-tuple-element.46.refs_7_), channel_id=1, source_target_pairs={{0,8},{1,17},{2,10},{3,19},{4,12},{5,21},{6,14},{7,23},{8,0},{9,25... | collective-permute-start | bytes 196616 | tf_op jit(solution)/shard_map/ppermute | solution.py:28

commit v8 on v6

--- a/solution.py
+++ b/solution.py
@@ -95,12 +95,12 @@
     return jnp.concatenate(parts, axis=-1)
 
 
-def gather_kernel(send_ref, neg_ref, entity_ref, negs, *refs):
-    *parcels, rows, sends, picks, sems = refs
+def gather_kernel(lists_ref, entity_ref, negs, *refs):
+    *parcels, rows, lists, sems = refs
     copies = [
         pltpu.make_async_copy(source, target, sems.at[i])
         for i, (source, target) in enumerate(
-            ((entity_ref, rows), (send_ref, sends), (neg_ref, picks))
+            ((entity_ref, rows), (lists_ref, lists))
         )
     ]
     for copy in copies:
@@ -108,14 +108,14 @@
     for copy in copies:
         copy.wait()
     rel_here = lax.axis_index("rel")
-    slots = send_ref.shape[2]
-    for i in range(neg_ref.shape[1]):
-        negs[pl.ds(i, 1), :] = rows[pl.ds(picks[rel_here, i], 1), :]
+    n_rel, slots = 2 * len(parcels), parcels[0].shape[0] // 2
+    for i in range(negs.shape[0]):
+        negs[pl.ds(i, 1), :] = rows[pl.ds(lists[n_rel + rel_here, i], 1), :]
     for s, ref in enumerate(parcels):
         for core in range(2):
             peer = (2 * s + core) ^ rel_here
             for t in range(slots):
-                ref[pl.ds(core * slots + t, 1), :] = rows[pl.ds(sends[0, peer, t], 1), :]
+                ref[pl.ds(core * slots + t, 1), :] = rows[pl.ds(lists[peer, t], 1), :]
 
 
 def unit_parts(rows):
@@ -296,17 +296,23 @@
     n_chip = n_rel // 2
 
     order = [*range(2, n_chip), *range(min(n_chip, 2))]
+    wide = max(slots, n_neg)
+    lists = jnp.concatenate(
+        [
+            jnp.pad(send_rows[0], ((0, 0), (0, wide - slots))),
+            jnp.pad(neg_rows, ((0, 0), (0, wide - n_neg))),
+        ]
+    )
     own_negs, *parcels = call(
         gather_kernel,
         [(n_neg, width)] + [(2 * slots, width)] * n_chip,
-        [HBM, HBM, HBM],
-        (send_rows, neg_rows, entity),
-        limit=60 * 1024,
+        [HBM, HBM],
+        (lists, entity),
+        limit=54784,
         scratch=[
             pltpu.VMEM(entity.shape, jnp.float32),
-            pltpu.SMEM(send_rows.shape, jnp.int32),
-            pltpu.SMEM(neg_rows.shape, jnp.int32),
-            pltpu.SemaphoreType.DMA((3,)),
+            pltpu.SMEM(lists.shape, jnp.int32),
+            pltpu.SemaphoreType.DMA((2,)),
         ],
     )
     spread = [own_negs] + [exchange(own_negs, "dom", n_dom, s) for s in range(1, n_dom)]

time: 50.7 us -> 50.4 us (level)
  Pallas kernels: 6.32 us -> 5.55 us
  other arithmetic: 0.04 us -> 0.79 us
  local copies, waits for them, and re-layouts: 0.59 us -> 0.04 us
    pallas_call x9, Pallas kernels: 6.32 us -> 5.55 us  [call(): pl.pallas_call(body, out_shape=shapes, in_specs=specs, out_specs=[VMEM] *...]
    concatenate x0 -> x1, other arithmetic: none -> 0.75 us  [shards(): jnp.concatenate([jnp.pad(send_rows[0], ((0, 0), (0, wide - slots))), jnp....]
    unnamed x24 -> x18, local copies, waits for them, and re-layouts: 0.59 us -> 0.04 us
where the time goes in v8:
time: 50.4 us; the launch traced here: 50.1 us
  starting transfers between devices  25.7 us (51%)
  waiting for transfers between devices  16.6 us (33%)
  Pallas kernels  5.55 us (11%)
  between operations  1.47 us (3%)
  other arithmetic  0.79 us (2%)
    ppermute x18, starting transfers between devices, exchange(): return lax.ppermute(block, axis, [(i, i ^ step) for i in range(size)])  22 us
    ppermute x18, waiting for transfers between devices, exchange(): return lax.ppermute(block, axis, [(i, i ^ step) for i in range(size)])  16.4 us
    pallas_call x9, Pallas kernels, call(): pl.pallas_call(body, out_shape=shapes, in_specs=specs, out_specs=[VMEM] *...  5.55 us
    ppermute x2, starting transfers between devices, cross_exchange(): return lax.ppermute(block, ('dom', 'rel'), pairs)  3.72 us
  transfers between devices with their start and end apart: 20, of which 12 were waited for; matrix products, arithmetic and copies ran while one was open for 0% of the time, Pallas kernels for 3%

profile of v8, /device:TPU:0, one launch (start us, length us, event | category | flops | bytes accessed | tf_op | source)
XLA Modules:
  0.0 50.1 jit_solution(13008965299170163580)
XLA Ops:
  0.6 0.8 %pad_add_fusion.lists_ref = s32[16,32]{1,0:T(8,128)S(1)} fusion(s32[8,16]{1,0:T(8,128)} %bitcast.1, s32[8,32]{1,0:T(8,128)} %refs_2_.1), kind=kLoop, calls=%fused_computation | loop fusion | flops 512 | bytes 3584 | tf_op jit(solution)/shard_map/concatenate | solution.py:300
  1.4 1.3 %shard_map.130 = (f32[32,512]{1,0:T(8,128)S(1)}, f32[32,512]{1,0:T(8,128)S(1)}, f32[32,512]{1,0:T(8,128)S(1)}, f32[32,512]{1,0:T(8,128)S(1)}, f32[32,512]{1,0:T(8,128)S(1)}) custom-call(s32[16,32]{1,0:T(8,128)S(1)} %pad_add_fusion.lists_ref, f32[128,512]{1,0:T(8,128)} %refs_3_.1), custom_call_target="tpu_custom_call" | custom-call | bytes 591872 | tf_op jit(solution)/shard_map/pallas_call | solution.py:34
  2.7 3.1 %collective-permute-start = (f32[32,512]{1,0:T(8,128)S(1)}, f32[32,512]{1,0:T(8,128)S(1)}, u32[]{:S(2)}, u32[]{:S(2)}) collective-permute-start(f32[32,512]{1,0:T(8,128)S(1)} %get-tuple-element.27), channel_id=1, source_target_pairs={{0,2},{1,3},{2,0},{3,1},{4,6},{5,7},{6,4},{7,5},{8,10},{9,11},{10,... | collective-permute-start | bytes 196616 | tf_op jit(solution)/shard_map/ppermute | solution.py:20
  5.8 1.5 %collective-permute-start.3 = (f32[32,512]{1,0:T(8,128)S(1)}, f32[32,512]{1,0:T(8,128)S(1)}, u32[]{:S(2)}, u32[]{:S(2)}) collective-permute-start(f32[32,512]{1,0:T(8,128)S(1)} %get-tuple-element.30.refs_0_), channel_id=1, source_target_pairs={{0,8},{8,0},{16,24},{24,16},{1,9},{9,1},{17,25},{25,17},{2,10},{10... | collective-permute-start | bytes 196616 | tf_op jit(solution)/shard_map/ppermute | solution.py:20
  7.3 1.5 %collective-permute-start.4 = (f32[32,512]{1,0:T(8,128)S(1)}, f32[32,512]{1,0:T(8,128)S(1)}, u32[]{:S(2)}, u32[]{:S(2)}) collective-permute-start(f32[32,512]{1,0:T(8,128)S(1)} %get-tuple-element.30.refs_0_), channel_id=1, source_target_pairs={{0,16},{8,24},{16,0},{24,8},{1,17},{9,25},{17,1},{25,9},{2,18},{10... | collective-permute-start | bytes 196616 | tf_op jit(solution)/shard_map/ppermute | solution.py:20
  8.8 0.5 collective-permute-start.5
  9.3 2.6 %collective-permute-start.1 = (f32[32,512]{1,0:T(8,128)S(1)}, f32[32,512]{1,0:T(8,128)S(1)}, u32[]{:S(2)}, u32[]{:S(2)}) collective-permute-start(f32[32,512]{1,0:T(8,128)S(1)} %get-tuple-element.28), channel_id=1, source_target_pairs={{0,4},{1,5},{2,6},{3,7},{4,0},{5,1},{6,2},{7,3},{8,12},{9,13},{10,... | collective-permute-start | bytes 196616 | tf_op jit(solution)/shard_map/ppermute | solution.py:20
  12.5 0.3 shard_map.129.after_ref.rot_ref
  12.8 0.0 collective-permute-done.refs_4_.refs_3_.refs_1_
  12.8 0.1 collective-permute-start.2
  12.9 0.0 collective-permute-done.3.refs_1_
  12.9 0.0 collective-permute-done.4.refs_2_
  12.9 1.0 %collective-permute-done.5.refs_3_ = f32[32,512]{1,0:T(8,128)S(1)} collective-permute-done((f32[32,512]{1,0:T(8,128)S(1)}, f32[32,512]{1,0:T(8,128)S(1)}, u32[]{:S(2)}, u32[]{:S(2)}) %collective-permute-start.5) | collective-permute-done | bytes 65568 | tf_op jit(solution)/shard_map/ppermute | solution.py:20
  14.0 2.8 %collective-permute-start.6 = (f32[32,512]{1,0:T(8,128)S(1)}, f32[32,512]{1,0:T(8,128)S(1)}, u32[]{:S(2)}, u32[]{:S(2)}) collective-permute-start(f32[32,512]{1,0:T(8,128)S(1)} %shard_map.131.refs_6_), channel_id=1, source_target_pairs={{0,6},{1,7},{2,4},{3,5},{4,2},{5,3},{6,0},{7,1},{8,14},{9,15},{10,... | collective-permute-start | bytes 196616 | tf_op jit(solution)/shard_map/ppermute | solution.py:20
  16.8 0.0 collective-permute-start.7
  16.8 1.6 %collective-permute-start.8 = (f32[32,512]{1,0:T(8,128)S(1)}, f32[32,512]{1,0:T(8,128)S(1)}, u32[]{:S(2)}, u32[]{:S(2)}) collective-permute-start(f32[32,512]{1,0:T(8,128)S(1)} %shard_map.131.refs_6_), channel_id=1, source_target_pairs={{0,2},{1,3},{2,0},{3,1},{4,6},{5,7},{6,4},{7,5},{8,10},{9,11},{10,... | collective-permute-start | bytes 196616 | tf_op jit(solution)/shard_map/ppermute | solution.py:20
  18.4 0.0 collective-permute-done.1.refs_0_.refs_2_
  18.4 0.9 %collective-permute-done.2.refs_1_.refs_3_ = f32[32,512]{1,0:T(8,128)S(1)} collective-permute-done((f32[32,512]{1,0:T(8,128)S(1)}, f32[32,512]{1,0:T(8,128)S(1)}, u32[]{:S(2)}, u32[]{:S(2)}) %collective-permute-start.2) | collective-permute-done | bytes 65568 | tf_op jit(solution)/shard_map/ppermute | solution.py:20
  19.3 1.5 %collective-permute-done.6.refs_4_ = f32[32,512]{1,0:T(8,128)S(1)} collective-permute-done((f32[32,512]{1,0:T(8,128)S(1)}, f32[32,512]{1,0:T(8,128)S(1)}, u32[]{:S(2)}, u32[]{:S(2)}) %collective-permute-start.6) | collective-permute-done | bytes 65568 | tf_op jit(solution)/shard_map/ppermute | solution.py:20
  20.8 2.4 %collective-permute-done.7.refs_5_ = f32[32,512]{1,0:T(8,128)S(1)} collective-permute-done((f32[32,512]{1,0:T(8,128)S(1)}, f32[32,512]{1,0:T(8,128)S(1)}, u32[]{:S(2)}, u32[]{:S(2)}) %collective-permute-start.7) | collective-permute-done | bytes 65568 | tf_op jit(solution)/shard_map/ppermute | solution.py:20
  23.2 0.0 collective-permute-done.8.refs_7_
  23.2 0.1 collective-permute-start.9
  23.3 1.7 %collective-permute-done.9.refs_5_.refs_1_ = f32[192,512]{1,0:T(8,128)S(1)} collective-permute-done((f32[192,512]{1,0:T(8,128)S(1)}, f32[192,512]{1,0:T(8,128)S(1)}, u32[]{:S(2)}, u32[]{:S(2)}) %collective-permute-start.9) | collective-permute-done | bytes 393248 | tf_op jit(solution)/shard_map/ppermute | solution.py:20
  25.0 1.4 %shard_map.133 = (f32[128,512]{1,0:T(8,128)S(1)}, f32[128,512]{1,0:T(8,128)S(1)}, f32[256,512]{1,0:T(8,128)S(1)}, f32[256,512]{1,0:T(8,128)S(1)}, f32[256,512]{1...) custom-call(s32[256]{0:T(256)S(1)} %copy-done.6, s32[256]{0:T(256)S(1)} %copy-done.7, ...), custom_call_target="tpu_custom_call" | custom-call | bytes 4065280 | tf_op jit(solution)/shard_map/pallas_call | solution.py:34
  26.4 0.2 collective-permute-start.10
  26.6 1.1 %shard_map.134 = (f32[128,512]{1,0:T(8,128)S(1)}, f32[128,512]{1,0:T(8,128)S(1)}) custom-call(s32[256]{0:T(256)S(1)} %copy-done.6, s32[256]{0:T(256)S(1)} %copy-done.8, s32[256]{0:T(256)S(1)} %copy-done.7, f32[128,512]{1,0:T(8,128)S(1)} %copy-done, f32[256,512]{1,0:T(8,128)S(1)} %shard_map.129.after_ref.rot_ref, f32[192,512]{1,0:T(8,128)S(1)} %shard_map.132.refs_4_.refs_0_, ...), custom_call_target="tpu_custom_call" | custom-call | bytes 4066304 | tf_op jit(solution)/shard_map/pallas_call | solution.py:34
  27.7 0.3 collective-permute-done.10.theirs
  28.0 0.1 shard_map.135
  28.1 1.8 %collective-permute-start.18 = (f32[128,512]{1,0:T(8,128)S(1)}, f32[128,512]{1,0:T(8,128)S(1)}, u32[]{:S(2)}, u32[]{:S(2)}) collective-permute-start(f32[128,512]{1,0:T(8,128)S(1)} %get-tuple-element.47), channel_id=1, source_target_pairs={{0,8},{1,17},{2,10},{3,19},{4,12},{5,21},{6,14},{7,23},{8,0},{9,25... | collective-permute-start | bytes 786440 | tf_op jit(solution)/shard_map/ppermute | solution.py:28
  29.9 0.5 %collective-permute-start.11 = (f32[64,512]{1,0:T(8,128)S(1)}, f32[64,512]{1,0:T(8,128)S(1)}, u32[]{:S(2)}, u32[]{:S(2)}) collective-permute-start(f32[64,512]{1,0:T(8,128)S(1)} %get-tuple-element.40), channel_id=1, source_target_pairs={{0,4},{1,5},{2,6},{3,7},{4,0},{5,1},{6,2},{7,3},{8,12},{9,13},{10,... | collective-permute-start | bytes 393224 | tf_op jit(solution)/shard_map/ppermute | solution.py:20
  30.5 2.1 %collective-permute-start.12 = (f32[64,512]{1,0:T(8,128)S(1)}, f32[64,512]{1,0:T(8,128)S(1)}, u32[]{:S(2)}, u32[]{:S(2)}) collective-permute-start(f32[64,512]{1,0:T(8,128)S(1)} %get-tuple-element.41), channel_id=1, source_target_pairs={{0,2},{1,3},{2,0},{3,1},{4,6},{5,7},{6,4},{7,5},{8,10},{9,11},{10,... | collective-permute-start | bytes 393224 | tf_op jit(solution)/shard_map/ppermute | solution.py:20
  32.5 1.8 %collective-permute-start.13 = (f32[64,512]{1,0:T(8,128)S(1)}, f32[64,512]{1,0:T(8,128)S(1)}, u32[]{:S(2)}, u32[]{:S(2)}) collective-permute-start(f32[64,512]{1,0:T(8,128)S(1)} %get-tuple-element.43), channel_id=1, source_target_pairs={{0,6},{1,7},{2,4},{3,5},{4,2},{5,3},{6,0},{7,1},{8,14},{9,15},{10,... | collective-permute-start | bytes 393224 | tf_op jit(solution)/shard_map/ppermute | solution.py:20
  34.3 0.2 collective-permute-done.18
  34.6 1.9 %collective-permute-start.19 = (f32[128,512]{1,0:T(8,128)S(1)}, f32[128,512]{1,0:T(8,128)S(1)}, u32[]{:S(2)}, u32[]{:S(2)}) collective-permute-start(f32[128,512]{1,0:T(8,128)S(1)} %add.5.refs_11_), channel_id=1, source_target_pairs={{0,16},{1,9},{2,18},{3,11},{4,20},{5,13},{6,22},{7,15},{8,24},{9,1... | collective-permute-start | bytes 786440 | tf_op jit(solution)/shard_map/ppermute | solution.py:28
  36.4 4.8 %collective-permute-done.11.refs_0_ = f32[64,512]{1,0:T(8,128)S(1)} collective-permute-done((f32[64,512]{1,0:T(8,128)S(1)}, f32[64,512]{1,0:T(8,128)S(1)}, u32[]{:S(2)}, u32[]{:S(2)}) %collective-permute-start.11) | collective-permute-done | bytes 131104 | tf_op jit(solution)/shard_map/ppermute | solution.py:20
  41.3 0.1 collective-permute-done.12.refs_1_
  41.4 0.0 collective-permute-done.13.refs_3_
  41.5 0.0 copy-start.4
  41.5 0.1 collective-permute-start.14
  41.5 1.6 %collective-permute-start.15 = (f32[32,512]{1,0:T(8,128)S(1)}, f32[32,512]{1,0:T(8,128)S(1)}, u32[]{:S(2)}, u32[]{:S(2)}) collective-permute-start(f32[32,512]{1,0:T(8,128)S(1)} %get-tuple-element.46.refs_7_), channel_id=1, source_target_pairs={{0,8},{8,0},{16,24},{24,16},{1,9},{9,1},{17,25},{25,17},{2,10},{10... | collective-permute-start | bytes 196616 | tf_op jit(solution)/shard_map/ppermute | solution.py:20
  43.1 0.5 %collective-permute-start.16 = (f32[32,512]{1,0:T(8,128)S(1)}, f32[32,512]{1,0:T(8,128)S(1)}, u32[]{:S(2)}, u32[]{:S(2)}) collective-permute-start(f32[32,512]{1,0:T(8,128)S(1)} %get-tuple-element.46.refs_7_), channel_id=1, source_target_pairs={{0,16},{8,24},{16,0},{24,8},{1,17},{9,25},{17,1},{25,9},{2,18},{10... | collective-permute-start | bytes 196616 | tf_op jit(solution)/shard_map/ppermute | solution.py:20
  43.6 1.5 %collective-permute-start.17 = (f32[32,512]{1,0:T(8,128)S(1)}, f32[32,512]{1,0:T(8,128)S(1)}, u32[]{:S(2)}, u32[]{:S(2)}) collective-permute-start(f32[32,512]{1,0:T(8,128)S(1)} %get-tuple-element.46.refs_7_), channel_id=1, source_target_pairs={{0,24},{8,16},{16,8},{24,0},{1,25},{9,17},{17,9},{25,1},{2,26},{10... | collective-permute-start | bytes 196616 | tf_op jit(solution)/shard_map/ppermute | solution.py:20
  45.1 1.0 %collective-permute-done.15.refs_8_ = f32[32,512]{1,0:T(8,128)S(1)} collective-permute-done((f32[32,512]{1,0:T(8,128)S(1)}, f32[32,512]{1,0:T(8,128)S(1)}, u32[]{:S(2)}, u32[]{:S(2)}) %collective-permute-start.15) | collective-permute-done | bytes 65568 | tf_op jit(solution)/shard_map/ppermute | solution.py:20
  46.1 2.0 %collective-permute-done.16.refs_9_ = f32[32,512]{1,0:T(8,128)S(1)} collective-permute-done((f32[32,512]{1,0:T(8,128)S(1)}, f32[32,512]{1,0:T(8,128)S(1)}, u32[]{:S(2)}, u32[]{:S(2)}) %collective-permute-start.16) | collective-permute-done | bytes 65568 | tf_op jit(solution)/shard_map/ppermute | solution.py:20
  48.1 0.7 %collective-permute-done.17.refs_10_ = f32[32,512]{1,0:T(8,128)S(1)} collective-permute-done((f32[32,512]{1,0:T(8,128)S(1)}, f32[32,512]{1,0:T(8,128)S(1)}, u32[]{:S(2)}, u32[]{:S(2)}) %collective-permute-start.17) | collective-permute-done | bytes 65568 | tf_op jit(solution)/shard_map/ppermute | solution.py:20
  48.8 0.0 collective-permute-done.14.refs_6_
  48.8 0.0 collective-permute-done.19.refs_12_
  48.8 1.3 %shard_map.137 = (f32[128,512]{1,0:T(8,128)}, f32[128,512]{1,0:T(8,128)}, f32[128,512]{1,0:T(8,128)}, f32[128,512]{1,0:T(8,128)}) custom-call(s32[1]{0:T(128)S(6)} %copy.14.part_ref.refs_0_, s32[1,8,16]{2,1,0:T(8,128)S(1)} %copy-done.4, s32[8,32]{1,0:T(8,128)S(1)} %copy-done.5, f32[128,512]{1,0:T(8,128)S(1)} %copy-done.1, f32[128,512]{1,0:T(8,128)S(1)} %copy-done.2, ...), custom_call_target="tpu_custom_call" | custom-call | bytes 3147268 | tf_op jit(solution)/shard_map/pallas_call | solution.py:34
  (21 shorter events, 0.1 us)
Async XLA Ops:
  0.6 11.9 %copy-start = (f32[128,512]{1,0:T(8,128)S(1)}, f32[128,512]{1,0:T(8,128)}, u32[]{:S(2)}) copy-start(f32[128,512]{1,0:T(8,128)} %refs_13_.1) | copy-start | bytes 786436
  2.7 10.1 %collective-permute-start = (f32[32,512]{1,0:T(8,128)S(1)}, f32[32,512]{1,0:T(8,128)S(1)}, u32[]{:S(2)}, u32[]{:S(2)}) collective-permute-start(f32[32,512]{1,0:T(8,128)S(1)} %get-tuple-element.27), channel_id=1, source_target_pairs={{0,2},{1,3},{2,0},{3,1},{4,6},{5,7},{6,4},{7,5},{8,10},{9,11},{10,... | collective-permute-start | bytes 196616 | tf_op jit(solution)/shard_map/ppermute | solution.py:20
  5.8 7.1 %collective-permute-start.3 = (f32[32,512]{1,0:T(8,128)S(1)}, f32[32,512]{1,0:T(8,128)S(1)}, u32[]{:S(2)}, u32[]{:S(2)}) collective-permute-start(f32[32,512]{1,0:T(8,128)S(1)} %get-tuple-element.30.refs_0_), channel_id=1, source_target_pairs={{0,8},{8,0},{16,24},{24,16},{1,9},{9,1},{17,25},{25,17},{2,10},{10... | collective-permute-start | bytes 196616 | tf_op jit(solution)/shard_map/ppermute | solution.py:20
  7.3 5.6 %collective-permute-start.4 = (f32[32,512]{1,0:T(8,128)S(1)}, f32[32,512]{1,0:T(8,128)S(1)}, u32[]{:S(2)}, u32[]{:S(2)}) collective-permute-start(f32[32,512]{1,0:T(8,128)S(1)} %get-tuple-element.30.refs_0_), channel_id=1, source_target_pairs={{0,16},{8,24},{16,0},{24,8},{1,17},{9,25},{17,1},{25,9},{2,18},{10... | collective-permute-start | bytes 196616 | tf_op jit(solution)/shard_map/ppermute | solution.py:20
  8.8 5.2 %collective-permute-start.5 = (f32[32,512]{1,0:T(8,128)S(1)}, f32[32,512]{1,0:T(8,128)S(1)}, u32[]{:S(2)}, u32[]{:S(2)}) collective-permute-start(f32[32,512]{1,0:T(8,128)S(1)} %get-tuple-element.30.refs_0_), channel_id=1, source_target_pairs={{0,24},{8,16},{16,8},{24,0},{1,25},{9,17},{17,9},{25,1},{2,26},{10... | collective-permute-start | bytes 196616 | tf_op jit(solution)/shard_map/ppermute | solution.py:20
  9.3 3.3 %copy-start.8 = (s32[256]{0:T(256)S(1)}, s32[256]{0:T(256)}, u32[]{:S(2)}) copy-start(s32[256]{0:T(256)} %rel_index_ref.3) | copy-start | bytes 3076
  9.3 9.2 %collective-permute-start.1 = (f32[32,512]{1,0:T(8,128)S(1)}, f32[32,512]{1,0:T(8,128)S(1)}, u32[]{:S(2)}, u32[]{:S(2)}) collective-permute-start(f32[32,512]{1,0:T(8,128)S(1)} %get-tuple-element.28), channel_id=1, source_target_pairs={{0,4},{1,5},{2,6},{3,7},{4,0},{5,1},{6,2},{7,3},{8,12},{9,13},{10,... | collective-permute-start | bytes 196616 | tf_op jit(solution)/shard_map/ppermute | solution.py:20
  12.8 6.5 %collective-permute-start.2 = (f32[32,512]{1,0:T(8,128)S(1)}, f32[32,512]{1,0:T(8,128)S(1)}, u32[]{:S(2)}, u32[]{:S(2)}) collective-permute-start(f32[32,512]{1,0:T(8,128)S(1)} %get-tuple-element.29), channel_id=1, source_target_pairs={{0,6},{1,7},{2,4},{3,5},{4,2},{5,3},{6,0},{7,1},{8,14},{9,15},{10,... | collective-permute-start | bytes 196616 | tf_op jit(solution)/shard_map/ppermute | solution.py:20
  14.0 6.8 %collective-permute-start.6 = (f32[32,512]{1,0:T(8,128)S(1)}, f32[32,512]{1,0:T(8,128)S(1)}, u32[]{:S(2)}, u32[]{:S(2)}) collective-permute-start(f32[32,512]{1,0:T(8,128)S(1)} %shard_map.131.refs_6_), channel_id=1, source_target_pairs={{0,6},{1,7},{2,4},{3,5},{4,2},{5,3},{6,0},{7,1},{8,14},{9,15},{10,... | collective-permute-start | bytes 196616 | tf_op jit(solution)/shard_map/ppermute | solution.py:20
  16.8 6.4 %collective-permute-start.7 = (f32[32,512]{1,0:T(8,128)S(1)}, f32[32,512]{1,0:T(8,128)S(1)}, u32[]{:S(2)}, u32[]{:S(2)}) collective-permute-start(f32[32,512]{1,0:T(8,128)S(1)} %shard_map.131.refs_6_), channel_id=1, source_target_pairs={{0,4},{1,5},{2,6},{3,7},{4,0},{5,1},{6,2},{7,3},{8,12},{9,13},{10,... | collective-permute-start | bytes 196616 | tf_op jit(solution)/shard_map/ppermute | solution.py:20
  16.8 6.4 %collective-permute-start.8 = (f32[32,512]{1,0:T(8,128)S(1)}, f32[32,512]{1,0:T(8,128)S(1)}, u32[]{:S(2)}, u32[]{:S(2)}) collective-permute-start(f32[32,512]{1,0:T(8,128)S(1)} %shard_map.131.refs_6_), channel_id=1, source_target_pairs={{0,2},{1,3},{2,0},{3,1},{4,6},{5,7},{6,4},{7,5},{8,10},{9,11},{10,... | collective-permute-start | bytes 196616 | tf_op jit(solution)/shard_map/ppermute | solution.py:20
  23.2 1.8 %copy-start.6 = (s32[256]{0:T(256)S(1)}, s32[256]{0:T(256)}, u32[]{:S(2)}) copy-start(s32[256]{0:T(256)} %head_ref.3) | copy-start | bytes 3076
  23.2 1.8 %copy-start.7 = (s32[256]{0:T(256)S(1)}, s32[256]{0:T(256)}, u32[]{:S(2)}) copy-start(s32[256]{0:T(256)} %tail_ref.3) | copy-start | bytes 3076
  23.2 1.8 %collective-permute-start.9 = (f32[192,512]{1,0:T(8,128)S(1)}, f32[192,512]{1,0:T(8,128)S(1)}, u32[]{:S(2)}, u32[]{:S(2)}) collective-permute-start(f32[192,512]{1,0:T(8,128)S(1)} %shard_map.132.refs_4_.refs_0_), channel_id=1, source_target_pairs={{0,1},{1,0},{2,3},{3,2},{4,5},{5,4},{6,7},{7,6},{8,9},{9,8},{10,11... | collective-permute-start | bytes 1179656 | tf_op jit(solution)/shard_map/ppermute | solution.py:20
  26.4 1.6 %collective-permute-start.10 = (f32[128,512]{1,0:T(8,128)S(1)}, f32[128,512]{1,0:T(8,128)S(1)}, u32[]{:S(2)}, u32[]{:S(2)}) collective-permute-start(f32[128,512]{1,0:T(8,128)S(1)} %get-tuple-element.32), channel_id=1, source_target_pairs={{0,1},{1,0},{2,3},{3,2},{4,5},{5,4},{6,7},{7,6},{8,9},{9,8},{10,11... | collective-permute-start | bytes 786440 | tf_op jit(solution)/shard_map/ppermute | solution.py:20
  28.1 6.4 %collective-permute-start.18 = (f32[128,512]{1,0:T(8,128)S(1)}, f32[128,512]{1,0:T(8,128)S(1)}, u32[]{:S(2)}, u32[]{:S(2)}) collective-permute-start(f32[128,512]{1,0:T(8,128)S(1)} %get-tuple-element.47), channel_id=1, source_target_pairs={{0,8},{1,17},{2,10},{3,19},{4,12},{5,21},{6,14},{7,23},{8,0},{9,25... | collective-permute-start | bytes 786440 | tf_op jit(solution)/shard_map/ppermute | solution.py:28
  29.9 11.4 %collective-permute-start.11 = (f32[64,512]{1,0:T(8,128)S(1)}, f32[64,512]{1,0:T(8,128)S(1)}, u32[]{:S(2)}, u32[]{:S(2)}) collective-permute-start(f32[64,512]{1,0:T(8,128)S(1)} %get-tuple-element.40), channel_id=1, source_target_pairs={{0,4},{1,5},{2,6},{3,7},{4,0},{5,1},{6,2},{7,3},{8,12},{9,13},{10,... | collective-permute-start | bytes 393224 | tf_op jit(solution)/shard_map/ppermute | solution.py:20
  30.5 10.9 %collective-permute-start.12 = (f32[64,512]{1,0:T(8,128)S(1)}, f32[64,512]{1,0:T(8,128)S(1)}, u32[]{:S(2)}, u32[]{:S(2)}) collective-permute-start(f32[64,512]{1,0:T(8,128)S(1)} %get-tuple-element.41), channel_id=1, source_target_pairs={{0,2},{1,3},{2,0},{3,1},{4,6},{5,7},{6,4},{7,5},{8,10},{9,11},{10,... | collective-permute-start | bytes 393224 | tf_op jit(solution)/shard_map/ppermute | solution.py:20
  32.5 8.9 %collective-permute-start.13 = (f32[64,512]{1,0:T(8,128)S(1)}, f32[64,512]{1,0:T(8,128)S(1)}, u32[]{:S(2)}, u32[]{:S(2)}) collective-permute-start(f32[64,512]{1,0:T(8,128)S(1)} %get-tuple-element.43), channel_id=1, source_target_pairs={{0,6},{1,7},{2,4},{3,5},{4,2},{5,3},{6,0},{7,1},{8,14},{9,15},{10,... | collective-permute-start | bytes 393224 | tf_op jit(solution)/shard_map/ppermute | solution.py:20
  34.5 14.3 %copy-start.3 = (f32[128,512]{1,0:T(8,128)S(1)}, f32[128,512]{1,0:T(8,128)}, u32[]{:S(2)}) copy-start(f32[128,512]{1,0:T(8,128)} %refs_14_.1) | copy-start | bytes 786436
  34.5 14.3 %copy-start.5 = (s32[8,32]{1,0:T(8,128)S(1)}, s32[8,32]{1,0:T(8,128)}, u32[]{:S(2)}) copy-start(s32[8,32]{1,0:T(8,128)} %refs_2_.1) | copy-start | bytes 3076
  34.6 14.2 %collective-permute-start.19 = (f32[128,512]{1,0:T(8,128)S(1)}, f32[128,512]{1,0:T(8,128)S(1)}, u32[]{:S(2)}, u32[]{:S(2)}) collective-permute-start(f32[128,512]{1,0:T(8,128)S(1)} %add.5.refs_11_), channel_id=1, source_target_pairs={{0,16},{1,9},{2,18},{3,11},{4,20},{5,13},{6,22},{7,15},{8,24},{9,1... | collective-permute-start | bytes 786440 | tf_op jit(solution)/shard_map/ppermute | solution.py:28
  41.4 7.4 %copy-start.1 = (f32[128,512]{1,0:T(8,128)S(1)}, f32[128,512]{1,0:T(8,128)}, u32[]{:S(2)}) copy-start(f32[128,512]{1,0:T(8,128)} %refs_3_.1) | copy-start | bytes 786436
  41.4 7.4 %copy-start.2 = (f32[128,512]{1,0:T(8,128)S(1)}, f32[128,512]{1,0:T(8,128)}, u32[]{:S(2)}) copy-start(f32[128,512]{1,0:T(8,128)} %refs_4_.1) | copy-start | bytes 786436
  41.5 7.4 %copy-start.4 = (s32[1,8,16]{2,1,0:T(8,128)S(1)}, s32[1,8,16]{2,1,0:T(8,128)}, u32[]{:S(2)}) copy-start(s32[1,8,16]{2,1,0:T(8,128)} %refs_1_.1) | copy-start | bytes 1540
  41.5 7.3 %collective-permute-start.14 = (f32[64,512]{1,0:T(8,128)S(1)}, f32[64,512]{1,0:T(8,128)S(1)}, u32[]{:S(2)}, u32[]{:S(2)}) collective-permute-start(f32[64,512]{1,0:T(8,128)S(1)} %get-tuple-element.45), channel_id=1, source_target_pairs={{0,1},{1,0},{2,3},{3,2},{4,5},{5,4},{6,7},{7,6},{8,9},{9,8},{10,11... | collective-permute-start | bytes 393224 | tf_op jit(solution)/shard_map/ppermute | solution.py:20
  41.5 4.5 %collective-permute-start.15 = (f32[32,512]{1,0:T(8,128)S(1)}, f32[32,512]{1,0:T(8,128)S(1)}, u32[]{:S(2)}, u32[]{:S(2)}) collective-permute-start(f32[32,512]{1,0:T(8,128)S(1)} %get-tuple-element.46.refs_7_), channel_id=1, source_target_pairs={{0,8},{8,0},{16,24},{24,16},{1,9},{9,1},{17,25},{25,17},{2,10},{10... | collective-permute-start | bytes 196616 | tf_op jit(solution)/shard_map/ppermute | solution.py:20
  43.1 5.0 %collective-permute-start.16 = (f32[32,512]{1,0:T(8,128)S(1)}, f32[32,512]{1,0:T(8,128)S(1)}, u32[]{:S(2)}, u32[]{:S(2)}) collective-permute-start(f32[32,512]{1,0:T(8,128)S(1)} %get-tuple-element.46.refs_7_), channel_id=1, source_target_pairs={{0,16},{8,24},{16,0},{24,8},{1,17},{9,25},{17,1},{25,9},{2,18},{10... | collective-permute-start | bytes 196616 | tf_op jit(solution)/shard_map/ppermute | solution.py:20
  43.6 5.2 %collective-permute-start.17 = (f32[32,512]{1,0:T(8,128)S(1)}, f32[32,512]{1,0:T(8,128)S(1)}, u32[]{:S(2)}, u32[]{:S(2)}) collective-permute-start(f32[32,512]{1,0:T(8,128)S(1)} %get-tuple-element.46.refs_7_), channel_id=1, source_target_pairs={{0,24},{8,16},{16,8},{24,0},{1,25},{9,17},{17,9},{25,1},{2,26},{10... | collective-permute-start | bytes 196616 | tf_op jit(solution)/shard_map/ppermute | solution.py:20
